TPU v7x, 128 devices: a whole 4x4x4 slice. The times are simulated.
128 devices in a mesh: row: 16 (over x, y), col: 8 (over z, core).
Axes of the slice: x: 4, y: 4, z: 4, core: 2. Of those that a mesh axis runs over, the one named last changes fastest.
Arguments:
- object_field: float32 [2, 4096, 4096], P(None, 'row', 'col'), may hold values from -5 to 5
- probe: float32 [3, 2, 256, 256], replicated, may hold values from -6 to 6
- corners: int32 [2, 16, 8, 2, 2], P(None, 'row', 'col'), may hold values from 0 to 3840, as said below
- counts: int32 [2, 16, 8], P(None, 'row', 'col'), may hold values from 1 to 2, as said below
- amplitude: bfloat16 [2, 16, 8, 2, 256, 256], P(None, 'row', 'col'), may hold values from 0.19921875 to 4
Outputs:
- object_out: float32 [2, 4096, 4096], P(None, 'row', 'col')
- probe_out: float32 [3, 2, 256, 256], replicated
- losses: float32 [2, 16, 8], P(None, 'row', 'col')
Inputs may be any that keep to these rules, and one draw needn't show every extreme that they name: corners[t, i, j, s] lies inside tile (i, j), i.e. its row in i * 256 to (i + 1) * 256 - 1 and its column in j * 512 to (j + 1) * 512 - 1, and the whole window lies inside the object of 4096 x 4096 pixels, so a window reaches at most into the tiles below, to the right and diagonally below right; in every iteration slot 0 of the first tile has corner (0, 0) and slot 0 of the last tile has corner (3840, 3840). Slots 0 to counts - 1 of a tile are live, the rest are ignored; in every iteration some tile has all 2 slots live.
All inputs are finite; a program needn't handle non-finite values.
Results may differ from a plain program's by a relative error of at most 0.0003.
Values sent between devices are 32-bit elements; how exact they have to be, the bound alone decides.
No kernel may reach another device: no remote copies, remote signals or barrier semaphores. Data moves between devices by JAX's collectives and lax.ppermute only.
A program may use at most 128 MiB of HBM per device.

v0:
```python
import math

import jax
import jax.numpy as jnp
from jax import lax
from jax.sharding import PartitionSpec as P

PRECISE = lax.Precision.HIGHEST


def from_behind(value, axis, steps):
    count = lax.axis_size(axis)
    leading, last = (max(0, -steps), min(count, count - steps))
    return lax.ppermute(value, axis, [(source, source + steps) for source in range(leading, last)])


def dft_tables(win_size):
    row_index = lax.broadcasted_iota(jnp.int32, (win_size, win_size), 0)
    col_index = lax.broadcasted_iota(jnp.int32, (win_size, win_size), 1)
    angles = (row_index * col_index % win_size).astype(jnp.float32) * (-2.0 * math.pi / win_size)
    unit_scale = 1.0 / math.sqrt(win_size)
    return (jnp.cos(angles) * unit_scale, jnp.sin(angles) * unit_scale)


def dft_pair(real_part, imag_part, cosine, sine_part):
    left_re = jnp.einsum("kn,bnj->bkj", cosine, real_part, precision=PRECISE) - jnp.einsum(
        "kn,bnj->bkj", sine_part, imag_part, precision=PRECISE
    )
    left_im = jnp.einsum("kn,bnj->bkj", cosine, imag_part, precision=PRECISE) + jnp.einsum(
        "kn,bnj->bkj", sine_part, real_part, precision=PRECISE
    )
    out_re = jnp.einsum("bjn,nk->bjk", left_re, cosine, precision=PRECISE) - jnp.einsum(
        "bjn,nk->bjk", left_im, sine_part, precision=PRECISE
    )
    out_im = jnp.einsum("bjn,nk->bjk", left_im, cosine, precision=PRECISE) + jnp.einsum(
        "bjn,nk->bjk", left_re, sine_part, precision=PRECISE
    )
    return (out_re, out_im)


def window_terms(obj_re, obj_im, measured, alive_mask, probe_now, cosine, sine_part):
    batch_size = obj_re.shape[0]
    mode_count = probe_now.shape[0]
    win_size = probe_now.shape[-1]
    inverse_area = 1.0 / (win_size * win_size)
    probe_re = probe_now[:, 0][None]
    probe_im = probe_now[:, 1][None]
    slot_re = obj_re[:, None]
    slot_im = obj_im[:, None]
    exit_re = (probe_re * slot_re - probe_im * slot_im).reshape(-1, win_size, win_size)
    exit_im = (probe_re * slot_im + probe_im * slot_re).reshape(-1, win_size, win_size)
    far_re, far_im = dft_pair(exit_re, exit_im, cosine, sine_part)
    far_re = far_re.reshape(batch_size, mode_count, win_size, win_size)
    far_im = far_im.reshape(batch_size, mode_count, win_size, win_size)
    intensity = jnp.sum(far_re * far_re + far_im * far_im, axis=1)
    modulus = jnp.sqrt(intensity + 1.0)
    slot_losses = alive_mask * jnp.sum((modulus - measured) ** 2, axis=(1, 2)) * inverse_area
    factor = ((1.0 - measured / modulus) * (2.0 * inverse_area) * alive_mask[:, None, None])[
        :, None
    ]
    back_re, back_im = dft_pair(
        (factor * far_re).reshape(-1, win_size, win_size),
        (factor * far_im).reshape(-1, win_size, win_size),
        cosine,
        -sine_part,
    )
    back_re = back_re.reshape(batch_size, mode_count, win_size, win_size)
    back_im = back_im.reshape(batch_size, mode_count, win_size, win_size)
    grad_obj_re = jnp.sum(probe_re * back_re + probe_im * back_im, axis=1)
    grad_obj_im = jnp.sum(probe_re * back_im - probe_im * back_re, axis=1)
    grad_probe_re = jnp.sum(slot_re * back_re + slot_im * back_im, axis=0)
    grad_probe_im = jnp.sum(slot_re * back_im - slot_im * back_re, axis=0)
    return (
        slot_losses,
        jnp.stack([grad_obj_re, grad_obj_im], axis=1),
        jnp.stack([grad_probe_re, grad_probe_im], axis=1),
    )


def extend_tile(tile, win_size):
    right_rim = from_behind(tile[:, :, :win_size], "col", -1)
    widened = jnp.concatenate([tile, right_rim], axis=2)
    below_rim = from_behind(widened, "row", -1)
    return jnp.concatenate([widened, below_rim], axis=1)


def fold_back(gradient, tile_rows, tile_cols, win_size):
    down_strip = from_behind(gradient[:, tile_rows:, :], "row", 1)
    gradient = gradient[:, :tile_rows, :].at[:, :win_size, :].add(down_strip)
    right_strip = from_behind(gradient[:, :, tile_cols:], "col", 1)
    return gradient[:, :, :tile_cols].at[:, :, :win_size].add(right_strip)


def body(object_field, probe, corners, counts, amplitude):
    tile_rows = object_field.shape[1]
    tile_cols = object_field.shape[2]
    win_size = probe.shape[-1]
    slot_total = corners.shape[3]
    iter_total = corners.shape[0]
    cosine, sine_part = dft_tables(win_size)
    anchor = jnp.stack([lax.axis_index("row") * tile_rows, lax.axis_index("col") * tile_cols])
    object_now = object_field
    probe_now = probe
    tile_losses = []
    for iteration in range(iter_total):
        extended = extend_tile(object_now, win_size)
        local_corner = corners[iteration, 0, 0] - anchor[None, :]
        live_count = counts[iteration, 0, 0]
        measured_all = amplitude[iteration, 0, 0]
        grad_start = jnp.zeros(extended.shape, jnp.float32)

        def cut_window(corner_row, corner_col):
            return lax.dynamic_slice(
                extended,
                (jnp.zeros((), jnp.int32), corner_row, corner_col),
                (2, win_size, win_size),
            )

        patches = jax.vmap(cut_window)(local_corner[:, 0], local_corner[:, 1])
        alive_mask = (jnp.arange(slot_total) < live_count).astype(jnp.float32)
        slot_losses, obj_grads, probe_part = window_terms(
            patches[:, 0],
            patches[:, 1],
            measured_all.astype(jnp.float32),
            alive_mask,
            probe_now,
            cosine,
            sine_part,
        )

        def deposit(index, grad_total):
            start = (jnp.zeros((), jnp.int32), local_corner[index, 0], local_corner[index, 1])
            previous = lax.dynamic_slice(grad_total, start, (2, win_size, win_size))
            return lax.dynamic_update_slice(grad_total, previous + obj_grads[index], start)

        object_grad = lax.fori_loop(0, slot_total, deposit, grad_start)
        loss_here = jnp.sum(slot_losses)
        tile_losses.append(loss_here)
        total_loss = lax.psum(loss_here, ("row", "col"))
        owned_grad = fold_back(object_grad, tile_rows, tile_cols, win_size)
        probe_grad = lax.psum(probe_part, ("row", "col"))
        object_square = lax.psum(jnp.sum(owned_grad * owned_grad), ("row", "col"))
        step_rate = total_loss / (object_square + jnp.sum(probe_grad * probe_grad) + 1e-06)
        object_now = object_now - step_rate * owned_grad
        probe_now = probe_now - step_rate * probe_grad
    losses_out = jnp.stack(tile_losses).reshape(iter_total, 1, 1)
    return (object_now, probe_now, losses_out)


def solution(mesh):
    in_specs = (
        P(None, "row", "col"),
        P(),
        P(None, "row", "col", None, None),
        P(None, "row", "col"),
        P(None, "row", "col", None, None, None),
    )
    out_specs = (P(None, "row", "col"), P(), P(None, "row", "col"))
    return jax.shard_map(body, mesh=mesh, in_specs=in_specs, out_specs=out_specs, check_vma=False)
```

profile of v0, /device:TPU:1, one launch (start us, length us, event | category | flops | bytes accessed | tf_op | source)
XLA Modules:
  0.0 866.0 jit_solution(10392306321167839662)
XLA Ops:
  8.4 3.5 collective-permute-start
  12.9 7.8 collective-permute-done
  25.6 27.8 %collective-permute-done.1 = f32[2,256,768]{2,1,0:T(8,128)} collective-permute-done((f32[2,256,768]{2,1,0:T(8,128)}, f32[2,256,768]{2,1,0:T(8,128)}, u32[]{:S(2)}, u32[]{:S(2)}) %collective-permute-start.1) | collective-permute-done | bytes 1572896 | tf_op jit(solution)/shard_map/ppermute | solution.py:14
  56.5 5.9 while.36
  64.8 3.6 fusion.107
  68.4 3.6 fusion.104
  72.0 3.7 convolution_add_fusion.3
  75.7 3.8 fusion.26
  79.5 3.6 fusion.24
  83.1 3.7 convolution_subtract_fusion.3
  86.9 3.9 fusion.32
  90.7 5.3 multiply_add_fusion.2
  96.1 2.4 reduce_sum.162
  101.6 3.6 fusion.101
  105.2 4.1 fusion.98
  109.3 3.7 convolution_add_fusion.2
  113.0 3.6 fusion.18
  116.6 3.6 fusion.16
  120.2 3.8 convolution_subtract_fusion.2
  124.0 3.6 fusion.38
  127.7 3.6 fusion.41
  135.3 24.3 %while.34 = (s32[]{:T(128)}, f32[2,512,768]{2,1,0:T(8,128)}, s32[2,2]{1,0:T(2,128)S(1)}, f32[2,2,256,256]{3,2,1,0:T(8,128)S(1)}, s32[]{:T(128)}, /*index=5*/s32[]{:T(128)}, s32[]{:T(128)}, s32[]{:T(128)}) while((s32[]{:T(128)}, f32[2,512,768]{2,1,0:T(8,128)}, s32[2,2]{1,0:T(2,128)S(1)}, f32[2,2,256,256]{3,2,1,0:T(8,128)S(1)}, s32[]{:T(128)}, ...), condition=%wide.region_7.8_spmd, body=%wide.region_6.7_spmd.sunk | while | flops 131080 | bytes 2621629 | solution.py:136
  141.1 6.1 dynamic_update_slice.16
  153.0 6.5 dynamic_update_slice.16
  161.2 4.0 collective-permute-start.2
  165.2 28.9 %collective-permute-done.2 = f32[2,256,768]{2,1,0:T(8,128)S(1)} collective-permute-done((f32[2,256,768]{2,1,0:T(8,128)S(1)}, f32[2,256,768]{2,1,0:T(8,128)S(1)}, u32[]{:S(2)}, u32[]{:S(2)}) %collective-permute-start.2) | collective-permute-done | bytes 1572896 | tf_op jit(solution)/shard_map/ppermute | solution.py:14
  195.4 12.3 %collective-permute-start.3 = (f32[2,256,256]{2,1,0:T(8,128)S(1)}, f32[2,256,256]{2,1,0:T(8,128)S(1)}, u32[]{:S(2)}, u32[]{:S(2)}) collective-permute-start(f32[2,256,256]{2,1,0:T(8,128)S(1)} %slice.234), channel_id=1, source_target_pairs={{0,1},{1,2},{2,3},{3,4},{4,5},{5,6},{6,7},{8,9},{9,10},{10,11},{11... | collective-permute-start | bytes 1572872 | tf_op jit(solution)/shard_map/ppermute | solution.py:14
  215.8 145.9 %all-reduce.5.cloned.1.call-done = f32[3,2,256,256]{3,2,1,0:T(8,128)} async-done(((f32[3,2,256,256]{3,2,1,0:T(8,128)}), f32[3,2,256,256]{3,2,1,0:T(8,128)}) %all-reduce.5.cloned.1.call-update) | async-done | bytes 1572880 | tf_op jit(solution)/shard_map/psum | solution.py:141
  361.8 2.4 multiply_reduce_fusion.1
  364.2 63.8 %all-reduce.1 = (f32[]{:T(128)}, f32[]{:T(128)}) all-reduce(f32[]{:T(128)} %fusion.123, f32[]{:T(128)} %multiply_reduce_fusion.3), channel_id=1, replica_groups=mesh['row'=16,'col'=8] {'row','col'}, use_global_device_ids=true, to_apply=%region_3.4 | all-reduce | flops 2 | bytes 16 | tf_op jit(solution)/shard_map/psum | solution.py:139
  430.3 2.5 collective-permute-start.4
  432.8 7.9 collective-permute-done.4
  447.1 27.7 %collective-permute-done.5 = f32[2,256,768]{2,1,0:T(8,128)} collective-permute-done((f32[2,256,768]{2,1,0:T(8,128)}, f32[2,256,768]{2,1,0:T(8,128)}, u32[]{:S(2)}, u32[]{:S(2)}) %collective-permute-start.5) | collective-permute-done | bytes 1572896 | tf_op jit(solution)/shard_map/ppermute | solution.py:14
  474.8 3.3 pad_maximum_fusion.1
  479.2 8.5 while.37
  479.8 3.4 bitcast_dynamic-update-slice_fusion.5
  483.8 3.4 bitcast_dynamic-update-slice_fusion.5
  490.0 3.6 fusion.95
  493.6 3.6 fusion.92
  497.3 3.7 convolution_add_fusion.1
  500.9 3.8 fusion.10
  504.7 3.6 fusion.8
  508.4 3.7 convolution_subtract_fusion.1
  512.1 3.8 fusion.44
  516.0 5.3 multiply_add_fusion
  521.3 2.4 reduce_sum.171
  527.3 3.6 fusion.89
  530.9 4.0 fusion.86
  535.0 3.7 convolution_add_fusion
  538.6 3.6 fusion.2
  542.2 3.6 fusion
  545.9 3.8 convolution_subtract_fusion
  549.7 3.6 fusion.50
  553.3 3.6 fusion.53
  561.9 26.0 %while.35 = (s32[]{:T(128)}, f32[2,512,768]{2,1,0:T(8,128)}, s32[2,2]{1,0:T(2,128)S(1)}, f32[2,2,256,256]{3,2,1,0:T(8,128)}, s32[]{:T(128)}, /*index=5*/s32[]{:T(128)}, s32[]{:T(128)}, s32[]{:T(128)}) while((s32[]{:T(128)}, f32[2,512,768]{2,1,0:T(8,128)}, s32[2,2]{1,0:T(2,128)S(1)}, f32[2,2,256,256]{3,2,1,0:T(8,128)}, s32[]{:T(128)}, ...), condition=%wide.region_21.22_spmd, body=%wide.region_20.21_spmd.sunk | while | flops 131080 | bytes 2621629 | solution.py:136
  568.3 6.8 dynamic_update_slice.17
  581.2 6.7 dynamic_update_slice.17
  589.6 2.4 collective-permute-start.6
  591.9 30.2 %collective-permute-done.6 = f32[2,256,768]{2,1,0:T(8,128)S(1)} collective-permute-done((f32[2,256,768]{2,1,0:T(8,128)S(1)}, f32[2,256,768]{2,1,0:T(8,128)S(1)}, u32[]{:S(2)}, u32[]{:S(2)}) %collective-permute-start.6) | collective-permute-done | bytes 1572896 | tf_op jit(solution)/shard_map/ppermute | solution.py:14
  624.3 11.7 %collective-permute-start.7 = (f32[2,256,256]{2,1,0:T(8,128)}, f32[2,256,256]{2,1,0:T(8,128)S(1)}, u32[]{:S(2)}, u32[]{:S(2)}) collective-permute-start(f32[2,256,256]{2,1,0:T(8,128)} %slice.240), channel_id=1, source_target_pairs={{0,1},{1,2},{2,3},{3,4},{4,5},{5,6},{6,7},{8,9},{9,10},{10,11},{11... | collective-permute-start | bytes 1572872 | tf_op jit(solution)/shard_map/ppermute | solution.py:14
  645.4 141.4 %all-reduce.7.cloned.1.call-done = f32[3,2,256,256]{3,2,1,0:T(8,128)} async-done(((f32[3,2,256,256]{3,2,1,0:T(8,128)}), f32[3,2,256,256]{3,2,1,0:T(8,128)}) %all-reduce.7.cloned.1.call-update) | async-done | bytes 1572880 | tf_op jit(solution)/shard_map/psum | solution.py:141
  786.8 2.5 multiply_reduce_fusion
  789.3 63.8 %all-reduce = (f32[]{:T(128)}, f32[]{:T(128)}) all-reduce(f32[]{:T(128)} %fusion.125, f32[]{:T(128)} %multiply_reduce_fusion.2), channel_id=1, replica_groups=mesh['row'=16,'col'=8] {'row','col'}, use_global_device_ids=true, to_apply=%region_17.18 | all-reduce | flops 2 | bytes 16 | tf_op jit(solution)/shard_map/psum | solution.py:139
  855.1 2.5 multiply_subtract_fusion.4
  (139 shorter events, 79.0 us)
Async XLA Ops:
  7.2 4.7 copy-start.10
  7.2 354.6 %all-reduce.5.cloned.1.call-start = ((), (), s32[]{:S(2)}) async-start(), calls=%async_computation | async-start | bytes 3145728 | tf_op jit(solution)/shard_map/psum | solution.py:141
  8.4 14.5 %copy-start.29 = (s32[2,1,1]{0,2,1:T(1,128)S(1)}, s32[2,1,1]{0,2,1:T(1,128)}, u32[]{:S(2)}) copy-start(s32[2,1,1]{0,2,1:T(1,128)} %param.24) | copy-start | bytes 28
  8.4 15.8 %copy-start.28 = (s32[2,1,1,2,2]{4,3,2,1,0:T(2,128)S(1)}, s32[2,1,1,2,2]{4,3,2,1,0:T(2,128)}, u32[]{:S(2)}) copy-start(s32[2,1,1,2,2]{4,3,2,1,0:T(2,128)} %param.23) | copy-start | bytes 100
  8.4 15.9 %copy-start.12 = (f32[3,2,256,256]{3,2,1,0:T(8,128)S(1)}, f32[3,2,256,256]{3,2,1,0:T(8,128)}, u32[]{:S(2)}) copy-start(f32[3,2,256,256]{3,2,1,0:T(8,128)} %param.22) | copy-start | bytes 4718596
  8.4 12.3 %collective-permute-start = (f32[2,256,256]{2,1,0:T(8,128)S(1)}, f32[2,256,256]{2,1,0:T(8,128)S(1)}, u32[]{:S(2)}, u32[]{:S(2)}) collective-permute-start(f32[2,256,256]{2,1,0:T(8,128)S(1)} %slice.174), channel_id=1, source_target_pairs={{1,0},{2,1},{3,2},{4,3},{5,4},{6,5},{7,6},{9,8},{10,9},{11,10},{12... | collective-permute-start | bytes 1572872 | tf_op jit(solution)/shard_map/ppermute | solution.py:14
  21.6 31.8 %collective-permute-start.1 = (f32[2,256,768]{2,1,0:T(8,128)}, f32[2,256,768]{2,1,0:T(8,128)}, u32[]{:S(2)}, u32[]{:S(2)}) collective-permute-start(f32[2,256,768]{2,1,0:T(8,128)} %constant_dynamic-update-slice_fusion), channel_id=1, source_target_pairs={{8,0},{16,8},{24,16},{32,24},{40,32},{48,40},{56,48},{64,56},{72,6... | collective-permute-start | bytes 4718600 | tf_op jit(solution)/shard_map/ppermute | solution.py:14
  62.4 1.4 copy-start.8
  62.4 1.7 copy-start.9
  63.8 0.8 copy-start.14
  63.8 1.0 copy-start.16
  127.7 3.7 copy-start.15
  127.7 3.7 copy-start.17
  159.5 34.5 %copy-start.1 = (f32[2,512,768]{2,1,0:T(8,128)S(1)}, f32[2,512,768]{2,1,0:T(8,128)}, u32[]{:S(2)}) copy-start(f32[2,512,768]{2,1,0:T(8,128)} %get-tuple-element.225) | copy-start | bytes 9437188
  161.2 32.8 %collective-permute-start.2 = (f32[2,256,768]{2,1,0:T(8,128)S(1)}, f32[2,256,768]{2,1,0:T(8,128)S(1)}, u32[]{:S(2)}, u32[]{:S(2)}) collective-permute-start(f32[2,256,768]{2,1,0:T(8,128)S(1)} %slice.183), channel_id=1, source_target_pairs={{0,8},{8,16},{16,24},{24,32},{32,40},{40,48},{48,56},{56,64},{64,7... | collective-permute-start | bytes 4718600 | tf_op jit(solution)/shard_map/ppermute | solution.py:14
  194.0 13.7 %copy-start.25 = (f32[3,256,256]{2,1,0:T(8,128)S(1)}, f32[3,256,256]{2,1,0:T(8,128)}, u32[]{:S(2)}) copy-start(f32[3,256,256]{2,1,0:T(8,128)} %get-tuple-element.250) | copy-start | bytes 2359300
  194.2 1.1 copy-start.5
  195.4 12.4 %copy-start.24 = (f32[3,256,256]{2,1,0:T(8,128)S(1)}, f32[3,256,256]{2,1,0:T(8,128)}, u32[]{:S(2)}) copy-start(f32[3,256,256]{2,1,0:T(8,128)} %get-tuple-element.249) | copy-start | bytes 2359300
  195.4 18.4 %collective-permute-start.3 = (f32[2,256,256]{2,1,0:T(8,128)S(1)}, f32[2,256,256]{2,1,0:T(8,128)S(1)}, u32[]{:S(2)}, u32[]{:S(2)}) collective-permute-start(f32[2,256,256]{2,1,0:T(8,128)S(1)} %slice.234), channel_id=1, source_target_pairs={{0,1},{1,2},{2,3},{3,4},{4,5},{5,6},{6,7},{8,9},{9,10},{10,11},{11... | collective-permute-start | bytes 1572872 | tf_op jit(solution)/shard_map/ppermute | solution.py:14
  209.0 577.8 %all-reduce.7.cloned.1.call-start = ((), (), s32[]{:S(2)}) async-start(), calls=%async_computation.1 | async-start | bytes 3145728 | tf_op jit(solution)/shard_map/psum | solution.py:141
  215.0 215.0 %copy-start.11 = (f32[2,256,512]{2,1,0:T(8,128)S(1)}, f32[2,256,512]{2,1,0:T(8,128)}, u32[]{:S(2)}) copy-start(f32[2,256,512]{2,1,0:T(8,128)} %param.21) | copy-start | bytes 3145732
  430.3 10.5 %collective-permute-start.4 = (f32[2,256,256]{2,1,0:T(8,128)S(1)}, f32[2,256,256]{2,1,0:T(8,128)S(1)}, u32[]{:S(2)}, u32[]{:S(2)}) collective-permute-start(f32[2,256,256]{2,1,0:T(8,128)S(1)} %slice.236), channel_id=1, source_target_pairs={{1,0},{2,1},{3,2},{4,3},{5,4},{6,5},{7,6},{9,8},{10,9},{11,10},{12... | collective-permute-start | bytes 1572872 | tf_op jit(solution)/shard_map/ppermute | solution.py:14
  440.8 1.3 copy-start.26
  442.1 32.7 %collective-permute-start.5 = (f32[2,256,768]{2,1,0:T(8,128)}, f32[2,256,768]{2,1,0:T(8,128)}, u32[]{:S(2)}, u32[]{:S(2)}) collective-permute-start(f32[2,256,768]{2,1,0:T(8,128)} %pad_maximum_fusion.3), channel_id=1, source_target_pairs={{8,0},{16,8},{24,16},{32,24},{40,32},{48,40},{56,48},{64,56},{72,6... | collective-permute-start | bytes 4718600 | tf_op jit(solution)/shard_map/ppermute | solution.py:14
  446.0 28.8 %copy-start.27 = (f32[2,256,256]{2,1,0:T(8,128)S(1)}, f32[2,256,256]{2,1,0:T(8,128)}, u32[]{:S(2)}) copy-start(f32[2,256,256]{2,1,0:T(8,128)} %copy-done.26) | copy-start | bytes 1572868
  487.7 1.4 copy-start.6
  489.0 0.8 copy-start.18
  489.1 1.0 copy-start.20
  516.0 5.4 copy-start.2
  553.3 3.7 copy-start.7
  553.3 3.7 copy-start.19
  553.3 3.7 copy-start.21
  587.9 34.2 %copy-start = (f32[2,512,768]{2,1,0:T(8,128)S(1)}, f32[2,512,768]{2,1,0:T(8,128)}, u32[]{:S(2)}) copy-start(f32[2,512,768]{2,1,0:T(8,128)} %get-tuple-element.226) | copy-start | bytes 9437188
  589.6 32.5 %collective-permute-start.6 = (f32[2,256,768]{2,1,0:T(8,128)S(1)}, f32[2,256,768]{2,1,0:T(8,128)S(1)}, u32[]{:S(2)}, u32[]{:S(2)}) collective-permute-start(f32[2,256,768]{2,1,0:T(8,128)S(1)} %slice.198), channel_id=1, source_target_pairs={{0,8},{8,16},{16,24},{24,32},{32,40},{40,48},{48,56},{56,64},{64,7... | collective-permute-start | bytes 4718600 | tf_op jit(solution)/shard_map/ppermute | solution.py:14
  622.1 13.9 %copy-start.23 = (f32[3,256,256]{2,1,0:T(8,128)S(1)}, f32[3,256,256]{2,1,0:T(8,128)}, u32[]{:S(2)}) copy-start(f32[3,256,256]{2,1,0:T(8,128)} %get-tuple-element.248) | copy-start | bytes 2359300
  622.3 1.1 copy-start.3
  623.4 12.6 %copy-start.22 = (f32[3,256,256]{2,1,0:T(8,128)S(1)}, f32[3,256,256]{2,1,0:T(8,128)}, u32[]{:S(2)}) copy-start(f32[3,256,256]{2,1,0:T(8,128)} %get-tuple-element.247) | copy-start | bytes 2359300
  624.3 18.1 %collective-permute-start.7 = (f32[2,256,256]{2,1,0:T(8,128)}, f32[2,256,256]{2,1,0:T(8,128)S(1)}, u32[]{:S(2)}, u32[]{:S(2)}) collective-permute-start(f32[2,256,256]{2,1,0:T(8,128)} %slice.240), channel_id=1, source_target_pairs={{0,1},{1,2},{2,3},{3,4},{4,5},{5,6},{6,7},{8,9},{9,10},{10,11},{11... | collective-permute-start | bytes 1572872 | tf_op jit(solution)/shard_map/ppermute | solution.py:14
  637.3 5.1 slice-start
  643.5 1.0 copy-start.4
  855.1 2.6 copy-start.13
Sparse Core Ops, SparseCore 0:
  209.2 152.5 all-reduce.4
  637.4 149.3 all-reduce.6
where the time goes:
time: 878 us; the launch traced here: 866 us
  waiting for transfers between devices  422 us (48%)
  blocking collectives  128 us (15%)
  matrix products  122 us (14%)
  local copies, waits for them, and re-layouts  66.9 us (8%)
  other arithmetic  53.8 us (6%)
  starting transfers between devices  39 us (4%)
  between operations  18.9 us (2%)
  loops' own time  16.3 us (2%)
    psum x2, waiting for transfers between devices, body(): probe_grad = lax.psum(probe_part, ('row', 'col'))  287 us
    ppermute x8, waiting for transfers between devices, from_behind(): lax.ppermute(value, axis, [(source, source + steps) for source in range(l...  134 us
    psum x2, blocking collectives, body(): total_loss = lax.psum(loss_here, ('row', 'col'))  128 us
    ppermute x8, starting transfers between devices, from_behind(): lax.ppermute(value, axis, [(source, source + steps) for source in range(l...  38.9 us
    dynamic_update_slice x4, local copies, waits for them, and re-layouts, deposit(): lax.dynamic_update_slice(grad_total, previous + obj_grads[index], start)  26.1 us
    dot_general x4, matrix products, dft_pair(): jnp.einsum('bjn,nk->bjk', left_re, sine_part, precision=PRECISE)  18 us
  transfers between devices with their start and end apart: 10, of which 10 were waited for; matrix products, arithmetic and copies ran while one was open for 2% of the time, Pallas kernels for 0%

commit v1 on v0

v1 whole, which is shorter than its diff:
```python
import math

import jax
import jax.numpy as jnp
import numpy as np
from jax import lax
from jax.experimental import pallas as pl
from jax.experimental.pallas import tpu as pltpu
from jax.sharding import PartitionSpec as P

WIN = 256
HALF = 128
MODES = 3
CAP = 2
AREA = float(WIN * WIN)


def split_bf16(value):
    high = value.astype(jnp.bfloat16)
    low = (value - high.astype(jnp.float32)).astype(jnp.bfloat16)
    return high, low


def transform_tables():
    freq = np.arange(HALF)[:, None]
    pixel = np.arange(HALF)[None, :]
    lefts, rights = [], []
    for odd in (0, 1):
        angle = -2.0 * math.pi * (((2 * freq + odd) * pixel) % WIN) / WIN
        cos, sin = np.cos(angle) / math.sqrt(WIN), np.sin(angle) / math.sqrt(WIN)
        matrix = np.block([[cos, -sin], [sin, cos]])
        for table in (matrix, matrix.T):
            table = table.astype(np.float32)
            high = table.astype(jnp.bfloat16)
            low = (table - high.astype(np.float32)).astype(jnp.bfloat16)
            lefts.append(np.concatenate([high, high, low], axis=1))
            rights.append(np.concatenate([high, high, low], axis=0))
    left = np.stack([lefts[0], lefts[2], lefts[1], lefts[3]])
    right = np.stack([rights[1], rights[3], rights[0], rights[2]])
    order = np.concatenate([np.arange(0, WIN, 2), np.arange(1, WIN, 2)])
    shuffle = np.zeros((WIN, WIN), np.float32)
    shuffle[np.arange(WIN), order] = 1.0
    return left, right, np.stack([shuffle, shuffle.T]).astype(jnp.bfloat16)


def left_apply(table, data):
    high, low = split_bf16(data)
    return jnp.dot(table, jnp.concatenate([high, low, high], axis=0), preferred_element_type=jnp.float32)


def right_apply(data, table):
    high, low = split_bf16(data)
    return jnp.dot(jnp.concatenate([high, low, high], axis=1), table, preferred_element_type=jnp.float32)


def slot_kernel(second, last_slot, *refs):
    refs = list(refs)
    place = refs.pop(0)
    rate_ref = refs.pop(0) if second else None
    patch_ref = refs.pop(0)
    patch_grad = refs.pop(0) if second else None
    probe_ref = refs.pop(0)
    probe_grad = refs.pop(0) if second else None
    amp_ref, left_ref, right_ref, shuffle_ref = refs[:4]
    refs = refs[4:]
    before = refs.pop(0) if last_slot else None
    out_grad, out_probe, out_loss, obj, field, factor = refs
    row, col, alive = place[0], place[1], place[2]

    def probe_plane(index):
        plane = probe_ref[index]
        if second:
            step = jnp.concatenate([probe_grad[2 * index], probe_grad[2 * index + 1]], axis=1)
            plane = plane - rate_ref[0] * step
        return plane

    for part in range(2):
        value = patch_ref[part]
        if second:
            value = value - rate_ref[0] * patch_grad[part]
        value = pltpu.roll(value, (WIN - row) % WIN, 0)
        obj[part] = pltpu.roll(value, (WIN - col) % WIN, 1)

    for mode in range(MODES):
        probe_re, probe_im = probe_plane(2 * mode), probe_plane(2 * mode + 1)
        exit_re = probe_re * obj[0] - probe_im * obj[1]
        exit_im = probe_re * obj[1] + probe_im * obj[0]
        half = []
        for odd in range(2):
            sign = -1.0 if odd else 1.0
            folded = jnp.concatenate(
                [exit_re[:HALF] + sign * exit_re[HALF:], exit_im[:HALF] + sign * exit_im[HALF:]], axis=0
            )
            half.append(left_apply(left_ref[odd], folded))
        mid_re = jnp.concatenate([half[0][:HALF], half[1][:HALF]], axis=0)
        mid_im = jnp.concatenate([half[0][HALF:], half[1][HALF:]], axis=0)
        for odd in range(2):
            sign = -1.0 if odd else 1.0
            folded = jnp.concatenate(
                [mid_re[:, :HALF] + sign * mid_re[:, HALF:], mid_im[:, :HALF] + sign * mid_im[:, HALF:]], axis=1
            )
            field[mode, odd] = right_apply(folded, right_ref[odd])

    amp = jnp.dot(shuffle_ref[0], amp_ref[...], preferred_element_type=jnp.float32).astype(jnp.bfloat16)
    amp = jnp.dot(amp, shuffle_ref[1], preferred_element_type=jnp.float32)
    loss = jnp.zeros((WIN, HALF), jnp.float32)
    for odd in range(2):
        total = jnp.ones((WIN, HALF), jnp.float32)
        for mode in range(MODES):
            real, imag = field[mode, odd, :, :HALF], field[mode, odd, :, HALF:]
            total = total + (real * real + imag * imag)
        inverse = lax.rsqrt(total)
        measured = amp[:, odd * HALF : (odd + 1) * HALF]
        gap = total * inverse - measured
        loss = loss + gap * gap
        factor[odd] = (1.0 - measured * inverse) * (2.0 / AREA * alive.astype(jnp.float32))
    out_loss[...] = jnp.sum(loss.reshape(WIN // 8, 8, HALF), axis=0) * (alive.astype(jnp.float32) / AREA)

    grad_re = jnp.zeros((WIN, WIN), jnp.float32)
    grad_im = jnp.zeros((WIN, WIN), jnp.float32)
    for mode in range(MODES):
        half = []
        for odd in range(2):
            scale = jnp.concatenate([factor[odd], factor[odd]], axis=1)
            half.append(right_apply(field[mode, odd] * scale, right_ref[2 + odd]))
        mid_re = jnp.concatenate(
            [half[0][:, :HALF] + half[1][:, :HALF], half[0][:, :HALF] - half[1][:, :HALF]], axis=1
        )
        mid_im = jnp.concatenate(
            [half[0][:, HALF:] + half[1][:, HALF:], half[0][:, HALF:] - half[1][:, HALF:]], axis=1
        )
        back = []
        for odd in range(2):
            rows = slice(odd * HALF, (odd + 1) * HALF)
            back.append(left_apply(left_ref[2 + odd], jnp.concatenate([mid_re[rows], mid_im[rows]], axis=0)))
        back_re = jnp.concatenate([back[0][:HALF] + back[1][:HALF], back[0][:HALF] - back[1][:HALF]], axis=0)
        back_im = jnp.concatenate([back[0][HALF:] + back[1][HALF:], back[0][HALF:] - back[1][HALF:]], axis=0)
        probe_re, probe_im = probe_plane(2 * mode), probe_plane(2 * mode + 1)
        grad_re = grad_re + (probe_re * back_re + probe_im * back_im)
        grad_im = grad_im + (probe_re * back_im - probe_im * back_re)
        terms = (obj[0] * back_re + obj[1] * back_im, obj[0] * back_im - obj[1] * back_re)
        for part in range(2):
            for side in range(2):
                index = (2 * mode + part) * 2 + side
                value = terms[part][:, side * HALF : (side + 1) * HALF]
                if last_slot:
                    value = value + before[index]
                out_probe[index] = value
    for part, value in enumerate((grad_re, grad_im)):
        out_grad[part] = pltpu.roll(pltpu.roll(value, row, 0), col, 1)


def run_slot(place, rate, patch, patch_grad, probe, probe_grad, amp, tables, before):
    second, last_slot = rate is not None, before is not None
    smem, vmem = pl.BlockSpec(memory_space=pltpu.SMEM), pl.BlockSpec(memory_space=pltpu.VMEM)
    args, specs = [place], [smem]
    if second:
        args.append(rate), specs.append(smem)
    big = [patch] + ([patch_grad] if second else []) + [probe] + ([probe_grad] if second else [])
    big += [amp, *tables] + ([before] if last_slot else [])
    args += big
    specs += [vmem] * len(big)
    return pl.pallas_call(
        lambda *refs: slot_kernel(second, last_slot, *refs),
        out_shape=(
            jax.ShapeDtypeStruct((2, WIN, WIN), jnp.float32),
            jax.ShapeDtypeStruct((4 * MODES, WIN, HALF), jnp.float32),
            jax.ShapeDtypeStruct((8, HALF), jnp.float32),
        ),
        in_specs=specs,
        out_specs=(vmem, vmem, vmem),
        scratch_shapes=[
            pltpu.VMEM((2, WIN, WIN), jnp.float32),
            pltpu.VMEM((MODES, 2, WIN, WIN), jnp.float32),
            pltpu.VMEM((2, WIN, HALF), jnp.float32),
        ],
        compiler_params=pltpu.CompilerParams(vmem_limit_bytes=40 * 1024 * 1024),
        cost_estimate=pl.CostEstimate(flops=5_000_000_000, bytes_accessed=6_000_000, transcendentals=65536),
    )(*args)


def shift(value, axis, steps):
    count = lax.axis_size(axis)
    first, last = max(0, -steps), min(count, count - steps)
    return lax.ppermute(value, axis, [(source, source + steps) for source in range(first, last)])


def row_mask(corner):
    return (lax.broadcasted_iota(jnp.int32, (WIN, WIN), 0) >= corner[0] % WIN)[None]


def col_mask(corner):
    return (lax.broadcasted_iota(jnp.int32, (WIN, WIN), 1) >= corner[1] % WIN)[None]


def block_of(corner):
    return (corner[1] // WIN) % 2


def pick(blocks, corner):
    left = block_of(corner) == 0
    return jnp.where(
        col_mask(corner), jnp.where(left, blocks[0], blocks[1]), jnp.where(left, blocks[1], blocks[2])
    )


def spread(window, corner, block):
    here = jnp.where(block_of(corner) == block, col_mask(corner), False)
    spill = jnp.where(block_of(corner) == block - 1, ~col_mask(corner), False)
    return jnp.where(here | spill, window, 0.0)


def body(object_field, probe, corners, counts, amplitude):
    core_pairs = lax.axis_size("col") // 2
    row_count = lax.axis_size("row")
    core = lax.axis_index("col") % 2
    layers = [[2 * z + c for z in range(core_pairs)] for c in range(2)]
    swap = [(c, c ^ 1) for c in range(2 * core_pairs)]
    tables = [jnp.asarray(table) for table in transform_tables()]
    probe = probe.reshape(2 * MODES, WIN, WIN)
    corners = corners[:, 0, 0]
    corners_above = shift(corners, "row", 1)
    corners_below = shift(corners, "row", -1)
    rim = shift(object_field[:, :, :WIN], "col", -1)
    blocks = [object_field[:, :, :WIN], object_field[:, :, WIN:], rim]

    def place_of(iteration, slot):
        corner = corners[iteration, slot]
        alive = (slot < counts[iteration, 0, 0]).astype(jnp.int32)
        return jnp.stack([corner[0] % WIN, corner[1] % WIN, alive])

    def patch_of(iteration, slot, after=None):
        packed = pick(blocks, corners_above[iteration, slot])
        if after is not None:
            packed, after = lax.optimization_barrier((packed, after))
        below = shift(packed, "row", -1)
        return jnp.where(row_mask(corners[iteration, slot]), pick(blocks, corners[iteration, slot]), below)

    def reduce_scatter(value):
        value = value.reshape(2, core_pairs * row_count, -1, HALF)
        other = lax.ppermute(lax.dynamic_index_in_dim(value, 1 - core, 0, keepdims=False), "col", swap)
        mine = lax.dynamic_index_in_dim(value, core, 0, keepdims=False) + other
        mine = mine.reshape(core_pairs, row_count, -1, HALF)
        mine = lax.all_to_all(mine, "col", 0, 0, axis_index_groups=layers, tiled=True).sum(axis=0)
        return lax.all_to_all(mine, "row", 0, 0, tiled=True).sum(axis=0)

    def all_gather(chunk, scalars):
        depth = chunk.shape[0]
        sent = jnp.concatenate([chunk, scalars], axis=0)
        got = lax.all_to_all(jnp.broadcast_to(sent[None], (row_count, *sent.shape)), "row", 0, 0, tiled=True)
        sent = jnp.concatenate([got[:, :depth].reshape(-1, HALF), got[:, depth:].sum(axis=0)], axis=0)
        got = lax.all_to_all(
            jnp.broadcast_to(sent[None], (core_pairs, *sent.shape)),
            "col", 0, 0, axis_index_groups=layers, tiled=True,
        )
        depth *= row_count
        mine, sums = got[:, :depth].reshape(-1, HALF), got[:, depth:].sum(axis=0)
        other = lax.ppermute(mine, "col", swap)
        sums = sums + lax.ppermute(sums, "col", swap)
        halves = jnp.where(core == 0, jnp.stack([mine, other]), jnp.stack([other, mine]))
        return halves.reshape(4 * MODES, WIN, HALF), sums

    def scalar_rows(loss, square_object, square_probe):
        lane = lax.broadcasted_iota(jnp.int32, (8, HALF), 0)
        return jnp.where(lane == 0, loss, jnp.where(lane == 1, square_object, jnp.where(lane == 2, square_probe, 0.0)))

    def finish(chunk, loss, tile_grad):
        square_object = jnp.sum(tile_grad * tile_grad)
        gathered, sums = all_gather(chunk, scalar_rows(loss, square_object, jnp.sum(chunk * chunk)))
        rate = sums[0, 0] / (sums[1, 0] + sums[2, 0] + 1e-06)
        return gathered, rate

    patches = [patch_of(0, slot) for slot in range(CAP)]
    grads, ups, downs, losses, probe_part = [], [], [], [], None
    for slot in range(CAP):
        grad, probe_part, loss = run_slot(
            place_of(0, slot), None, patches[slot], None, probe, None, amplitude[0, 0, 0, slot], tables, probe_part
        )
        grads.append(grad)
        downs.append(shift(grad, "row", 1))
        ups.append(shift(grad, "row", -1))
        losses.append(loss)
    loss_first = sum(jnp.sum(loss) for loss in losses)
    chunk = reduce_scatter(probe_part)
    next_patches = [patch_of(1, slot, chunk) for slot in range(CAP)]

    def column_block(block):
        top, bottom = 0.0, 0.0
        for slot in range(CAP):
            own = spread(grads[slot], corners[0, slot], block)
            mask = row_mask(corners[0, slot])
            above = spread(downs[slot], corners_above[0, slot], block)
            below = spread(ups[slot], corners_below[0, slot], block)
            top = top + jnp.where(mask, own, 0.0) + jnp.where(row_mask(corners_above[0, slot]), 0.0, above)
            bottom = bottom + jnp.where(mask, 0.0, own) + jnp.where(row_mask(corners_below[0, slot]), below, 0.0)
        return jnp.stack([top, bottom])

    sums = [column_block(block) for block in range(3)]
    from_left = shift(sums[2], "col", 1)
    from_right = shift(sums[0], "col", -1)
    sums = [sums[0] + from_left, sums[1], sums[2] + from_right]
    tile_grad = jnp.concatenate([sums[0][0], sums[1][0]], axis=2)
    patch_grads = [
        jnp.where(
            row_mask(corners[1, slot]),
            pick([s[0] for s in sums], corners[1, slot]),
            pick([s[1] for s in sums], corners[1, slot]),
        )
        for slot in range(CAP)
    ]
    probe_grad, rate = finish(chunk, loss_first, tile_grad)
    object_mid = object_field - rate * tile_grad

    grads, downs, losses, probe_part = [], [], [], None
    for slot in range(CAP):
        grad, probe_part, loss = run_slot(
            place_of(1, slot), rate[None], next_patches[slot], patch_grads[slot], probe, probe_grad,
            amplitude[1, 0, 0, slot], tables, probe_part,
        )
        grads.append(grad)
        downs.append(shift(grad, "row", 1))
        losses.append(loss)
    loss_second = sum(jnp.sum(loss) for loss in losses)
    chunk = reduce_scatter(probe_part)

    def top_block(block):
        top = 0.0
        for slot in range(CAP):
            own = spread(grads[slot], corners[1, slot], block)
            above = spread(downs[slot], corners_above[1, slot], block)
            top = top + jnp.where(row_mask(corners[1, slot]), own, 0.0)
            top = top + jnp.where(row_mask(corners_above[1, slot]), 0.0, above)
        return top

    from_left = shift(top_block(2), "col", 1)
    tile_grad = jnp.concatenate([top_block(0) + from_left, top_block(1)], axis=2)
    probe_step, rate_second = finish(chunk, loss_second, tile_grad)
    object_out = object_mid - rate_second * tile_grad

    def unflatten(value):
        return value.reshape(2 * MODES, 2, WIN, HALF).transpose(0, 2, 1, 3).reshape(2 * MODES, WIN, WIN)

    probe_out = (probe - rate * unflatten(probe_grad)) - rate_second * unflatten(probe_step)
    losses_out = jnp.stack([loss_first, loss_second]).reshape(2, 1, 1)
    return (object_out, probe_out.reshape(MODES, 2, WIN, WIN), losses_out)


def solution(mesh):
    in_specs = (
        P(None, "row", "col"),
        P(),
        P(None, "row", "col", None, None),
        P(None, "row", "col"),
        P(None, "row", "col", None, None, None),
    )
    out_specs = (P(None, "row", "col"), P(), P(None, "row", "col"))
    return jax.shard_map(body, mesh=mesh, in_specs=in_specs, out_specs=out_specs, check_vma=False)
```

time: 878 us -> 337 us (0.38); the launches traced: 866 us -> 334 us
  waiting for transfers between devices: 422 us -> 65.4 us
  matrix products: 122 us -> 0 us
  blocking collectives: 128 us -> 25.9 us
  starting transfers between devices: 39 us -> 94.4 us
  local copies, waits for them, and re-layouts: 66.9 us -> 23.8 us
  between operations: 18.9 us -> 54 us
  Pallas kernels: 0 us -> 22.2 us
  loops' own time: 16.3 us -> 0 us
    psum x2 -> x0, waiting for transfers between devices: 287 us -> none  [body(): probe_grad = lax.psum(probe_part, ('row', 'col'))]
    psum x2 -> x0, blocking collectives: 128 us -> none  [body(): total_loss = lax.psum(loss_here, ('row', 'col'))]
    dot_general x32 -> x0, matrix products: 122 us -> none  [the longest x4 18 us: dft_pair(): jnp.einsum('bjn,nk->bjk', left_re, sine_part, precision=PRECISE)]
    ppermute x8 -> x22, waiting for transfers between devices: 134 us -> 48.6 us  [the longest x16 48.6 us: shift(): lax.ppermute(value, axis, [(source, source + steps) for source in range(f...]
    all_to_all x0 -> x6, starting transfers between devices: none -> 44 us  [the longest x2 21.5 us: reduce_scatter(): return lax.all_to_all(mine, 'row', 0, 0, tiled=True).sum(axis=0)]
    dynamic_update_slice x4 -> x0, local copies, waits for them, and re-layouts: 26.1 us -> none  [deposit(): lax.dynamic_update_slice(grad_total, previous + obj_grads[index], start)]
    all_to_all x0 -> x2, blocking collectives: none -> 25.9 us  [the longest x1 15.1 us: all_gather(): lax.all_to_all(jnp.broadcast_to(sent[None], (core_pairs, *sent.shape)), '...]
    pallas_call x0 -> x4, Pallas kernels: none -> 22.2 us  [run_slot(): pl.pallas_call(lambda *refs: slot_kernel(second, last_slot, *refs), out_s...]
  transfers between devices with their start and end apart: 10 -> 28, of which waited for: 10 -> 10; matrix products, arithmetic and copies ran while one was open for 2% -> 13% of each run, Pallas kernels for 0% -> 0%
where the time goes in v1:
time: 337 us; the launch traced here: 334 us
  starting transfers between devices  94.4 us (28%)
  waiting for transfers between devices  65.4 us (19%)
  between operations  54 us (16%)
  other arithmetic  48.3 us (14%)
  blocking collectives  25.9 us (8%)
  local copies, waits for them, and re-layouts  23.8 us (7%)
  Pallas kernels  22.2 us (7%)
    ppermute x16, waiting for transfers between devices, shift(): lax.ppermute(value, axis, [(source, source + steps) for source in range(f...  48.6 us
    ppermute x16, starting transfers between devices, shift(): lax.ppermute(value, axis, [(source, source + steps) for source in range(f...  43 us
    pallas_call x4, Pallas kernels, run_slot(): pl.pallas_call(lambda *refs: slot_kernel(second, last_slot, *refs), out_s...  22.2 us
    all_to_all x2, starting transfers between devices, reduce_scatter(): return lax.all_to_all(mine, 'row', 0, 0, tiled=True).sum(axis=0)  21.5 us
    all_to_all x1, blocking collectives, all_gather(): lax.all_to_all(jnp.broadcast_to(sent[None], (core_pairs, *sent.shape)), '...  15.1 us
    all_to_all x2, starting transfers between devices, reduce_scatter(): lax.all_to_all(mine, 'col', 0, 0, axis_index_groups=layers, tiled=True)  11.1 us
    all_to_all x1, blocking collectives, all_gather(): lax.all_to_all(jnp.broadcast_to(sent[None], (row_count, *sent.shape)), 'r...  10.8 us
    all_to_all x2, waiting for transfers between devices, reduce_scatter(): return lax.all_to_all(mine, 'row', 0, 0, tiled=True).sum(axis=0)  8.47 us
  transfers between devices with their start and end apart: 28, of which 10 were waited for; matrix products, arithmetic and copies ran while one was open for 13% of the time, Pallas kernels for 0%

profile of v1, /device:TPU:1, one launch (start us, length us, event | category | flops | bytes accessed | tf_op | source)
XLA Modules:
  0.0 334.0 jit_solution(4139006558663234730)
XLA Ops:
  0.6 4.2 %collective-permute-start.1 = (s32[2,2,2]{2,1,0:T(2,128)}, s32[2,2,2]{2,1,0:T(2,128)S(1)}, u32[]{:S(2)}, u32[]{:S(2)}) collective-permute-start(s32[2,2,2]{2,1,0:T(2,128)} %bitcast.131), channel_id=1, source_target_pairs={{0,8},{8,16},{16,24},{24,32},{32,40},{40,48},{48,56},{56,64},{64,7... | collective-permute-start | bytes 104 | tf_op jit(solution)/shard_map/ppermute | solution.py:185
  4.8 1.3 collective-permute-start.7
  7.2 2.9 collective-permute-start
  10.1 1.5 fusion.8
  20.7 1.3 fusion.10
  32.3 1.3 select_select_fusion.1
  33.6 1.3 collective-permute-start.3
  34.9 1.3 collective-permute-start.2
  44.3 6.2 %collective-permute-done.3 = f32[2,256,256]{2,1,0:T(8,128)S(1)} collective-permute-done((f32[2,256,256]{2,1,0:T(8,128)}, f32[2,256,256]{2,1,0:T(8,128)S(1)}, u32[]{:S(2)}, u32[]{:S(2)}) %collective-permute-start.3) | collective-permute-done | bytes 524320 | tf_op jit(solution)/shard_map/ppermute | solution.py:185
  50.6 10.6 %collective-permute-done.2 = f32[2,256,256]{2,1,0:T(8,128)} collective-permute-done((f32[2,256,256]{2,1,0:T(8,128)}, f32[2,256,256]{2,1,0:T(8,128)}, u32[]{:S(2)}, u32[]{:S(2)}) %collective-permute-start.2) | collective-permute-done | bytes 524320 | tf_op jit(solution)/shard_map/ppermute | solution.py:185
  61.2 1.9 select_select_fusion.7
  63.7 5.5 %shard_map.103 = (f32[2,256,256]{2,1,0:T(8,128)S(1)}, f32[12,256,128]{2,1,0:T(8,128)S(1)}, f32[8,128]{1,0:T(8,128)S(1)}) custom-call(s32[3]{0:T(128)S(1)} %get-tuple-element.86.refs_0_, f32[2,256,256]{2,1,0:T(8,128)S(1)} %get-tuple-element.47.refs_1_, f32[6,256,256]{2,1,0:T(8,128)S(1)} %bitcast.116, bf16[256,256]{1,0:T(8,128)(2,1)S(1)} %get-tuple-element.52.refs_3_, ...), custom_call_target="tpu_custom_call" | custom-call | flops 5000000000 | bytes 6000000 | tf_op jit(solution)/shard_map/pallas_call | solution.py:163
  69.2 5.7 %shard_map.104 = (f32[2,256,256]{2,1,0:T(8,128)S(1)}, f32[12,256,128]{2,1,0:T(8,128)S(1)}, f32[8,128]{1,0:T(8,128)S(1)}) custom-call(s32[3]{0:T(128)S(1)} %get-tuple-element.85.refs_0_, f32[2,256,256]{2,1,0:T(8,128)S(1)} %get-tuple-element.48.refs_1_, f32[6,256,256]{2,1,0:T(8,128)S(1)} %bitcast.117, bf16[256,256]{1,0:T(8,128)(2,1)S(1)} %get-tuple-element.53.refs_3_, ...), custom_call_target="tpu_custom_call" | custom-call | flops 5000000000 | bytes 6000000 | tf_op jit(solution)/shard_map/pallas_call | solution.py:163
  74.9 1.3 collective-permute-start.9
  76.2 1.3 collective-permute-start.8
  82.1 5.1 %collective-permute-start.6 = (f32[2,256,256]{2,1,0:T(8,128)S(1)}, f32[2,256,256]{2,1,0:T(8,128)S(1)}, u32[]{:S(2)}, u32[]{:S(2)}) collective-permute-start(f32[2,256,256]{2,1,0:T(8,128)S(1)} %get-tuple-element.22), channel_id=1, source_target_pairs={{0,8},{8,16},{16,24},{24,32},{32,40},{40,48},{48,56},{56,64},{64,7... | collective-permute-start | bytes 1572872 | tf_op jit(solution)/shard_map/ppermute | solution.py:185
  87.1 3.4 %collective-permute-start.5 = (f32[2,256,256]{2,1,0:T(8,128)S(1)}, f32[2,256,256]{2,1,0:T(8,128)S(1)}, u32[]{:S(2)}, u32[]{:S(2)}) collective-permute-start(f32[2,256,256]{2,1,0:T(8,128)S(1)} %get-tuple-element.21), channel_id=1, source_target_pairs={{0,8},{8,16},{16,24},{24,32},{32,40},{40,48},{48,56},{56,64},{64,7... | collective-permute-start | bytes 1572872 | tf_op jit(solution)/shard_map/ppermute | solution.py:185
  92.7 9.3 %collective-permute-done.8 = f32[2,256,256]{2,1,0:T(8,128)} collective-permute-done((f32[2,256,256]{2,1,0:T(8,128)S(1)}, f32[2,256,256]{2,1,0:T(8,128)}, u32[]{:S(2)}, u32[]{:S(2)}) %collective-permute-start.8) | collective-permute-done | bytes 524320 | tf_op jit(solution)/shard_map/ppermute | solution.py:185
  102.0 2.5 add_bitcast_fusion
  104.5 4.8 %collective-permute-done.5 = f32[2,256,256]{2,1,0:T(8,128)S(1)} collective-permute-done((f32[2,256,256]{2,1,0:T(8,128)S(1)}, f32[2,256,256]{2,1,0:T(8,128)S(1)}, u32[]{:S(2)}, u32[]{:S(2)}) %collective-permute-start.5) | collective-permute-done | bytes 524320 | tf_op jit(solution)/shard_map/ppermute | solution.py:185
  109.2 1.3 add_bitcast_fusion.1
  111.8 4.8 %collective-permute-start.10 = (f32[2,2,256,256]{3,2,1,0:T(8,128)}, f32[2,2,256,256]{3,2,1,0:T(8,128)}, u32[]{:S(2)}, u32[]{:S(2)}) collective-permute-start(f32[2,2,256,256]{3,2,1,0:T(8,128)} %pad_maximum_fusion.1), channel_id=1, source_target_pairs={{0,1},{1,2},{2,3},{3,4},{4,5},{5,6},{6,7},{8,9},{9,10},{10,11},{11... | collective-permute-start | bytes 3145736 | tf_op jit(solution)/shard_map/ppermute | solution.py:185
  116.6 2.1 bitcast_add_fusion.1
  118.7 4.8 %all-to-all-start = ((f32[4,16,24,128]{3,2,1,0:T(8,128)}), f32[4,16,24,128]{3,2,1,0:T(8,128)}, u32[]{:S(2)}, u32[]{:S(2)}) async-start(f32[4,16,24,128]{3,2,1,0:T(8,128)} %bitcast.124), calls=%async_computation | async-start | bytes 1572864 | tf_op jit(solution)/shard_map/all_to_all | solution.py:244
  123.5 9.4 %collective-permute-done.10 = f32[2,2,256,256]{3,2,1,0:T(8,128)} collective-permute-done((f32[2,2,256,256]{3,2,1,0:T(8,128)}, f32[2,2,256,256]{3,2,1,0:T(8,128)}, u32[]{:S(2)}, u32[]{:S(2)}) %collective-permute-start.10) | collective-permute-done | bytes 1048608 | tf_op jit(solution)/shard_map/ppermute | solution.py:185
  132.8 2.5 fusion.4
  135.3 2.0 collective-permute-start.13
  141.4 1.9 reduce_sum.144
  143.2 11.8 %all-to-all-start.1 = ((f32[16,24,128]{2,1,0:T(8,128)}), f32[16,24,128]{2,1,0:T(8,128)S(1)}, u32[]{:S(2)}, u32[]{:S(2)}) async-start(f32[16,24,128]{2,1,0:T(8,128)} %reduce_sum.144), calls=%async_computation.1 | async-start | bytes 393216 | tf_op jit(solution)/shard_map/all_to_all | solution.py:245
  157.6 4.4 %all-to-all-done.1 = f32[16,24,128]{2,1,0:T(8,128)S(1)} async-done(((f32[16,24,128]{2,1,0:T(8,128)}), f32[16,24,128]{2,1,0:T(8,128)S(1)}, u32[]{:S(2)}, u32[]{:S(2)}) %all-to-all-start.1) | async-done | bytes 196640 | tf_op jit(solution)/shard_map/all_to_all | solution.py:245
  163.3 1.7 fusion.3
  165.2 3.0 select_select_fusion
  171.3 3.5 %all-to-all-start.2 = ((f32[16,32,128]{2,1,0:T(8,128)}), f32[16,32,128]{2,1,0:T(8,128)S(1)}, u32[]{:S(2)}, u32[]{:S(2)}) async-start(f32[16,32,128]{2,1,0:T(8,128)} %broadcast_in_dim.683), calls=%async_computation.2 | async-start | bytes 524288 | tf_op jit(solution)/shard_map/all_to_all | solution.py:250
  174.8 1.3 collective-permute-start.15
  185.3 7.8 %all-to-all-start.3 = ((f32[4,392,128]{2,1,0:T(8,128)}), f32[4,392,128]{2,1,0:T(8,128)}, u32[]{:S(2)}, u32[]{:S(2)}) async-start(f32[4,392,128]{2,1,0:T(8,128)} %broadcast_in_dim.684), calls=%async_computation.3 | async-start | bytes 1605632 | tf_op jit(solution)/shard_map/all_to_all | solution.py:252
  193.2 2.0 select_select_fusion.2
  195.2 1.4 collective-permute-start.12
  196.6 8.3 %all-to-all-done.3 = f32[4,392,128]{2,1,0:T(8,128)} async-done(((f32[4,392,128]{2,1,0:T(8,128)}), f32[4,392,128]{2,1,0:T(8,128)}, u32[]{:S(2)}, u32[]{:S(2)}) %all-to-all-start.3) | async-done | bytes 802848 | tf_op jit(solution)/shard_map/all_to_all | solution.py:252
  204.9 1.3 slice.200
  206.2 1.8 collective-permute-start.14
  208.9 1.8 collective-permute-done.12
  210.7 1.9 select_select_fusion.3
  215.1 1.4 broadcast_multiply_fusion
  218.0 5.5 %shard_map.105 = (f32[2,256,256]{2,1,0:T(8,128)S(1)}, f32[12,256,128]{2,1,0:T(8,128)S(1)}, f32[8,128]{1,0:T(8,128)S(1)}) custom-call(s32[3]{0:T(128)S(1)} %pad_add_fusion.3.refs_0_, f32[1]{0:T(128)} %bitcast.38.refs_1_, f32[2,256,256]{2,1,0:T(8,128)S(1)} %get-tuple-element.42.refs_2_, f32[2,256,256]{2,1,0:T(8,128)S(1)} %get-tuple-element.33.refs_3_, ...), custom_call_target="tpu_custom_call" | custom-call | flops 5000000000 | bytes 6000000 | tf_op jit(solution)/shard_map/pallas_call | solution.py:163
  223.5 5.5 %shard_map.106 = (f32[2,256,256]{2,1,0:T(8,128)S(1)}, f32[12,256,128]{2,1,0:T(8,128)S(1)}, f32[8,128]{1,0:T(8,128)S(1)}) custom-call(s32[3]{0:T(128)S(1)} %pad_add_fusion.2.refs_0_, f32[1]{0:T(128)} %bitcast.38.refs_1_, f32[2,256,256]{2,1,0:T(8,128)S(1)} %get-tuple-element.82.refs_2_, f32[2,256,256]{2,1,0:T(8,128)S(1)} %get-tuple-element.81.refs_3_, ...), custom_call_target="tpu_custom_call" | custom-call | flops 5000000000 | bytes 6000000 | tf_op jit(solution)/shard_map/pallas_call | solution.py:163
  230.0 1.8 collective-permute-start.16
  231.7 3.5 %collective-permute-start.18 = (f32[2,256,256]{2,1,0:T(8,128)S(1)}, f32[2,256,256]{2,1,0:T(8,128)S(1)}, u32[]{:S(2)}, u32[]{:S(2)}) collective-permute-start(f32[2,256,256]{2,1,0:T(8,128)S(1)} %get-tuple-element.30), channel_id=1, source_target_pairs={{0,8},{8,16},{16,24},{24,32},{32,40},{40,48},{48,56},{56,64},{64,7... | collective-permute-start | bytes 1572872 | tf_op jit(solution)/shard_map/ppermute | solution.py:185
  235.3 3.9 %collective-permute-start.17 = (f32[2,256,256]{2,1,0:T(8,128)S(1)}, f32[2,256,256]{2,1,0:T(8,128)}, u32[]{:S(2)}, u32[]{:S(2)}) collective-permute-start(f32[2,256,256]{2,1,0:T(8,128)S(1)} %get-tuple-element.29), channel_id=1, source_target_pairs={{0,8},{8,16},{16,24},{24,32},{32,40},{40,48},{48,56},{56,64},{64,7... | collective-permute-start | bytes 1572872 | tf_op jit(solution)/shard_map/ppermute | solution.py:185
  242.8 2.1 bitcast_add_fusion
  244.9 6.3 %all-to-all-start.4 = ((f32[4,16,24,128]{3,2,1,0:T(8,128)}), f32[4,16,24,128]{3,2,1,0:T(8,128)S(1)}, u32[]{:S(2)}, u32[]{:S(2)}) async-start(f32[4,16,24,128]{3,2,1,0:T(8,128)} %bitcast.125), calls=%async_computation.4 | async-start | bytes 1572864 | tf_op jit(solution)/shard_map/all_to_all | solution.py:244
  251.3 6.5 %collective-permute-done.17 = f32[2,256,256]{2,1,0:T(8,128)} collective-permute-done((f32[2,256,256]{2,1,0:T(8,128)S(1)}, f32[2,256,256]{2,1,0:T(8,128)}, u32[]{:S(2)}, u32[]{:S(2)}) %collective-permute-start.17) | collective-permute-done | bytes 524320 | tf_op jit(solution)/shard_map/ppermute | solution.py:185
  257.8 1.3 select_add_fusion.1
  259.1 4.1 %collective-permute-start.19 = (f32[2,256,256]{2,1,0:T(8,128)S(1)}, f32[2,256,256]{2,1,0:T(8,128)}, u32[]{:S(2)}, u32[]{:S(2)}) collective-permute-start(f32[2,256,256]{2,1,0:T(8,128)S(1)} %select_add_fusion.1), channel_id=1, source_target_pairs={{0,1},{1,2},{2,3},{3,4},{4,5},{5,6},{6,7},{8,9},{9,10},{10,11},{11... | collective-permute-start | bytes 1572872 | tf_op jit(solution)/shard_map/ppermute | solution.py:185
  266.5 9.7 %all-to-all-start.5 = ((f32[16,24,128]{2,1,0:T(8,128)}), f32[16,24,128]{2,1,0:T(8,128)S(1)}, u32[]{:S(2)}, u32[]{:S(2)}) async-start(f32[16,24,128]{2,1,0:T(8,128)} %reduce_sum.152), calls=%async_computation.5 | async-start | bytes 393216 | tf_op jit(solution)/shard_map/all_to_all | solution.py:245
  276.2 1.7 add_add_fusion
  279.9 4.1 %all-to-all-done.5 = f32[16,24,128]{2,1,0:T(8,128)S(1)} async-done(((f32[16,24,128]{2,1,0:T(8,128)}), f32[16,24,128]{2,1,0:T(8,128)S(1)}, u32[]{:S(2)}, u32[]{:S(2)}) %all-to-all-start.5) | async-done | bytes 196640 | tf_op jit(solution)/shard_map/all_to_all | solution.py:245
  286.0 10.8 %all_to_all.40 = f32[16,32,128]{2,1,0:T(8,128)S(1)} all-to-all(f32[16,32,128]{2,1,0:T(8,128)S(1)} %broadcast_in_dim.711), channel_id=1, replica_groups=mesh['row'=16,'col'=8] {'row'}, dimensions={0} | all-to-all | bytes 524288 | tf_op jit(solution)/shard_map/all_to_all | solution.py:250
  296.9 15.1 %all_to_all.41 = f32[4,392,128]{2,1,0:T(8,128)S(1)} all-to-all(f32[4,392,128]{2,1,0:T(8,128)S(1)} %broadcast_in_dim.712), channel_id=1, replica_groups={{0,2,4,6},{1,3,5,7},{8,10,12,14},{9,11,13,15},{16,18,20,22},{17,19,21,2..., dimensions={0} | all-to-all | bytes 1605632 | tf_op jit(solution)/shard_map/all_to_all | solution.py:252
  313.0 2.6 collective-permute-start.21
  317.4 2.4 mul.68
  322.4 2.6 multiply_subtract_fusion
  325.0 2.0 fusion
  328.2 2.4 mul.73
  330.6 3.3 subtract_subtract_fusion
  (164 shorter events, 28.0 us)
Async XLA Ops:
  0.6 31.7 %copy-start.9 = (f32[2,256,512]{2,1,0:T(8,128)S(1)}, f32[2,256,512]{2,1,0:T(8,128)}, u32[]{:S(2)}) copy-start(f32[2,256,512]{2,1,0:T(8,128)} %param.8) | copy-start | bytes 3145732
  0.6 22.9 %collective-permute-start.1 = (s32[2,2,2]{2,1,0:T(2,128)}, s32[2,2,2]{2,1,0:T(2,128)S(1)}, u32[]{:S(2)}, u32[]{:S(2)}) collective-permute-start(s32[2,2,2]{2,1,0:T(2,128)} %bitcast.131), channel_id=1, source_target_pairs={{0,8},{8,16},{16,24},{24,32},{32,40},{40,48},{48,56},{56,64},{64,7... | collective-permute-start | bytes 104 | tf_op jit(solution)/shard_map/ppermute | solution.py:185
  4.8 31.4 %collective-permute-start.7 = (s32[2,2,2]{2,1,0:T(2,128)}, s32[2,2,2]{2,1,0:T(2,128)S(1)}, u32[]{:S(2)}, u32[]{:S(2)}) collective-permute-start(s32[2,2,2]{2,1,0:T(2,128)} %bitcast.132), channel_id=1, source_target_pairs={{8,0},{16,8},{24,16},{32,24},{40,32},{48,40},{56,48},{64,56},{72,6... | collective-permute-start | bytes 104 | tf_op jit(solution)/shard_map/ppermute | solution.py:185
  7.2 25.1 %collective-permute-start = (f32[2,256,256]{2,1,0:T(8,128)S(1)}, f32[2,256,256]{2,1,0:T(8,128)S(1)}, u32[]{:S(2)}, u32[]{:S(2)}) collective-permute-start(f32[2,256,256]{2,1,0:T(8,128)S(1)} %slice.135), channel_id=1, source_target_pairs={{1,0},{2,1},{3,2},{4,3},{5,4},{6,5},{7,6},{9,8},{10,9},{11,10},{12... | collective-permute-start | bytes 1572872 | tf_op jit(solution)/shard_map/ppermute | solution.py:185
  32.3 2.6 copy-start.18
  32.3 3.9 %copy-start.32 = (bf16[2,1,1,2,256,256]{5,4,3,2,1,0:T(8,128)(2,1)S(1)}, bf16[2,1,1,2,256,256]{5,4,3,2,1,0:T(8,128)(2,1)}, u32[]{:S(2)}) copy-start(bf16[2,1,1,2,256,256]{5,4,3,2,1,0:T(8,128)(2,1)} %param.12) | copy-start | bytes 1572868
  32.3 30.7 %copy-start.8 = (bf16[2,256,256]{2,1,0:T(8,128)(2,1)S(1)}, bf16[2,256,256]{2,1,0:T(8,128)(2,1)}, u32[]{:S(2)}) copy-start(bf16[2,256,256]{2,1,0:T(8,128)(2,1)} %constant.698.clone.refs_6_.refs_9_) | copy-start | bytes 786436
  33.6 17.0 %collective-permute-start.3 = (f32[2,256,256]{2,1,0:T(8,128)}, f32[2,256,256]{2,1,0:T(8,128)S(1)}, u32[]{:S(2)}, u32[]{:S(2)}) collective-permute-start(f32[2,256,256]{2,1,0:T(8,128)} %get-tuple-element.45), channel_id=1, source_target_pairs={{8,0},{16,8},{24,16},{32,24},{40,32},{48,40},{56,48},{64,56},{72,6... | collective-permute-start | bytes 1572872 | tf_op jit(solution)/shard_map/ppermute | solution.py:185
  34.9 26.3 %collective-permute-start.2 = (f32[2,256,256]{2,1,0:T(8,128)}, f32[2,256,256]{2,1,0:T(8,128)}, u32[]{:S(2)}, u32[]{:S(2)}) collective-permute-start(f32[2,256,256]{2,1,0:T(8,128)} %get-tuple-element.46), channel_id=1, source_target_pairs={{8,0},{16,8},{24,16},{32,24},{40,32},{48,40},{56,48},{64,56},{72,6... | collective-permute-start | bytes 1572872 | tf_op jit(solution)/shard_map/ppermute | solution.py:185
  36.2 26.8 %copy-start.5 = (bf16[4,768,256]{2,1,0:T(8,128)(2,1)S(1)}, bf16[4,768,256]{2,1,0:T(8,128)(2,1)}, u32[]{:S(2)}) copy-start(bf16[4,768,256]{2,1,0:T(8,128)(2,1)} %constant.697.clone.refs_5_.refs_8_) | copy-start | bytes 4718596
  61.1 2.0 copy-start
  61.2 2.5 copy-start.3
  63.7 5.5 %copy-start.6 = (bf16[4,768,256]{2,1,0:T(8,128)(2,1)S(1)}, bf16[4,768,256]{2,1,0:T(8,128)(2,1)}, u32[]{:S(2)}) copy-start(bf16[4,768,256]{2,1,0:T(8,128)(2,1)} %constant.697.clone.refs_5_.refs_8_) | copy-start | bytes 4718596
  74.9 17.8 %collective-permute-start.9 = (f32[2,256,256]{2,1,0:T(8,128)S(1)}, f32[2,256,256]{2,1,0:T(8,128)}, u32[]{:S(2)}, u32[]{:S(2)}) collective-permute-start(f32[2,256,256]{2,1,0:T(8,128)S(1)} %get-tuple-element.22), channel_id=1, source_target_pairs={{8,0},{16,8},{24,16},{32,24},{40,32},{48,40},{56,48},{64,56},{72,6... | collective-permute-start | bytes 1572872 | tf_op jit(solution)/shard_map/ppermute | solution.py:185
  76.2 25.8 %collective-permute-start.8 = (f32[2,256,256]{2,1,0:T(8,128)S(1)}, f32[2,256,256]{2,1,0:T(8,128)}, u32[]{:S(2)}, u32[]{:S(2)}) collective-permute-start(f32[2,256,256]{2,1,0:T(8,128)S(1)} %get-tuple-element.21), channel_id=1, source_target_pairs={{8,0},{16,8},{24,16},{32,24},{40,32},{48,40},{56,48},{64,56},{72,6... | collective-permute-start | bytes 1572872 | tf_op jit(solution)/shard_map/ppermute | solution.py:185
  82.1 22.4 %collective-permute-start.6 = (f32[2,256,256]{2,1,0:T(8,128)S(1)}, f32[2,256,256]{2,1,0:T(8,128)S(1)}, u32[]{:S(2)}, u32[]{:S(2)}) collective-permute-start(f32[2,256,256]{2,1,0:T(8,128)S(1)} %get-tuple-element.22), channel_id=1, source_target_pairs={{0,8},{8,16},{16,24},{24,32},{32,40},{40,48},{48,56},{56,64},{64,7... | collective-permute-start | bytes 1572872 | tf_op jit(solution)/shard_map/ppermute | solution.py:185
  87.1 22.1 %collective-permute-start.5 = (f32[2,256,256]{2,1,0:T(8,128)S(1)}, f32[2,256,256]{2,1,0:T(8,128)S(1)}, u32[]{:S(2)}, u32[]{:S(2)}) collective-permute-start(f32[2,256,256]{2,1,0:T(8,128)S(1)} %get-tuple-element.21), channel_id=1, source_target_pairs={{0,8},{8,16},{16,24},{24,32},{32,40},{40,48},{48,56},{56,64},{64,7... | collective-permute-start | bytes 1572872 | tf_op jit(solution)/shard_map/ppermute | solution.py:185
  91.5 25.1 %collective-permute-start.4 = (f32[64,24,128]{2,1,0:T(8,128)}, f32[64,24,128]{2,1,0:T(8,128)}, u32[]{:S(2)}, u32[]{:S(2)}) collective-permute-start(f32[64,24,128]{2,1,0:T(8,128)} %dynamic-slice_bitcast_fusion.1), channel_id=1, source_target_pairs={{0,1},{1,0},{2,3},{3,2},{4,5},{5,4},{6,7},{7,6},{8,9},{9,8},{10,11... | collective-permute-start | bytes 2359304 | tf_op jit(solution)/shard_map/ppermute | solution.py:241
  104.5 6.1 %copy-start.24 = (f32[1,2,256,256]{3,2,1,0:T(8,128)}, f32[1,2,256,256]{3,2,1,0:T(8,128)S(1)}, u32[]{:S(2)}) copy-start(f32[1,2,256,256]{3,2,1,0:T(8,128)S(1)} %get-tuple-element.40) | copy-start | bytes 1572868
  104.5 6.1 %copy-start.27 = (f32[2,256,256]{2,1,0:T(8,128)}, f32[2,256,256]{2,1,0:T(8,128)S(1)}, u32[]{:S(2)}) copy-start(f32[2,256,256]{2,1,0:T(8,128)S(1)} %collective-permute-done.6) | copy-start | bytes 1572868
  109.2 1.4 copy-start.29
  110.6 1.2 copy-start.26
  111.8 21.0 %collective-permute-start.10 = (f32[2,2,256,256]{3,2,1,0:T(8,128)}, f32[2,2,256,256]{3,2,1,0:T(8,128)}, u32[]{:S(2)}, u32[]{:S(2)}) collective-permute-start(f32[2,2,256,256]{3,2,1,0:T(8,128)} %pad_maximum_fusion.1), channel_id=1, source_target_pairs={{0,1},{1,2},{2,3},{3,4},{4,5},{5,6},{6,7},{8,9},{9,10},{10,11},{11... | collective-permute-start | bytes 3145736 | tf_op jit(solution)/shard_map/ppermute | solution.py:185
  118.7 14.1 %copy-start.31 = (f32[1,2,256,256]{3,2,1,0:T(8,128)S(1)}, f32[1,2,256,256]{3,2,1,0:T(8,128)}, u32[]{:S(2)}) copy-start(f32[1,2,256,256]{3,2,1,0:T(8,128)} %get-tuple-element.41) | copy-start | bytes 1572868
  118.7 22.7 %all-to-all-start = ((f32[4,16,24,128]{3,2,1,0:T(8,128)}), f32[4,16,24,128]{3,2,1,0:T(8,128)}, u32[]{:S(2)}, u32[]{:S(2)}) async-start(f32[4,16,24,128]{3,2,1,0:T(8,128)} %bitcast.124), calls=%async_computation | async-start | bytes 1572864 | tf_op jit(solution)/shard_map/all_to_all | solution.py:244
  135.3 29.7 %copy-start.12 = (f32[2,2,256,256]{3,2,1,0:T(8,128)}, f32[2,2,256,256]{3,2,1,0:T(8,128)S(1)}, u32[]{:S(2)}) copy-start(f32[2,2,256,256]{3,2,1,0:T(8,128)S(1)} %get-tuple-element.49) | copy-start | bytes 3145732
  135.3 28.0 %copy-start.25 = (f32[1,2,256,256]{3,2,1,0:T(8,128)S(1)}, f32[1,2,256,256]{3,2,1,0:T(8,128)}, u32[]{:S(2)}) copy-start(f32[1,2,256,256]{3,2,1,0:T(8,128)} %copy-done.24) | copy-start | bytes 1572868
  135.3 28.0 %collective-permute-start.13 = (f32[2,2,256,256]{3,2,1,0:T(8,128)}, f32[2,2,256,256]{3,2,1,0:T(8,128)}, u32[]{:S(2)}, u32[]{:S(2)}) collective-permute-start(f32[2,2,256,256]{3,2,1,0:T(8,128)} %get-tuple-element.50), channel_id=1, source_target_pairs={{1,0},{2,1},{3,2},{4,3},{5,4},{6,5},{7,6},{9,8},{10,9},{11,10},{12... | collective-permute-start | bytes 3145736 | tf_op jit(solution)/shard_map/ppermute | solution.py:185
  143.2 18.7 %all-to-all-start.1 = ((f32[16,24,128]{2,1,0:T(8,128)}), f32[16,24,128]{2,1,0:T(8,128)S(1)}, u32[]{:S(2)}, u32[]{:S(2)}) async-start(f32[16,24,128]{2,1,0:T(8,128)} %reduce_sum.144), calls=%async_computation.1 | async-start | bytes 393216 | tf_op jit(solution)/shard_map/all_to_all | solution.py:245
  163.3 4.9 %copy-start.21 = (f32[2,256,256]{2,1,0:T(8,128)}, f32[2,256,256]{2,1,0:T(8,128)S(1)}, u32[]{:S(2)}) copy-start(f32[2,256,256]{2,1,0:T(8,128)S(1)} %slice_bitcast_fusion.3) | copy-start | bytes 1572868
  163.3 1.8 copy-start.28
  163.3 1.9 copy-start.30
  165.0 3.1 copy-start.14
  168.1 0.8 copy-start.15
  171.3 12.9 %all-to-all-start.2 = ((f32[16,32,128]{2,1,0:T(8,128)}), f32[16,32,128]{2,1,0:T(8,128)S(1)}, u32[]{:S(2)}, u32[]{:S(2)}) async-start(f32[16,32,128]{2,1,0:T(8,128)} %broadcast_in_dim.683), calls=%async_computation.2 | async-start | bytes 524288 | tf_op jit(solution)/shard_map/all_to_all | solution.py:250
  174.8 18.3 %collective-permute-start.15 = (f32[2,256,256]{2,1,0:T(8,128)}, f32[2,256,256]{2,1,0:T(8,128)}, u32[]{:S(2)}, u32[]{:S(2)}) collective-permute-start(f32[2,256,256]{2,1,0:T(8,128)} %get-tuple-element.24), channel_id=1, source_target_pairs={{8,0},{16,8},{24,16},{32,24},{40,32},{48,40},{56,48},{64,56},{72,6... | collective-permute-start | bytes 1572872 | tf_op jit(solution)/shard_map/ppermute | solution.py:185
  184.3 8.9 %copy-start.10 = (f32[2,256,512]{2,1,0:T(8,128)S(1)}, f32[2,256,512]{2,1,0:T(8,128)}, u32[]{:S(2)}) copy-start(f32[2,256,512]{2,1,0:T(8,128)} %param.8) | copy-start | bytes 3145732
  184.3 8.9 %copy-start.19 = (f32[2,256,256]{2,1,0:T(8,128)S(1)}, f32[2,256,256]{2,1,0:T(8,128)}, u32[]{:S(2)}) copy-start(f32[2,256,256]{2,1,0:T(8,128)} %copy-done.18) | copy-start | bytes 1572868
  185.3 19.6 %all-to-all-start.3 = ((f32[4,392,128]{2,1,0:T(8,128)}), f32[4,392,128]{2,1,0:T(8,128)}, u32[]{:S(2)}, u32[]{:S(2)}) async-start(f32[4,392,128]{2,1,0:T(8,128)} %broadcast_in_dim.684), calls=%async_computation.3 | async-start | bytes 1605632 | tf_op jit(solution)/shard_map/all_to_all | solution.py:252
  195.2 15.5 %copy-start.16 = (f32[2,256,256]{2,1,0:T(8,128)S(1)}, f32[2,256,256]{2,1,0:T(8,128)}, u32[]{:S(2)}) copy-start(f32[2,256,256]{2,1,0:T(8,128)} %copy-done.15) | copy-start | bytes 1572868
  195.2 15.5 %collective-permute-start.12 = (f32[2,256,256]{2,1,0:T(8,128)}, f32[2,256,256]{2,1,0:T(8,128)}, u32[]{:S(2)}, u32[]{:S(2)}) collective-permute-start(f32[2,256,256]{2,1,0:T(8,128)} %get-tuple-element.23), channel_id=1, source_target_pairs={{8,0},{16,8},{24,16},{32,24},{40,32},{48,40},{56,48},{64,56},{72,6... | collective-permute-start | bytes 1572872 | tf_op jit(solution)/shard_map/ppermute | solution.py:185
  204.9 5.8 %copy-start.13 = (f32[2,2,256,256]{3,2,1,0:T(8,128)S(1)}, f32[2,2,256,256]{3,2,1,0:T(8,128)}, u32[]{:S(2)}) copy-start(f32[2,2,256,256]{3,2,1,0:T(8,128)} %copy-done.12) | copy-start | bytes 3145732
  206.2 8.9 %collective-permute-start.14 = (f32[1536,128]{1,0:T(8,128)S(1)}, f32[1536,128]{1,0:T(8,128)S(1)}, u32[]{:S(2)}, u32[]{:S(2)}) collective-permute-start(f32[1536,128]{1,0:T(8,128)S(1)} %bitcast.126), channel_id=1, source_target_pairs={{0,1},{1,0},{2,3},{3,2},{4,5},{5,4},{6,7},{7,6},{8,9},{9,8},{10,11... | collective-permute-start | bytes 2359304 | tf_op jit(solution)/shard_map/ppermute | solution.py:258
  208.9 3.7 %collective-permute-start.11 = (f32[8,128]{1,0:T(8,128)S(1)}, f32[8,128]{1,0:T(8,128)S(1)}, u32[]{:S(2)}, u32[]{:S(2)}) collective-permute-start(f32[8,128]{1,0:T(8,128)S(1)} %slice_reduce_fusion.3), channel_id=1, source_target_pairs={{0,1},{1,0},{2,3},{3,2},{4,5},{5,4},{6,7},{7,6},{8,9},{9,8},{10,11... | collective-permute-start | bytes 12296 | tf_op jit(solution)/shard_map/ppermute | solution.py:259
  215.1 2.0 copy-start.1
  215.1 2.4 copy-start.4
  215.1 2.9 copy-start.7
  230.0 12.8 %collective-permute-start.16 = (f32[64,24,128]{2,1,0:T(8,128)}, f32[64,24,128]{2,1,0:T(8,128)}, u32[]{:S(2)}, u32[]{:S(2)}) collective-permute-start(f32[64,24,128]{2,1,0:T(8,128)} %dynamic-slice_bitcast_fusion), channel_id=1, source_target_pairs={{0,1},{1,0},{2,3},{3,2},{4,5},{5,4},{6,7},{7,6},{8,9},{9,8},{10,11... | collective-permute-start | bytes 2359304 | tf_op jit(solution)/shard_map/ppermute | solution.py:241
  231.7 19.5 %collective-permute-start.18 = (f32[2,256,256]{2,1,0:T(8,128)S(1)}, f32[2,256,256]{2,1,0:T(8,128)S(1)}, u32[]{:S(2)}, u32[]{:S(2)}) collective-permute-start(f32[2,256,256]{2,1,0:T(8,128)S(1)} %get-tuple-element.30), channel_id=1, source_target_pairs={{0,8},{8,16},{16,24},{24,32},{32,40},{40,48},{48,56},{56,64},{64,7... | collective-permute-start | bytes 1572872 | tf_op jit(solution)/shard_map/ppermute | solution.py:185
  235.3 22.5 %collective-permute-start.17 = (f32[2,256,256]{2,1,0:T(8,128)S(1)}, f32[2,256,256]{2,1,0:T(8,128)}, u32[]{:S(2)}, u32[]{:S(2)}) collective-permute-start(f32[2,256,256]{2,1,0:T(8,128)S(1)} %get-tuple-element.29), channel_id=1, source_target_pairs={{0,8},{8,16},{16,24},{24,32},{32,40},{40,48},{48,56},{56,64},{64,7... | collective-permute-start | bytes 1572872 | tf_op jit(solution)/shard_map/ppermute | solution.py:185
  244.9 20.8 %all-to-all-start.4 = ((f32[4,16,24,128]{3,2,1,0:T(8,128)}), f32[4,16,24,128]{3,2,1,0:T(8,128)S(1)}, u32[]{:S(2)}, u32[]{:S(2)}) async-start(f32[4,16,24,128]{3,2,1,0:T(8,128)} %bitcast.125), calls=%async_computation.4 | async-start | bytes 1572864 | tf_op jit(solution)/shard_map/all_to_all | solution.py:244
  259.1 17.1 %collective-permute-start.19 = (f32[2,256,256]{2,1,0:T(8,128)S(1)}, f32[2,256,256]{2,1,0:T(8,128)}, u32[]{:S(2)}, u32[]{:S(2)}) collective-permute-start(f32[2,256,256]{2,1,0:T(8,128)S(1)} %select_add_fusion.1), channel_id=1, source_target_pairs={{0,1},{1,2},{2,3},{3,4},{4,5},{5,6},{6,7},{8,9},{9,10},{10,11},{11... | collective-permute-start | bytes 1572872 | tf_op jit(solution)/shard_map/ppermute | solution.py:185
  266.5 17.4 %all-to-all-start.5 = ((f32[16,24,128]{2,1,0:T(8,128)}), f32[16,24,128]{2,1,0:T(8,128)S(1)}, u32[]{:S(2)}, u32[]{:S(2)}) async-start(f32[16,24,128]{2,1,0:T(8,128)} %reduce_sum.152), calls=%async_computation.5 | async-start | bytes 393216 | tf_op jit(solution)/shard_map/all_to_all | solution.py:245
  278.0 0.8 copy-start.22
  278.0 1.0 copy-start.23
  296.9 19.3 %copy-start.20 = (f32[2,1536,128]{2,1,0:T(8,128)S(1)}, f32[2,1536,128]{2,1,0:T(8,128)}, u32[]{:S(2)}) copy-start(f32[2,1536,128]{2,1,0:T(8,128)} %get-tuple-element.31) | copy-start | bytes 4718596
  313.0 12.0 %collective-permute-start.21 = (f32[1536,128]{1,0:T(8,128)}, f32[1536,128]{1,0:T(8,128)}, u32[]{:S(2)}, u32[]{:S(2)}) collective-permute-start(f32[1536,128]{1,0:T(8,128)} %bitcast.66), channel_id=1, source_target_pairs={{0,1},{1,0},{2,3},{3,2},{4,5},{5,4},{6,7},{7,6},{8,9},{9,8},{10,11... | collective-permute-start | bytes 2359304 | tf_op jit(solution)/shard_map/ppermute | solution.py:258
  315.6 4.3 %collective-permute-start.20 = (f32[8,128]{1,0:T(8,128)S(1)}, f32[8,128]{1,0:T(8,128)S(1)}, u32[]{:S(2)}, u32[]{:S(2)}) collective-permute-start(f32[8,128]{1,0:T(8,128)S(1)} %slice_reduce_fusion.2), channel_id=1, source_target_pairs={{0,1},{1,0},{2,3},{3,2},{4,5},{5,4},{6,7},{7,6},{8,9},{9,8},{10,11... | collective-permute-start | bytes 12296 | tf_op jit(solution)/shard_map/ppermute | solution.py:259
  317.4 5.0 %copy-start.11 = (f32[2,256,512]{2,1,0:T(8,128)S(1)}, f32[2,256,512]{2,1,0:T(8,128)}, u32[]{:S(2)}) copy-start(f32[2,256,512]{2,1,0:T(8,128)} %param.8) | copy-start | bytes 3145732
  317.4 5.0 %copy-start.17 = (f32[2,256,256]{2,1,0:T(8,128)S(1)}, f32[2,256,256]{2,1,0:T(8,128)}, u32[]{:S(2)}) copy-start(f32[2,256,256]{2,1,0:T(8,128)} %copy-done.15) | copy-start | bytes 1572868
  328.2 2.4 copy-start.2

commit v2 on v0

v2 whole, which is shorter than its diff:
```python
import math

import jax
import jax.numpy as jnp
import numpy as np
from jax import lax
from jax.experimental import pallas as pl
from jax.experimental.pallas import tpu as pltpu
from jax.sharding import Mesh
from jax.sharding import PartitionSpec as P

WIN = 256
HALF = 128
MODES = 3
CAP = 2
AREA = float(WIN * WIN)
CHUNK = 24
INFO = 8
SENT = 32
MEGA = 1024 * 1024
F32 = jnp.float32
SMEM = pl.BlockSpec(memory_space=pltpu.SMEM)
VMEM = pl.BlockSpec(memory_space=pltpu.VMEM)
ANY = pl.BlockSpec(memory_space=pl.ANY)


def f32(*shape):
    return jax.ShapeDtypeStruct(shape, F32)


def split_bf16(value):
    high = value.astype(jnp.bfloat16)
    low = (value - high.astype(F32)).astype(jnp.bfloat16)
    return high, low


def transform_tables():
    freq = np.arange(HALF)[:, None]
    pixel = np.arange(HALF)[None, :]
    tables = []
    for odd in (0, 1):
        angle = -2.0 * math.pi * (((2 * freq + odd) * pixel) % WIN) / WIN
        cos, sin = np.cos(angle) / math.sqrt(WIN), np.sin(angle) / math.sqrt(WIN)
        tables.append(np.block([[cos, -sin], [sin, cos]]).astype(np.float32))
    tables = np.stack([tables[0], tables[1], tables[0].T, tables[1].T])
    high = tables.astype(jnp.bfloat16)
    low = (tables - high.astype(np.float32)).astype(jnp.bfloat16)
    order = np.concatenate([np.arange(0, WIN, 2), np.arange(1, WIN, 2)])
    shuffle = np.zeros((WIN, WIN), np.float32)
    shuffle[np.arange(WIN), order] = 1.0
    return np.stack([high, low], axis=1), np.stack([shuffle, shuffle.T]).astype(jnp.bfloat16)


def product(left, right):
    return jnp.dot(left, right, preferred_element_type=F32)


def left_apply(table_ref, index, data):
    high, low = split_bf16(data)
    table = jnp.concatenate([table_ref[index, 0], table_ref[index, 0], table_ref[index, 1]], axis=1)
    return product(table, jnp.concatenate([high, low, high], axis=0))


def right_apply(data, table_ref, index):
    high, low = split_bf16(data)
    table = jnp.concatenate([table_ref[index, 0], table_ref[index, 0], table_ref[index, 1]], axis=0)
    return product(jnp.concatenate([high, low, high], axis=1), table)


def row_place(shape=(WIN, WIN)):
    return lax.broadcasted_iota(jnp.int32, shape, 0)


def col_place(shape=(WIN, WIN)):
    return lax.broadcasted_iota(jnp.int32, shape, 1)


def corner_of(corner_ref, iteration, slot):
    row, col = corner_ref[iteration, slot, 0], corner_ref[iteration, slot, 1]
    return lax.rem(row, WIN), lax.rem(col, WIN), lax.rem(lax.div(col, WIN), 2)


def cut(corner, upper, lower):
    row, col, block = corner
    first = row_place() >= row
    blocks = [jnp.where(first, above, below) for above, below in zip(upper, lower)]
    left = jnp.where(block == 0, blocks[0], blocks[1])
    right = jnp.where(block == 0, blocks[1], blocks[2])
    value = jnp.where(col_place() >= col, left, right)
    value = pltpu.roll(value, lax.rem(WIN - row, WIN), 0)
    return pltpu.roll(value, lax.rem(WIN - col, WIN), 1)


def rate_of(mine, other):
    total = jnp.sum(mine[:, CHUNK:], axis=0) + jnp.sum(other[:, CHUNK:], axis=0)
    return total[0:1] / (total[1:2] + 1e-06)


def gathered_plane(half, index):
    pieces, row, end = [], index * WIN, (index + 1) * WIN
    while row < end:
        chunk, offset = divmod(row, CHUNK)
        size = min(CHUNK - offset, end - row)
        pieces.append(half[chunk, offset : offset + size])
        row += size
    return jnp.concatenate(pieces, axis=0)


def probe_step(mine, other, core):
    planes = []
    for plane in range(2 * MODES):
        sides = []
        for side in range(2):
            half, index = divmod(2 * plane + side, 2 * MODES)
            own, swapped = gathered_plane(mine, index), gathered_plane(other, index)
            sides.append(jnp.where(core == half, own, swapped))
        planes.append(jnp.concatenate(sides, axis=1))
    return planes


def window_kernel(iteration, corner_ref, count_ref, *refs):
    refs = list(refs)
    core = lax.axis_index("core")
    n_big = 9 if iteration == 0 else 8
    sources, refs = refs[:n_big], refs[n_big:]
    out_grad, out_keep, out_send = refs[:3]
    refs = refs[3:]
    if iteration:
        out_mid, out_rate = refs[:2]
        refs = refs[2:]
    out_loss, obj, field, factor, total_probe, grads, sems, out_sems, probe_sems, mid_sem = refs[:10]
    held = refs[10:]
    fetch = [pltpu.make_async_copy(src, dst, sems.at[k]) for k, (src, dst) in enumerate(zip(sources, held))]
    for copy in fetch:
        copy.start()
    if iteration == 0:
        tile, below0, below1, rim, diag, probe_ref, tables, amp_ref, shuffle = held
    else:
        mine, other, patch, patch_grad, probe_ref, tables, amp_ref, shuffle = held
    for copy in fetch[:-3]:
        copy.wait()

    if iteration:
        rate = rate_of(mine, other)
        out_rate[...] = jnp.broadcast_to(rate, (8, HALF))
        wide = jnp.concatenate([rate, rate], axis=1)
        for plane, step in enumerate(probe_step(mine, other, core)):
            probe_ref[plane] = probe_ref[plane] - wide * step
        mid_copy = pltpu.make_async_copy(probe_ref, out_mid, mid_sem.at[0])
        mid_copy.start()

    def deliver(index):
        half, place = divmod(index, 2 * MODES)
        keep = pltpu.make_async_copy(total_probe.at[index], out_keep.at[place], probe_sems.at[index])
        send = pltpu.make_async_copy(total_probe.at[index], out_send.at[place], probe_sems.at[index])
        return half, keep, send

    losses = jnp.zeros((8, HALF), F32)
    for slot in range(CAP):
        corner = corner_of(corner_ref, iteration, slot)
        alive = (slot < count_ref[iteration]).astype(F32)
        for part in range(2):
            if iteration == 0:
                obj[part] = cut(
                    corner,
                    (tile[part, :, :WIN], tile[part, :, WIN:], rim[part]),
                    (below0[part], below1[part], diag[part]),
                )
            else:
                obj[part] = patch[slot, part] - wide * patch_grad[slot, part]

        if slot == 0:
            fetch[-3].wait()
        for mode in range(MODES):
            probe_re, probe_im = probe_ref[2 * mode], probe_ref[2 * mode + 1]
            exit_re = probe_re * obj[0] - probe_im * obj[1]
            exit_im = probe_re * obj[1] + probe_im * obj[0]
            half = []
            for odd in range(2):
                sign = -1.0 if odd else 1.0
                folded = jnp.concatenate(
                    [exit_re[:HALF] + sign * exit_re[HALF:], exit_im[:HALF] + sign * exit_im[HALF:]], axis=0
                )
                half.append(left_apply(tables, odd, folded))
            mid_re = jnp.concatenate([half[0][:HALF], half[1][:HALF]], axis=0)
            mid_im = jnp.concatenate([half[0][HALF:], half[1][HALF:]], axis=0)
            for odd in range(2):
                sign = -1.0 if odd else 1.0
                folded = jnp.concatenate(
                    [mid_re[:, :HALF] + sign * mid_re[:, HALF:], mid_im[:, :HALF] + sign * mid_im[:, HALF:]], axis=1
                )
                field[mode, odd] = right_apply(folded, tables, 2 + odd)

        if slot == 0:
            fetch[-2].wait()
            fetch[-1].wait()
        amp = product(shuffle[0], amp_ref[iteration, slot]).astype(jnp.bfloat16)
        amp = product(amp, shuffle[1])
        loss = jnp.zeros((WIN, HALF), F32)
        for odd in range(2):
            total = jnp.ones((WIN, HALF), F32)
            for mode in range(MODES):
                real, imag = field[mode, odd, :, :HALF], field[mode, odd, :, HALF:]
                total = total + (real * real + imag * imag)
            inverse = lax.rsqrt(total)
            measured = amp[:, odd * HALF : (odd + 1) * HALF]
            gap = total * inverse - measured
            loss = loss + gap * gap
            factor[odd] = (1.0 - measured * inverse) * (2.0 / AREA * alive)
        losses = losses + jnp.sum(loss.reshape(WIN // 8, 8, HALF), axis=0) * (alive / AREA)

        grad_re = jnp.zeros((WIN, WIN), F32)
        grad_im = jnp.zeros((WIN, WIN), F32)
        for mode in range(MODES):
            half = []
            for odd in range(2):
                scale = jnp.concatenate([factor[odd], factor[odd]], axis=1)
                half.append(right_apply(field[mode, odd] * scale, tables, odd))
            mid_re = jnp.concatenate(
                [half[0][:, :HALF] + half[1][:, :HALF], half[0][:, :HALF] - half[1][:, :HALF]], axis=1
            )
            mid_im = jnp.concatenate(
                [half[0][:, HALF:] + half[1][:, HALF:], half[0][:, HALF:] - half[1][:, HALF:]], axis=1
            )
            back = []
            for odd in range(2):
                rows = slice(odd * HALF, (odd + 1) * HALF)
                back.append(left_apply(tables, 2 + odd, jnp.concatenate([mid_re[rows], mid_im[rows]], axis=0)))
            back_re = jnp.concatenate([back[0][:HALF] + back[1][:HALF], back[0][:HALF] - back[1][:HALF]], axis=0)
            back_im = jnp.concatenate([back[0][HALF:] + back[1][HALF:], back[0][HALF:] - back[1][HALF:]], axis=0)
            probe_re, probe_im = probe_ref[2 * mode], probe_ref[2 * mode + 1]
            grad_re = grad_re + (probe_re * back_re + probe_im * back_im)
            grad_im = grad_im + (probe_re * back_im - probe_im * back_re)
            terms = (obj[0] * back_re + obj[1] * back_im, obj[0] * back_im - obj[1] * back_re)
            for part in range(2):
                for side in range(2):
                    index = (2 * mode + part) * 2 + side
                    value = terms[part][:, side * HALF : (side + 1) * HALF]
                    if slot:
                        value = value + total_probe[index]
                    total_probe[index] = value
                    if slot:
                        half, keep, send = deliver(index)
                        pl.when(core == half)(keep.start)
                        pl.when(core != half)(send.start)
        for part, value in enumerate((grad_re, grad_im)):
            grads[slot, part, :WIN] = pltpu.roll(pltpu.roll(value, corner[0], 0), corner[1], 1)
            row = row_place((INFO, WIN))
            info = jnp.where(row == 0, corner[0], jnp.where(row == 1, corner[1], corner[2]))
            grads[slot, part, WIN:] = info.astype(F32)
        pltpu.make_async_copy(grads.at[slot], out_grad.at[slot], out_sems.at[slot]).start()
    out_loss[...] = losses
    for index in range(4 * MODES):
        half, keep, send = deliver(index)
        pl.when(core == half)(keep.wait)
        pl.when(core != half)(send.wait)
    for slot in range(CAP):
        pltpu.make_async_copy(grads.at[slot], out_grad.at[slot], out_sems.at[slot]).wait()
    if iteration:
        mid_copy.wait()


def call(kernel, args, out_shape, n_smem):
    size = sum(math.prod(a.shape) * a.dtype.itemsize for a in (*args, *out_shape))
    return pl.pallas_call(
        kernel,
        out_shape=tuple(out_shape),
        in_specs=[SMEM] * n_smem + [VMEM] * (len(args) - n_smem),
        out_specs=tuple([VMEM] * len(out_shape)),
        compiler_params=pltpu.CompilerParams(vmem_limit_bytes=60 * MEGA),
        cost_estimate=pl.CostEstimate(flops=10_000_000, bytes_accessed=size, transcendentals=0),
    )(*args)


def window_call(iteration, corners, counts, data, amplitude, tables):
    outs = [f32(CAP, 2, WIN + INFO, WIN), f32(2 * MODES, WIN, HALF), f32(2 * MODES, WIN, HALF)]
    out_specs = [ANY] * 3
    if iteration:
        outs += [f32(2 * MODES, WIN, WIN), f32(8, HALF)]
        out_specs += [ANY, VMEM]
    big = [*data, tables[0], amplitude, tables[1]]
    return pl.pallas_call(
        lambda *refs: window_kernel(iteration, *refs),
        out_shape=(*outs, f32(8, HALF)),
        in_specs=[SMEM] * 2 + [ANY] * len(big),
        out_specs=(*out_specs, VMEM),
        scratch_shapes=[
            pltpu.VMEM((2, WIN, WIN), F32),
            pltpu.VMEM((MODES, 2, WIN, WIN), F32),
            pltpu.VMEM((2, WIN, HALF), F32),
            pltpu.VMEM((4 * MODES, WIN, HALF), F32),
            pltpu.VMEM((CAP, 2, WIN + INFO, WIN), F32),
            pltpu.SemaphoreType.DMA((len(big),)),
            pltpu.SemaphoreType.DMA((CAP,)),
            pltpu.SemaphoreType.DMA((4 * MODES,)),
            pltpu.SemaphoreType.DMA((1,)),
            *[pltpu.VMEM(value.shape, value.dtype) for value in big],
        ],
        compiler_params=pltpu.CompilerParams(vmem_limit_bytes=60 * MEGA),
        cost_estimate=pl.CostEstimate(flops=8_000_000_000, bytes_accessed=12_000_000, transcendentals=0),
    )(corners, counts, *big)


def fold_kernel(both, *refs):
    *refs, token, out0, out1, out2 = refs
    outs = (out0, out1, out2)
    rows, cols = row_place(), col_place((1, WIN))
    masks = []
    for windows in refs:
        for slot in range(CAP):
            info = windows[slot, 0, WIN:].astype(jnp.int32)
            masks.append((rows >= info[0:1], jnp.where(cols >= info[1:2], info[2:3], info[2:3] + 1)))
    for part in range(2):
        top, bottom = [0.0] * 3, [0.0] * 3
        for which, windows in enumerate(refs):
            for slot in range(CAP):
                first, target = masks[which * CAP + slot]
                window = windows[slot, part, :WIN]
                upper = jnp.where(first, window, 0.0) if which != 1 else None
                lower = jnp.where(first, 0.0, window) if which != 2 else None
                for index in range(3):
                    here = target == index
                    if which == 0:
                        top[index] += jnp.where(here, upper, 0.0)
                        if both:
                            bottom[index] += jnp.where(here, lower, 0.0)
                    elif which == 1:
                        top[index] += jnp.where(here, lower, 0.0)
                    else:
                        bottom[index] += jnp.where(here, upper, 0.0)
        for index in range(3):
            outs[index][0, part] = top[index]
            if both:
                outs[index][1, part] = bottom[index]
    outs[0][0, 0, :8, :HALF] = outs[0][0, 0, :8, :HALF] + token[...]


def add_kernel(keep, other, out):
    out[...] = keep[...] + other[...]


def sum_kernel(parts, out, out_token):
    out[...] = jnp.sum(parts[...], axis=0)
    out_token[...] = jnp.zeros_like(out_token)


def tile_kernel(block0, block1, from_left, parts, loss, loss_before, out_tile, out_sent, out_loss):
    chunk = jnp.sum(parts[...], axis=0)
    square = sum(chunk[k : k + 8] * chunk[k : k + 8] for k in range(0, CHUNK, 8))
    for part in range(2):
        values = (block0[0, part] + from_left[0, part], block1[0, part])
        for index, value in enumerate(values):
            out_tile[part, :, index * WIN : (index + 1) * WIN] = value
            pieces = jnp.sum((value * value).reshape(WIN // 8, 8, WIN), axis=0)
            square = square + (pieces[:, :HALF] + pieces[:, HALF:])
    loss = jnp.sum(loss[...])
    out_loss[...] = jnp.where(col_place((1, 2)) == 0, jnp.sum(loss_before[...]), loss)
    scalars = jnp.where(row_place((SENT - CHUNK, HALF)) == 0, loss, jnp.sum(square))
    value = jnp.concatenate([chunk, scalars], axis=0)
    for index in range(out_sent.shape[0]):
        out_sent[index] = value


def patch_kernel(corner_ref, tile, below0, below1, rim, diag, block0, block1, block2, left, right, out_obj, out_grad):
    for part in range(2):
        upper = (tile[part, :, :WIN], tile[part, :, WIN:], rim[part])
        lower = (below0[part], below1[part], diag[part])
        grad = [
            (block0[k, part] + left[k, part], block1[k, part], block2[k, part] + right[k, part]) for k in range(2)
        ]
        for slot in range(CAP):
            corner = corner_of(corner_ref, 1, slot)
            out_obj[slot, part] = cut(corner, upper, lower)
            out_grad[slot, part] = cut(corner, grad[0], grad[1])


def final_kernel(tile, grad_first, grad_second, rate_first, probe, mine, other, out_tile, out_probe):
    core = lax.axis_index("core")
    rate = rate_of(mine, other)
    wide = jnp.concatenate([rate, rate], axis=1)
    for plane, step in enumerate(probe_step(mine, other, core)):
        out_probe[plane] = probe[plane] - wide * step
    first = jnp.concatenate([rate_first[0:1]] * 4, axis=1)
    second = jnp.concatenate([rate] * 4, axis=1)
    for part in range(2):
        out_tile[part] = (tile[part] - first * grad_first[part]) - second * grad_second[part]


def shift(value, axis, steps):
    count = math.prod(lax.axis_size(a) for a in axis) if isinstance(axis, tuple) else lax.axis_size(axis)
    first, last = max(0, -steps), min(count, count - steps)
    return lax.ppermute(value, axis, [(source, source + steps) for source in range(first, last)])


COL = ("layer", "core")
CHIPS = ("layer", "row")


def body(object_field, probe, corners, counts, amplitude):
    layers, rows = lax.axis_size("layer"), lax.axis_size("row")
    tables = [jnp.asarray(table) for table in transform_tables()]
    probe = probe.reshape(2 * MODES, WIN, WIN)
    corners, counts = corners[:, 0, 0], counts[:, 0, 0]
    amplitude = amplitude[:, 0, 0]

    first_cols = object_field[:, :, :WIN]
    below0 = shift(first_cols, "row", -1)
    rim = shift(first_cols, COL, -1)
    below1 = shift(object_field[:, :, WIN:], "row", -1)
    diag = shift(below0, COL, -1)
    rims = (below0, below1, rim, diag)

    def swap(value):
        return lax.ppermute(value, "core", [(0, 1), (1, 0)])

    def reduce_chips(keep, send):
        (value,) = call(add_kernel, [keep, swap(send)], [f32(*keep.shape)], 0)
        parts = lax.all_to_all(value.reshape(layers, rows * CHUNK, HALF), "layer", 0, 0, tiled=True)
        return call(sum_kernel, [parts], [f32(rows * CHUNK, HALF), f32(8, HALF)], 0)

    def reduce_rows(part):
        return lax.all_to_all(part.reshape(rows, CHUNK, HALF), "row", 0, 0, tiled=True)

    def finish_tile(sums, from_left, parts, loss, loss_before):
        outs = [f32(2, WIN, 2 * WIN), f32(layers * rows, SENT, HALF), f32(1, 2)]
        args = [sums[0], sums[1], from_left, parts, loss, loss_before]
        tile, sent, losses = call(tile_kernel, args, outs, 0)
        return tile, lax.all_to_all(sent, CHIPS, 0, 0, tiled=True), losses

    def fold(*windows, token):
        both = len(windows) == 3
        strip = f32(1 + both, 2, WIN, WIN)
        return call(lambda *refs: fold_kernel(both, *refs), [*windows, token], [strip] * 3, 0)

    grads, keep, send, loss_first = window_call(
        0, corners, counts, [object_field, *rims, probe], amplitude, tables
    )
    down, up = shift(grads, "row", 1), shift(grads, "row", -1)
    part, token = reduce_chips(keep, send)
    sums = fold(grads, down, up, token=token)
    from_left, from_right = lax.optimization_barrier((shift(sums[2], COL, 1), shift(sums[0], COL, -1)))
    tile_first, mine, _ = finish_tile(sums, from_left, reduce_rows(part), loss_first, loss_first)
    patches = call(
        patch_kernel,
        [corners, object_field, *rims, *sums, from_left, from_right],
        [f32(CAP, 2, WIN, WIN)] * 2,
        1,
    )

    mine, patches = lax.optimization_barrier((mine, patches))

    grads, keep, send, probe_mid, rate_first, loss_second = window_call(
        1, corners, counts, [mine, swap(mine), *patches, probe], amplitude, tables
    )
    down = shift(grads, "row", 1)
    part, token = reduce_chips(keep, send)
    sums = fold(grads, down, token=token)
    from_left = shift(sums[2], COL, 1)
    tile_second, mine, losses = finish_tile(sums, from_left, reduce_rows(part), loss_second, loss_first)
    object_out, probe_out = call(
        final_kernel,
        [object_field, tile_first, tile_second, rate_first, probe_mid, mine, swap(mine)],
        [f32(2, WIN, 2 * WIN), f32(2 * MODES, WIN, WIN)],
        0,
    )
    losses = losses.reshape(1, 1, 2).transpose(2, 0, 1)
    return (object_out, probe_out.reshape(MODES, 2, WIN, WIN), losses)


def solution(mesh):
    rows, cols = mesh.shape["row"], mesh.shape["col"]
    fine = Mesh(mesh.devices.reshape(rows, cols // 2, 2), ("row", "layer", "core"))
    in_specs = (
        P(None, "row", COL),
        P(),
        P(None, "row", COL, None, None),
        P(None, "row", COL),
        P(None, "row", COL, None, None, None),
    )
    out_specs = (P(None, "row", COL), P(), P(None, "row", COL))
    return jax.shard_map(body, mesh=fine, in_specs=in_specs, out_specs=out_specs, check_vma=False)
```

time: 878 us -> 243 us (0.28); the launches traced: 866 us -> 242 us
  waiting for transfers between devices: 422 us -> 43 us
  matrix products: 122 us -> 0 us
  Pallas kernels: 0 us -> 64.2 us
  local copies, waits for them, and re-layouts: 66.9 us -> 9.34 us
  blocking collectives: 128 us -> 70.9 us
  other arithmetic: 53.8 us -> 0 us
  between operations: 18.9 us -> 0.84 us
  loops' own time: 16.3 us -> 0 us
  starting transfers between devices: 39 us -> 53.9 us
    psum x2 -> x0, waiting for transfers between devices: 287 us -> none  [body(): probe_grad = lax.psum(probe_part, ('row', 'col'))]
    psum x2 -> x0, blocking collectives: 128 us -> none  [body(): total_loss = lax.psum(loss_here, ('row', 'col'))]
    dot_general x32 -> x0, matrix products: 122 us -> none  [the longest x4 18 us: dft_pair(): jnp.einsum('bjn,nk->bjk', left_re, sine_part, precision=PRECISE)]
    ppermute x8 -> x14, waiting for transfers between devices: 134 us -> 28.2 us  [the longest x10 23.3 us: shift(): lax.ppermute(value, axis, [(source, source + steps) for source in range(f...]
    all_to_all x0 -> x4, blocking collectives: none -> 70.9 us  [the longest x2 33.1 us: reduce_chips(): lax.all_to_all(value.reshape(layers, rows * CHUNK, HALF), 'layer', 0, 0,...]
    pallas_call x0 -> x12, Pallas kernels: none -> 64.2 us  [the longest x10 35.3 us: call(): pl.pallas_call(kernel, out_shape=tuple(out_shape), in_specs=[SMEM] * n_sm...]
    dynamic_update_slice x4 -> x0, local copies, waits for them, and re-layouts: 26.1 us -> none  [deposit(): lax.dynamic_update_slice(grad_total, previous + obj_grads[index], start)]
    all_to_all x0 -> x2, starting transfers between devices: none -> 23.1 us  [the longest x1 11.7 us: reduce_rows(): lax.all_to_all(part.reshape(rows, CHUNK, HALF), 'row', 0, 0, tiled=True)]
  transfers between devices with their start and end apart: 10 -> 16, of which waited for: 10 -> 10; matrix products, arithmetic and copies ran while one was open for 2% -> 0% of each run, Pallas kernels for 0% -> 7%
where the time goes in v2:
time: 243 us; the launch traced here: 242 us
  blocking collectives  70.9 us (29%)
  Pallas kernels  64.2 us (26%)
  starting transfers between devices  53.9 us (22%)
  waiting for transfers between devices  43 us (18%)
  local copies, waits for them, and re-layouts  9.34 us (4%)
    pallas_call x10, Pallas kernels, call(): pl.pallas_call(kernel, out_shape=tuple(out_shape), in_specs=[SMEM] * n_sm...  35.3 us
    all_to_all x2, blocking collectives, reduce_chips(): lax.all_to_all(value.reshape(layers, rows * CHUNK, HALF), 'layer', 0, 0,...  33.1 us
    pallas_call x2, Pallas kernels, window_call(): pl.pallas_call(lambda *refs: window_kernel(iteration, *refs), out_shape=(...  28.9 us
    ppermute x10, starting transfers between devices, shift(): lax.ppermute(value, axis, [(source, source + steps) for source in range(f...  28.3 us
    ppermute x10, waiting for transfers between devices, shift(): lax.ppermute(value, axis, [(source, source + steps) for source in range(f...  23.3 us
    all_to_all x1, blocking collectives, finish_tile(): return (tile, lax.all_to_all(sent, CHIPS, 0, 0, tiled=True), losses)  23.3 us
    all_to_all x1, blocking collectives, reduce_rows(): lax.all_to_all(part.reshape(rows, CHUNK, HALF), 'row', 0, 0, tiled=True)  14.5 us
    all_to_all x1, starting transfers between devices, reduce_rows(): lax.all_to_all(part.reshape(rows, CHUNK, HALF), 'row', 0, 0, tiled=True)  11.7 us
  transfers between devices with their start and end apart: 16, of which 10 were waited for; matrix products, arithmetic and copies ran while one was open for 0% of the time, Pallas kernels for 7%

profile of v2, /device:TPU:1, one launch (start us, length us, event | category | flops | bytes accessed | tf_op | source)
XLA Modules:
  0.0 242.2 jit_solution(3411149386538033691)
XLA Ops:
  0.6 1.3 fusion
  1.9 1.3 collective-permute-start
  3.2 3.3 %collective-permute-start.2 = (f32[2,256,256]{2,1,0:T(8,128)S(1)}, f32[2,256,256]{2,1,0:T(8,128)S(1)}, u32[]{:S(2)}, u32[]{:S(2)}) collective-permute-start(f32[2,256,256]{2,1,0:T(8,128)S(1)} %get-tuple-element.72), channel_id=1, source_target_pairs={{1,0},{2,1},{3,2},{4,3},{5,4},{6,5},{7,6},{9,8},{10,9},{11,10},{12... | collective-permute-start | bytes 1572872 | tf_op jit(solution)/shard_map/ppermute | solution.py:392
  6.6 1.3 collective-permute-start.1
  7.9 9.3 %collective-permute-done.refs_3_.below0 = f32[2,256,256]{2,1,0:T(8,128)S(1)} collective-permute-done((f32[2,256,256]{2,1,0:T(8,128)S(1)}, f32[2,256,256]{2,1,0:T(8,128)S(1)}, u32[]{:S(2)}, u32[]{:S(2)}) %collective-permute-start) | collective-permute-done | bytes 524320 | tf_op jit(solution)/shard_map/ppermute | solution.py:392
  17.2 4.8 %collective-permute-start.3 = (f32[2,256,256]{2,1,0:T(8,128)S(1)}, f32[2,256,256]{2,1,0:T(8,128)S(1)}, u32[]{:S(2)}, u32[]{:S(2)}) collective-permute-start(f32[2,256,256]{2,1,0:T(8,128)S(1)} %collective-permute-done.refs_3_.below0), channel_id=1, source_target_pairs={{1,0},{2,1},{3,2},{4,3},{5,4},{6,5},{7,6},{9,8},{10,9},{11,10},{12... | collective-permute-start | bytes 1572872 | tf_op jit(solution)/shard_map/ppermute | solution.py:392
  22.0 6.5 %collective-permute-done.1.refs_4_.below1 = f32[2,256,256]{2,1,0:T(8,128)S(1)} collective-permute-done((f32[2,256,256]{2,1,0:T(8,128)S(1)}, f32[2,256,256]{2,1,0:T(8,128)S(1)}, u32[]{:S(2)}, u32[]{:S(2)}) %collective-permute-start.1) | collective-permute-done | bytes 524320 | tf_op jit(solution)/shard_map/ppermute | solution.py:392
  28.4 0.0 collective-permute-done.2.refs_5_.rim
  28.4 2.0 collective-permute-done.3.refs_6_.diag
  30.4 0.0 copy-done.11
  30.4 0.0 copy-done.13
  30.4 0.0 copy-done.12
  30.4 0.8 copy-done.14
  31.2 14.6 %shard_map.94 = (f32[2,2,264,256]{3,2,1,0:T(8,128)}, f32[6,256,128]{2,1,0:T(8,128)}, f32[6,256,128]{2,1,0:T(8,128)}, f32[8,128]{1,0:T(8,128)}) custom-call(s32[2,2,2]{2,1,0:T(2,128)} %bitcast.13, s32[2]{0:T(128)} %bitcast.21, f32[2,256,512]{2,1,0:T(8,128)} %tile.3, f32[2,256,256]{2,1,0:T(8,128)} %copy-done.11, f32[2,256,256]{2,1,0:T(8,128)} %copy-done.13, ...), custom_call_target="tpu_custom_call" | custom-call | flops 8000000000 | bytes 12000000 | tf_op jit(solution)/shard_map/pallas_call | solution.py:282
  45.9 0.1 collective-permute-start.6
  46.0 1.3 collective-permute-start.5
  47.3 4.1 %collective-permute-start.4 = (f32[2,2,264,256]{3,2,1,0:T(8,128)}, f32[2,2,264,256]{3,2,1,0:T(8,128)S(1)}, u32[]{:S(2)}, u32[]{:S(2)}) collective-permute-start(f32[2,2,264,256]{3,2,1,0:T(8,128)} %get-tuple-element.37.refs_0_), channel_id=1, source_target_pairs={{0,8},{8,16},{16,24},{24,32},{32,40},{40,48},{48,56},{56,64},{64,7... | collective-permute-start | bytes 3244040 | tf_op jit(solution)/shard_map/ppermute | solution.py:392
  51.3 0.0 collective-permute-done.6.other
  51.3 0.9 copy-done.9
  52.2 2.3 shard_map.95
  54.6 17.0 %all_to_all.30.parts = f32[4,384,128]{2,1,0:T(8,128)} all-to-all(f32[4,384,128]{2,1,0:T(8,128)} %bitcast.10), channel_id=1, replica_groups=mesh['row'=16,'layer'=4,'core'=2] {'layer'}, dimensions={0} | all-to-all | bytes 1572864 | tf_op jit(solution)/shard_map/all_to_all | solution.py:418
  71.5 1.8 shard_map.96
  73.4 0.0 collective-permute-done.5.refs_2_
  73.4 0.6 collective-permute-done.4.refs_1_
  74.0 0.4 copy-done.2
  74.4 0.6 copy-done.3
  75.0 4.7 %shard_map.97 = (f32[2,2,256,256]{3,2,1,0:T(8,128)}, f32[2,2,256,256]{3,2,1,0:T(8,128)}, f32[2,2,256,256]{3,2,1,0:T(8,128)}) custom-call(f32[2,2,264,256]{3,2,1,0:T(8,128)} %get-tuple-element.37.refs_0_, f32[2,2,264,256]{3,2,1,0:T(8,128)} %copy-done.3, f32[2,2,264,256]{3,2,1,0:T(8,128)} %copy-done.2, f32[8,128]{1,0:T(8,128)} %get-tuple-element.40.refs_3_), custom_call_target="tpu_custom_call" | custom-call | flops 10000000 | bytes 6393856 | tf_op jit(solution)/shard_map/pallas_call | solution.py:265
  79.7 5.2 %collective-permute-start.7 = (f32[2,2,256,256]{3,2,1,0:T(8,128)}, f32[2,2,256,256]{3,2,1,0:T(8,128)S(1)}, u32[]{:S(2)}, u32[]{:S(2)}) collective-permute-start(f32[2,2,256,256]{3,2,1,0:T(8,128)} %get-tuple-element.43.block2), channel_id=1, source_target_pairs={{0,1},{1,2},{2,3},{3,4},{4,5},{5,6},{6,7},{8,9},{9,10},{10,11},{11... | collective-permute-start | bytes 3145736 | tf_op jit(solution)/shard_map/ppermute | solution.py:392
  84.9 1.9 collective-permute-start.8
  86.9 11.7 %all-to-all-start.1 = ((f32[16,24,128]{2,1,0:T(8,128)}), f32[16,24,128]{2,1,0:T(8,128)S(1)}, u32[]{:S(2)}, u32[]{:S(2)}) async-start(f32[16,24,128]{2,1,0:T(8,128)} %bitcast.5), calls=%async_computation.1 | async-start | bytes 393216 | tf_op jit(solution)/shard_map/all_to_all | solution.py:422
  98.6 0.0 collective-permute-done.7.from_left.left
  98.6 0.0 copy-start
  98.6 2.9 %collective-permute-done.8.right = f32[2,2,256,256]{3,2,1,0:T(8,128)S(1)} collective-permute-done((f32[2,2,256,256]{3,2,1,0:T(8,128)}, f32[2,2,256,256]{3,2,1,0:T(8,128)S(1)}, u32[]{:S(2)}, u32[]{:S(2)}) %collective-permute-start.8) | collective-permute-done | bytes 1048608 | tf_op jit(solution)/shard_map/ppermute | solution.py:392
  101.6 4.0 %all-to-all-done.1.parts = f32[16,24,128]{2,1,0:T(8,128)S(1)} async-done(((f32[16,24,128]{2,1,0:T(8,128)}), f32[16,24,128]{2,1,0:T(8,128)S(1)}, u32[]{:S(2)}, u32[]{:S(2)}) %all-to-all-start.1) | async-done | bytes 196640 | tf_op jit(solution)/shard_map/all_to_all | solution.py:422
  105.5 0.7 copy-done.8
  106.2 3.4 %shard_map.98 = (f32[2,256,512]{2,1,0:T(8,128)}, f32[64,32,128]{2,1,0:T(8,128)}, f32[1,2]{1,0:T(1,128)}) custom-call(f32[2,2,256,256]{3,2,1,0:T(8,128)} %get-tuple-element.41.block0, f32[2,2,256,256]{3,2,1,0:T(8,128)} %get-tuple-element.42.block1, f32[2,2,256,256]{3,2,1,0:T(8,128)} %copy-done, f32[16,24,128]{2,1,0:T(8,128)} %copy-done.8, ...), custom_call_target="tpu_custom_call" | custom-call | flops 10000000 | bytes 5447688 | tf_op jit(solution)/shard_map/pallas_call | solution.py:265
  109.7 11.4 %all-to-all-start.2 = ((f32[64,32,128]{2,1,0:T(8,128)}), f32[64,32,128]{2,1,0:T(8,128)S(1)}, u32[]{:S(2)}, u32[]{:S(2)}) async-start(f32[64,32,128]{2,1,0:T(8,128)} %get-tuple-element.48), calls=%async_computation.2 | async-start | bytes 2097152 | tf_op jit(solution)/shard_map/all_to_all | solution.py:428
  121.1 7.6 %shard_map.99 = (f32[2,2,256,256]{3,2,1,0:T(8,128)}, f32[2,2,256,256]{3,2,1,0:T(8,128)}) custom-call(s32[2,2,2]{2,1,0:T(2,128)} %bitcast.14, f32[2,256,512]{2,1,0:T(8,128)} %tile.3, f32[2,256,256]{2,1,0:T(8,128)} %copy-done.11, f32[2,256,256]{2,1,0:T(8,128)} %copy-done.13, f32[2,256,256]{2,1,0:T(8,128)} %copy-done.12, f32[2,256,256]{2,1,0:T(8,128)} %copy-done.14, ...), custom_call_target="tpu_custom_call" | custom-call | flops 10000000 | bytes 10485792 | tf_op jit(solution)/shard_map/pallas_call | solution.py:265
  128.7 10.9 %all-to-all-done.2.refs_2_ = f32[64,32,128]{2,1,0:T(8,128)S(1)} async-done(((f32[64,32,128]{2,1,0:T(8,128)}), f32[64,32,128]{2,1,0:T(8,128)S(1)}, u32[]{:S(2)}, u32[]{:S(2)}) %all-to-all-start.2) | async-done | bytes 1048608 | tf_op jit(solution)/shard_map/all_to_all | solution.py:428
  139.6 0.1 collective-permute-start.9
  139.7 2.6 %collective-permute-done.9.refs_3_ = f32[64,32,128]{2,1,0:T(8,128)S(1)} collective-permute-done((f32[64,32,128]{2,1,0:T(8,128)S(1)}, f32[64,32,128]{2,1,0:T(8,128)S(1)}, u32[]{:S(2)}, u32[]{:S(2)}) %collective-permute-start.9) | collective-permute-done | bytes 1048608 | tf_op jit(solution)/shard_map/ppermute | solution.py:414
  142.3 1.0 copy-done.17
  143.2 14.2 %shard_map.100 = (f32[2,2,264,256]{3,2,1,0:T(8,128)}, f32[6,256,128]{2,1,0:T(8,128)}, f32[6,256,128]{2,1,0:T(8,128)}, f32[6,256,256]{2,1,0:T(8,128)}, f32[8,128]{1,0:T(8,128)}, /*index=5*/f32[8,128]{1,0:T(8,128)}) custom-call(s32[2,2,2]{2,1,0:T(2,128)} %bitcast.15, s32[2]{0:T(128)} %bitcast.22, f32[64,32,128]{2,1,0:T(8,128)} %copy-done.6, ...), custom_call_target="tpu_custom_call" | custom-call | flops 8000000000 | bytes 12000000 | tf_op jit(solution)/shard_map/pallas_call | solution.py:282
  157.5 0.2 collective-permute-start.11
  157.7 2.6 %collective-permute-start.10 = (f32[2,2,264,256]{3,2,1,0:T(8,128)}, f32[2,2,264,256]{3,2,1,0:T(8,128)S(1)}, u32[]{:S(2)}, u32[]{:S(2)}) collective-permute-start(f32[2,2,264,256]{3,2,1,0:T(8,128)} %get-tuple-element.55.refs_0_), channel_id=1, source_target_pairs={{0,8},{8,16},{16,24},{24,32},{32,40},{40,48},{48,56},{56,64},{64,7... | collective-permute-start | bytes 3244040 | tf_op jit(solution)/shard_map/ppermute | solution.py:392
  160.3 0.0 collective-permute-done.11.other
  160.3 0.0 copy-start.10
  160.3 0.9 copy-done.10
  161.2 2.4 shard_map.101
  163.5 16.1 %all_to_all.31.parts = f32[4,384,128]{2,1,0:T(8,128)} all-to-all(f32[4,384,128]{2,1,0:T(8,128)} %bitcast.11), channel_id=1, replica_groups=mesh['row'=16,'layer'=4,'core'=2] {'layer'}, dimensions={0} | all-to-all | bytes 1572864 | tf_op jit(solution)/shard_map/all_to_all | solution.py:418
  179.6 1.9 shard_map.102
  181.5 2.0 collective-permute-done.10.refs_1_
  183.5 1.0 copy-done.4
  184.5 3.4 %shard_map.103 = (f32[1,2,256,256]{3,2,1,0:T(8,128)}, f32[1,2,256,256]{3,2,1,0:T(8,128)}, f32[1,2,256,256]{3,2,1,0:T(8,128)}) custom-call(f32[2,2,264,256]{3,2,1,0:T(8,128)} %get-tuple-element.55.refs_0_, f32[2,2,264,256]{3,2,1,0:T(8,128)} %copy-done.4, f32[8,128]{1,0:T(8,128)} %get-tuple-element.58.refs_2_), custom_call_target="tpu_custom_call" | custom-call | flops 10000000 | bytes 3739648 | tf_op jit(solution)/shard_map/pallas_call | solution.py:265
  187.9 2.6 %collective-permute-start.12 = (f32[1,2,256,256]{3,2,1,0:T(8,128)}, f32[1,2,256,256]{3,2,1,0:T(8,128)S(1)}, u32[]{:S(2)}, u32[]{:S(2)}) collective-permute-start(f32[1,2,256,256]{3,2,1,0:T(8,128)} %get-tuple-element.61), channel_id=1, source_target_pairs={{0,1},{1,2},{2,3},{3,4},{4,5},{5,6},{6,7},{8,9},{9,10},{10,11},{11... | collective-permute-start | bytes 1572872 | tf_op jit(solution)/shard_map/ppermute | solution.py:392
  190.5 14.5 %all_to_all.32.parts = f32[16,24,128]{2,1,0:T(8,128)} all-to-all(f32[16,24,128]{2,1,0:T(8,128)S(1)} %bitcast.12), channel_id=1, replica_groups=mesh['row'=16,'layer'=4,'core'=2] {'row'}, dimensions={0} | all-to-all | bytes 393216 | tf_op jit(solution)/shard_map/all_to_all | solution.py:422
  205.0 0.0 collective-permute-done.12.from_left
  205.0 0.8 copy-done.15
  205.8 3.0 %shard_map.104 = (f32[2,256,512]{2,1,0:T(8,128)}, f32[64,32,128]{2,1,0:T(8,128)}, f32[1,2]{1,0:T(1,128)}) custom-call(f32[1,2,256,256]{3,2,1,0:T(8,128)} %get-tuple-element.59.block0, f32[1,2,256,256]{3,2,1,0:T(8,128)} %get-tuple-element.60.block1, f32[1,2,256,256]{3,2,1,0:T(8,128)} %copy-done.15, f32[16,24,128]{2,1,0:T(8,128)} %all_to_all.32.parts, ...), custom_call_target="tpu_custom_call" | custom-call | flops 10000000 | bytes 3874824 | tf_op jit(solution)/shard_map/pallas_call | solution.py:265
  208.8 23.3 %all_to_all.33.mine = f32[64,32,128]{2,1,0:T(8,128)S(1)} all-to-all(f32[64,32,128]{2,1,0:T(8,128)} %get-tuple-element.67), channel_id=1, replica_groups=mesh['row'=16,'layer'=4,'core'=2] {'layer','row'}, dimensions={0} | all-to-all | bytes 2097152 | tf_op jit(solution)/shard_map/all_to_all | solution.py:428
  232.1 2.1 collective-permute-start.13
  234.1 2.3 collective-permute-done.13.other
  236.4 1.0 copy-done.7
  237.4 4.8 %shard_map.105 = (f32[2,256,512]{2,1,0:T(8,128)}, f32[6,256,256]{2,1,0:T(8,128)}) custom-call(f32[2,256,512]{2,1,0:T(8,128)} %tile.3, f32[2,256,512]{2,1,0:T(8,128)} %get-tuple-element.47.grad_first, f32[2,256,512]{2,1,0:T(8,128)} %get-tuple-element.64.grad_second, f32[8,128]{1,0:T(8,128)} %get-tuple-element.65.rate_first, ...), custom_call_target="tpu_custom_call" | custom-call | flops 10000000 | bytes 9441280 | tf_op jit(solution)/shard_map/pallas_call | solution.py:265
  (21 shorter events, 0.0 us)
Async XLA Ops:
  1.9 15.3 %collective-permute-start = (f32[2,256,256]{2,1,0:T(8,128)S(1)}, f32[2,256,256]{2,1,0:T(8,128)S(1)}, u32[]{:S(2)}, u32[]{:S(2)}) collective-permute-start(f32[2,256,256]{2,1,0:T(8,128)S(1)} %get-tuple-element.72), channel_id=1, source_target_pairs={{8,0},{16,8},{24,16},{32,24},{40,32},{48,40},{56,48},{64,56},{72,6... | collective-permute-start | bytes 1572872 | tf_op jit(solution)/shard_map/ppermute | solution.py:392
  3.2 25.2 %collective-permute-start.2 = (f32[2,256,256]{2,1,0:T(8,128)S(1)}, f32[2,256,256]{2,1,0:T(8,128)S(1)}, u32[]{:S(2)}, u32[]{:S(2)}) collective-permute-start(f32[2,256,256]{2,1,0:T(8,128)S(1)} %get-tuple-element.72), channel_id=1, source_target_pairs={{1,0},{2,1},{3,2},{4,3},{5,4},{6,5},{7,6},{9,8},{10,9},{11,10},{12... | collective-permute-start | bytes 1572872 | tf_op jit(solution)/shard_map/ppermute | solution.py:392
  6.6 21.9 %collective-permute-start.1 = (f32[2,256,256]{2,1,0:T(8,128)S(1)}, f32[2,256,256]{2,1,0:T(8,128)S(1)}, u32[]{:S(2)}, u32[]{:S(2)}) collective-permute-start(f32[2,256,256]{2,1,0:T(8,128)S(1)} %get-tuple-element.71), channel_id=1, source_target_pairs={{8,0},{16,8},{24,16},{32,24},{40,32},{48,40},{56,48},{64,56},{72,6... | collective-permute-start | bytes 1572872 | tf_op jit(solution)/shard_map/ppermute | solution.py:392
  17.2 13.2 %copy-start.11 = (f32[2,256,256]{2,1,0:T(8,128)}, f32[2,256,256]{2,1,0:T(8,128)S(1)}, u32[]{:S(2)}) copy-start(f32[2,256,256]{2,1,0:T(8,128)S(1)} %collective-permute-done.refs_3_.below0) | copy-start | bytes 1572868
  17.2 13.2 %collective-permute-start.3 = (f32[2,256,256]{2,1,0:T(8,128)S(1)}, f32[2,256,256]{2,1,0:T(8,128)S(1)}, u32[]{:S(2)}, u32[]{:S(2)}) collective-permute-start(f32[2,256,256]{2,1,0:T(8,128)S(1)} %collective-permute-done.refs_3_.below0), channel_id=1, source_target_pairs={{1,0},{2,1},{3,2},{4,3},{5,4},{6,5},{7,6},{9,8},{10,9},{11,10},{12... | collective-permute-start | bytes 1572872 | tf_op jit(solution)/shard_map/ppermute | solution.py:392
  28.4 2.0 copy-start.13
  28.4 2.0 copy-start.12
  30.4 0.8 copy-start.14
  45.9 5.5 %collective-permute-start.6 = (f32[6,256,128]{2,1,0:T(8,128)}, f32[6,256,128]{2,1,0:T(8,128)S(1)}, u32[]{:S(2)}, u32[]{:S(2)}) collective-permute-start(f32[6,256,128]{2,1,0:T(8,128)} %get-tuple-element.39), channel_id=1, source_target_pairs={{0,1},{1,0},{2,3},{3,2},{4,5},{5,4},{6,7},{7,6},{8,9},{9,8},{10,11... | collective-permute-start | bytes 2359304 | tf_op jit(solution)/shard_map/ppermute | solution.py:414
  46.0 27.4 %collective-permute-start.5 = (f32[2,2,264,256]{3,2,1,0:T(8,128)}, f32[2,2,264,256]{3,2,1,0:T(8,128)S(1)}, u32[]{:S(2)}, u32[]{:S(2)}) collective-permute-start(f32[2,2,264,256]{3,2,1,0:T(8,128)} %get-tuple-element.37.refs_0_), channel_id=1, source_target_pairs={{8,0},{16,8},{24,16},{32,24},{40,32},{48,40},{56,48},{64,56},{72,6... | collective-permute-start | bytes 3244040 | tf_op jit(solution)/shard_map/ppermute | solution.py:392
  47.3 26.7 %collective-permute-start.4 = (f32[2,2,264,256]{3,2,1,0:T(8,128)}, f32[2,2,264,256]{3,2,1,0:T(8,128)S(1)}, u32[]{:S(2)}, u32[]{:S(2)}) collective-permute-start(f32[2,2,264,256]{3,2,1,0:T(8,128)} %get-tuple-element.37.refs_0_), channel_id=1, source_target_pairs={{0,8},{8,16},{16,24},{24,32},{32,40},{40,48},{48,56},{56,64},{64,7... | collective-permute-start | bytes 3244040 | tf_op jit(solution)/shard_map/ppermute | solution.py:392
  51.3 0.9 copy-start.9
  73.4 1.0 copy-start.2
  74.0 1.0 copy-start.3
  79.7 18.9 %collective-permute-start.7 = (f32[2,2,256,256]{3,2,1,0:T(8,128)}, f32[2,2,256,256]{3,2,1,0:T(8,128)S(1)}, u32[]{:S(2)}, u32[]{:S(2)}) collective-permute-start(f32[2,2,256,256]{3,2,1,0:T(8,128)} %get-tuple-element.43.block2), channel_id=1, source_target_pairs={{0,1},{1,2},{2,3},{3,4},{4,5},{5,6},{6,7},{8,9},{9,10},{10,11},{11... | collective-permute-start | bytes 3145736 | tf_op jit(solution)/shard_map/ppermute | solution.py:392
  84.9 16.6 %collective-permute-start.8 = (f32[2,2,256,256]{3,2,1,0:T(8,128)}, f32[2,2,256,256]{3,2,1,0:T(8,128)S(1)}, u32[]{:S(2)}, u32[]{:S(2)}) collective-permute-start(f32[2,2,256,256]{3,2,1,0:T(8,128)} %get-tuple-element.41.block0), channel_id=1, source_target_pairs={{1,0},{2,1},{3,2},{4,3},{5,4},{6,5},{7,6},{9,8},{10,9},{11,10},{12... | collective-permute-start | bytes 3145736 | tf_op jit(solution)/shard_map/ppermute | solution.py:392
  86.9 18.7 %all-to-all-start.1 = ((f32[16,24,128]{2,1,0:T(8,128)}), f32[16,24,128]{2,1,0:T(8,128)S(1)}, u32[]{:S(2)}, u32[]{:S(2)}) async-start(f32[16,24,128]{2,1,0:T(8,128)} %bitcast.5), calls=%async_computation.1 | async-start | bytes 393216 | tf_op jit(solution)/shard_map/all_to_all | solution.py:422
  98.6 6.9 %copy-start = (f32[2,2,256,256]{3,2,1,0:T(8,128)}, f32[2,2,256,256]{3,2,1,0:T(8,128)S(1)}, u32[]{:S(2)}) copy-start(f32[2,2,256,256]{3,2,1,0:T(8,128)S(1)} %collective-permute-done.7.from_left.left) | copy-start | bytes 3145732
  101.6 8.1 %copy-start.5 = (f32[2,2,256,256]{3,2,1,0:T(8,128)}, f32[2,2,256,256]{3,2,1,0:T(8,128)S(1)}, u32[]{:S(2)}) copy-start(f32[2,2,256,256]{3,2,1,0:T(8,128)S(1)} %collective-permute-done.8.right) | copy-start | bytes 3145732
  105.5 0.7 copy-start.8
  109.7 30.0 %all-to-all-start.2 = ((f32[64,32,128]{2,1,0:T(8,128)}), f32[64,32,128]{2,1,0:T(8,128)S(1)}, u32[]{:S(2)}, u32[]{:S(2)}) async-start(f32[64,32,128]{2,1,0:T(8,128)} %get-tuple-element.48), calls=%async_computation.2 | async-start | bytes 2097152 | tf_op jit(solution)/shard_map/all_to_all | solution.py:428
  139.6 2.7 %copy-start.6 = (f32[64,32,128]{2,1,0:T(8,128)}, f32[64,32,128]{2,1,0:T(8,128)S(1)}, u32[]{:S(2)}) copy-start(f32[64,32,128]{2,1,0:T(8,128)S(1)} %all-to-all-done.2.refs_2_) | copy-start | bytes 3145732
  139.6 2.7 %collective-permute-start.9 = (f32[64,32,128]{2,1,0:T(8,128)S(1)}, f32[64,32,128]{2,1,0:T(8,128)S(1)}, u32[]{:S(2)}, u32[]{:S(2)}) collective-permute-start(f32[64,32,128]{2,1,0:T(8,128)S(1)} %all-to-all-done.2.refs_2_), channel_id=1, source_target_pairs={{0,1},{1,0},{2,3},{3,2},{4,5},{5,4},{6,7},{7,6},{8,9},{9,8},{10,11... | collective-permute-start | bytes 3145736 | tf_op jit(solution)/shard_map/ppermute | solution.py:414
  142.3 1.0 copy-start.17
  157.5 2.8 %collective-permute-start.11 = (f32[6,256,128]{2,1,0:T(8,128)}, f32[6,256,128]{2,1,0:T(8,128)S(1)}, u32[]{:S(2)}, u32[]{:S(2)}) collective-permute-start(f32[6,256,128]{2,1,0:T(8,128)} %get-tuple-element.57), channel_id=1, source_target_pairs={{0,1},{1,0},{2,3},{3,2},{4,5},{5,4},{6,7},{7,6},{8,9},{9,8},{10,11... | collective-permute-start | bytes 2359304 | tf_op jit(solution)/shard_map/ppermute | solution.py:414
  157.7 25.8 %collective-permute-start.10 = (f32[2,2,264,256]{3,2,1,0:T(8,128)}, f32[2,2,264,256]{3,2,1,0:T(8,128)S(1)}, u32[]{:S(2)}, u32[]{:S(2)}) collective-permute-start(f32[2,2,264,256]{3,2,1,0:T(8,128)} %get-tuple-element.55.refs_0_), channel_id=1, source_target_pairs={{0,8},{8,16},{16,24},{24,32},{32,40},{40,48},{48,56},{56,64},{64,7... | collective-permute-start | bytes 3244040 | tf_op jit(solution)/shard_map/ppermute | solution.py:392
  160.3 0.9 copy-start.10
  183.5 1.0 copy-start.4
  184.5 6.0 %copy-start.16 = (f32[384,128]{1,0:T(8,128)S(1)}, f32[384,128]{1,0:T(8,128)}, u32[]{:S(2)}) copy-start(f32[384,128]{1,0:T(8,128)} %get-tuple-element.62) | copy-start | bytes 589828
  187.9 17.2 %collective-permute-start.12 = (f32[1,2,256,256]{3,2,1,0:T(8,128)}, f32[1,2,256,256]{3,2,1,0:T(8,128)S(1)}, u32[]{:S(2)}, u32[]{:S(2)}) collective-permute-start(f32[1,2,256,256]{3,2,1,0:T(8,128)} %get-tuple-element.61), channel_id=1, source_target_pairs={{0,1},{1,2},{2,3},{3,4},{4,5},{5,6},{6,7},{8,9},{9,10},{10,11},{11... | collective-permute-start | bytes 1572872 | tf_op jit(solution)/shard_map/ppermute | solution.py:392
  205.0 0.8 copy-start.15
  232.1 4.3 %copy-start.1 = (f32[64,32,128]{2,1,0:T(8,128)}, f32[64,32,128]{2,1,0:T(8,128)S(1)}, u32[]{:S(2)}) copy-start(f32[64,32,128]{2,1,0:T(8,128)S(1)} %all_to_all.33.mine) | copy-start | bytes 3145732
  232.1 4.3 %collective-permute-start.13 = (f32[64,32,128]{2,1,0:T(8,128)S(1)}, f32[64,32,128]{2,1,0:T(8,128)S(1)}, u32[]{:S(2)}, u32[]{:S(2)}) collective-permute-start(f32[64,32,128]{2,1,0:T(8,128)S(1)} %all_to_all.33.mine), channel_id=1, source_target_pairs={{0,1},{1,0},{2,3},{3,2},{4,5},{5,4},{6,7},{7,6},{8,9},{9,8},{10,11... | collective-permute-start | bytes 3145736 | tf_op jit(solution)/shard_map/ppermute | solution.py:414
  236.4 1.0 copy-start.7

commit v3 on v2

--- a/solution.py
+++ b/solution.py
@@ -61,10 +61,10 @@
     return product(table, jnp.concatenate([high, low, high], axis=0))
 
 
-def right_apply(data, table_ref, index):
-    high, low = split_bf16(data)
+def right_apply(lhs, odd, table_ref, index):
+    both, high = lhs[odd], lhs[odd, :, :WIN]
     table = jnp.concatenate([table_ref[index, 0], table_ref[index, 0], table_ref[index, 1]], axis=0)
-    return product(jnp.concatenate([high, low, high], axis=1), table)
+    return product(jnp.concatenate([both, high], axis=1), table)
 
 
 def row_place(shape=(WIN, WIN)):
@@ -128,16 +128,16 @@
     if iteration:
         out_mid, out_rate = refs[:2]
         refs = refs[2:]
-    out_loss, obj, field, factor, total_probe, grads, sems, out_sems, probe_sems, mid_sem = refs[:10]
-    held = refs[10:]
+    out_loss, obj, field, lhs, factor, total_probe, grads, sems, out_sems, probe_sems, mid_sem = refs[:11]
+    held = refs[11:]
     fetch = [pltpu.make_async_copy(src, dst, sems.at[k]) for k, (src, dst) in enumerate(zip(sources, held))]
     for copy in fetch:
         copy.start()
     if iteration == 0:
-        tile, below0, below1, rim, diag, probe_ref, tables, amp_ref, shuffle = held
+        tile, below0, below1, rim, diag, tables, probe_ref, amp_ref, shuffle = held
     else:
-        mine, other, patch, patch_grad, probe_ref, tables, amp_ref, shuffle = held
-    for copy in fetch[:-3]:
+        mine, other, probe_ref, patch, patch_grad, tables, amp_ref, shuffle = held
+    for copy in fetch[: 5 if iteration == 0 else 3]:
         copy.wait()
 
     if iteration:
@@ -159,6 +159,9 @@
     for slot in range(CAP):
         corner = corner_of(corner_ref, iteration, slot)
         alive = (slot < count_ref[iteration]).astype(F32)
+        if iteration and slot == 0:
+            for copy in fetch[3:5]:
+                copy.wait()
         for part in range(2):
             if iteration == 0:
                 obj[part] = cut(
@@ -170,7 +173,8 @@
                 obj[part] = patch[slot, part] - wide * patch_grad[slot, part]
 
         if slot == 0:
-            fetch[-3].wait()
+            for copy in fetch[5:-2]:
+                copy.wait()
         for mode in range(MODES):
             probe_re, probe_im = probe_ref[2 * mode], probe_ref[2 * mode + 1]
             exit_re = probe_re * obj[0] - probe_im * obj[1]
@@ -189,7 +193,11 @@
                 folded = jnp.concatenate(
                     [mid_re[:, :HALF] + sign * mid_re[:, HALF:], mid_im[:, :HALF] + sign * mid_im[:, HALF:]], axis=1
                 )
-                field[mode, odd] = right_apply(folded, tables, 2 + odd)
+                high, low = split_bf16(folded)
+                rows = slice(mode * WIN, (mode + 1) * WIN)
+                lhs[odd, rows, :WIN], lhs[odd, rows, WIN:] = high, low
+        for odd in range(2):
+            field[odd] = right_apply(lhs, odd, tables, 2 + odd)
 
         if slot == 0:
             fetch[-2].wait()
@@ -200,7 +208,8 @@
         for odd in range(2):
             total = jnp.ones((WIN, HALF), F32)
             for mode in range(MODES):
-                real, imag = field[mode, odd, :, :HALF], field[mode, odd, :, HALF:]
+                rows = slice(mode * WIN, (mode + 1) * WIN)
+                real, imag = field[odd, rows, :HALF], field[odd, rows, HALF:]
                 total = total + (real * real + imag * imag)
             inverse = lax.rsqrt(total)
             measured = amp[:, odd * HALF : (odd + 1) * HALF]
@@ -211,11 +220,16 @@
 
         grad_re = jnp.zeros((WIN, WIN), F32)
         grad_im = jnp.zeros((WIN, WIN), F32)
+        for odd in range(2):
+            scale = jnp.concatenate([factor[odd], factor[odd]], axis=1)
+            for mode in range(MODES):
+                rows = slice(mode * WIN, (mode + 1) * WIN)
+                high, low = split_bf16(field[odd, rows] * scale)
+                lhs[odd, rows, :WIN], lhs[odd, rows, WIN:] = high, low
+        for odd in range(2):
+            field[odd] = right_apply(lhs, odd, tables, odd)
         for mode in range(MODES):
-            half = []
-            for odd in range(2):
-                scale = jnp.concatenate([factor[odd], factor[odd]], axis=1)
-                half.append(right_apply(field[mode, odd] * scale, tables, odd))
+            half = [field[odd, mode * WIN : (mode + 1) * WIN] for odd in range(2)]
             mid_re = jnp.concatenate(
                 [half[0][:, :HALF] + half[1][:, :HALF], half[0][:, :HALF] - half[1][:, :HALF]], axis=1
             )
@@ -278,7 +292,7 @@
     if iteration:
         outs += [f32(2 * MODES, WIN, WIN), f32(8, HALF)]
         out_specs += [ANY, VMEM]
-    big = [*data, tables[0], amplitude, tables[1]]
+    big = [*data, amplitude, tables[1]]
     return pl.pallas_call(
         lambda *refs: window_kernel(iteration, *refs),
         out_shape=(*outs, f32(8, HALF)),
@@ -286,7 +300,8 @@
         out_specs=(*out_specs, VMEM),
         scratch_shapes=[
             pltpu.VMEM((2, WIN, WIN), F32),
-            pltpu.VMEM((MODES, 2, WIN, WIN), F32),
+            pltpu.VMEM((2, MODES * WIN, WIN), F32),
+            pltpu.VMEM((2, MODES * WIN, 2 * WIN), jnp.bfloat16),
             pltpu.VMEM((2, WIN, HALF), F32),
             pltpu.VMEM((4 * MODES, WIN, HALF), F32),
             pltpu.VMEM((CAP, 2, WIN + INFO, WIN), F32),
@@ -374,16 +389,51 @@
             out_grad[slot, part] = cut(corner, grad[0], grad[1])
 
 
-def final_kernel(tile, grad_first, grad_second, rate_first, probe, mine, other, out_tile, out_probe):
+def final_kernel(rate_first, *refs):
+    sources, (out_tile, out_probe) = refs[:6], refs[6:8]
+    held, (new_tile, new_probe), sems, tile_sems, probe_sems = refs[8:14], refs[14:16], *refs[16:]
+    fetch = [pltpu.make_async_copy(src, dst, sems.at[k]) for k, (src, dst) in enumerate(zip(sources, held))]
+    for copy in fetch:
+        copy.start()
+    mine, other, probe, tile, grad_first, grad_second = held
     core = lax.axis_index("core")
+    for copy in fetch[:3]:
+        copy.wait()
     rate = rate_of(mine, other)
     wide = jnp.concatenate([rate, rate], axis=1)
+    back = []
     for plane, step in enumerate(probe_step(mine, other, core)):
-        out_probe[plane] = probe[plane] - wide * step
+        new_probe[plane] = probe[plane] - wide * step
+        back.append(pltpu.make_async_copy(new_probe.at[plane], out_probe.at[plane], probe_sems.at[plane]))
+        back[-1].start()
+    for copy in fetch[3:]:
+        copy.wait()
     first = jnp.concatenate([rate_first[0:1]] * 4, axis=1)
     second = jnp.concatenate([rate] * 4, axis=1)
     for part in range(2):
-        out_tile[part] = (tile[part] - first * grad_first[part]) - second * grad_second[part]
+        new_tile[part] = (tile[part] - first * grad_first[part]) - second * grad_second[part]
+        back.append(pltpu.make_async_copy(new_tile.at[part], out_tile.at[part], tile_sems.at[part]))
+        back[-1].start()
+    for copy in back:
+        copy.wait()
+
+
+def final_call(rate_first, data):
+    outs = (f32(2, WIN, 2 * WIN), f32(2 * MODES, WIN, WIN))
+    return pl.pallas_call(
+        final_kernel,
+        out_shape=outs,
+        in_specs=[VMEM] + [ANY] * len(data),
+        out_specs=(ANY, ANY),
+        scratch_shapes=[
+            *[pltpu.VMEM(value.shape, value.dtype) for value in (*data, *outs)],
+            pltpu.SemaphoreType.DMA((len(data),)),
+            pltpu.SemaphoreType.DMA((2,)),
+            pltpu.SemaphoreType.DMA((2 * MODES,)),
+        ],
+        compiler_params=pltpu.CompilerParams(vmem_limit_bytes=60 * MEGA),
+        cost_estimate=pl.CostEstimate(flops=10_000_000, bytes_accessed=9_000_000, transcendentals=0),
+    )(rate_first, *data)
 
 
 def shift(value, axis, steps):
@@ -421,9 +471,9 @@
     def reduce_rows(part):
         return lax.all_to_all(part.reshape(rows, CHUNK, HALF), "row", 0, 0, tiled=True)
 
-    def finish_tile(sums, from_left, parts, loss, loss_before):
+    def finish_tile(sums, from_left, chunk, loss, loss_before):
         outs = [f32(2, WIN, 2 * WIN), f32(layers * rows, SENT, HALF), f32(1, 2)]
-        args = [sums[0], sums[1], from_left, parts, loss, loss_before]
+        args = [sums[0], sums[1], from_left, chunk, loss, loss_before]
         tile, sent, losses = call(tile_kernel, args, outs, 0)
         return tile, lax.all_to_all(sent, CHIPS, 0, 0, tiled=True), losses
 
@@ -433,13 +483,14 @@
         return call(lambda *refs: fold_kernel(both, *refs), [*windows, token], [strip] * 3, 0)
 
     grads, keep, send, loss_first = window_call(
-        0, corners, counts, [object_field, *rims, probe], amplitude, tables
+        0, corners, counts, [object_field, *rims, tables[0], probe], amplitude, tables
     )
     down, up = shift(grads, "row", 1), shift(grads, "row", -1)
     part, token = reduce_chips(keep, send)
     sums = fold(grads, down, up, token=token)
-    from_left, from_right = lax.optimization_barrier((shift(sums[2], COL, 1), shift(sums[0], COL, -1)))
-    tile_first, mine, _ = finish_tile(sums, from_left, reduce_rows(part), loss_first, loss_first)
+    chunk, sums = lax.optimization_barrier((reduce_rows(part), sums))
+    from_left, from_right = shift(sums[2], COL, 1), shift(sums[0], COL, -1)
+    tile_first, mine, _ = finish_tile(sums, from_left, chunk, loss_first, loss_first)
     patches = call(
         patch_kernel,
         [corners, object_field, *rims, *sums, from_left, from_right],
@@ -450,18 +501,16 @@
     mine, patches = lax.optimization_barrier((mine, patches))
 
     grads, keep, send, probe_mid, rate_first, loss_second = window_call(
-        1, corners, counts, [mine, swap(mine), *patches, probe], amplitude, tables
+        1, corners, counts, [mine, swap(mine), probe, *patches, tables[0]], amplitude, tables
     )
     down = shift(grads, "row", 1)
     part, token = reduce_chips(keep, send)
     sums = fold(grads, down, token=token)
+    chunk, sums = lax.optimization_barrier((reduce_rows(part), sums))
     from_left = shift(sums[2], COL, 1)
-    tile_second, mine, losses = finish_tile(sums, from_left, reduce_rows(part), loss_second, loss_first)
-    object_out, probe_out = call(
-        final_kernel,
-        [object_field, tile_first, tile_second, rate_first, probe_mid, mine, swap(mine)],
-        [f32(2, WIN, 2 * WIN), f32(2 * MODES, WIN, WIN)],
-        0,
+    tile_second, mine, losses = finish_tile(sums, from_left, chunk, loss_second, loss_first)
+    object_out, probe_out = final_call(
+        rate_first, [mine, swap(mine), probe_mid, object_field, tile_first, tile_second]
     )
     losses = losses.reshape(1, 1, 2).transpose(2, 0, 1)
     return (object_out, probe_out.reshape(MODES, 2, WIN, WIN), losses)

time: 243 us -> 240 us (0.988)
  blocking collectives: 70.9 us -> 55.4 us
  waiting for transfers between devices: 43 us -> 50.5 us
  starting transfers between devices: 53.9 us -> 59.5 us
  Pallas kernels: 64.2 us -> 61.4 us
    all_to_all x1 -> x0, blocking collectives: 14.5 us -> none  [reduce_rows(): lax.all_to_all(part.reshape(rows, CHUNK, HALF), 'row', 0, 0, tiled=True)]
    ppermute x10, waiting for transfers between devices: 23.3 us -> 34.3 us  [shift(): lax.ppermute(value, axis, [(source, source + steps) for source in range(f...]
    pallas_call x10 -> x9, Pallas kernels: 35.3 us -> 30.5 us  [call(): pl.pallas_call(kernel, out_shape=tuple(out_shape), in_specs=[SMEM] * n_sm...]
    pallas_call x0 -> x1, Pallas kernels: none -> 4.8 us  [final_call(): pl.pallas_call(final_kernel, out_shape=outs, in_specs=[VMEM] + [ANY] * le...]
    all_to_all x1, starting transfers between devices: 11.4 us -> 7.11 us  [finish_tile(): return (tile, lax.all_to_all(sent, CHIPS, 0, 0, tiled=True), losses)]
    ppermute x4, starting transfers between devices: 2.46 us -> 6.63 us  [swap(): return lax.ppermute(value, 'core', [(0, 1), (1, 0)])]
    all_to_all x1 -> x2, starting transfers between devices: 11.7 us -> 15.2 us  [reduce_rows(): lax.all_to_all(part.reshape(rows, CHUNK, HALF), 'row', 0, 0, tiled=True)]
    all_to_all x1, waiting for transfers between devices: 10.9 us -> 8.08 us  [finish_tile(): return (tile, lax.all_to_all(sent, CHIPS, 0, 0, tiled=True), losses)]
  transfers between devices with their start and end apart: 16 -> 17, of which waited for: 10 -> 10; matrix products, arithmetic and copies ran while one was open for 0% -> 0% of each run, Pallas kernels for 7% -> 12%
where the time goes in v3:
time: 240 us; the launch traced here: 239 us
  Pallas kernels  61.4 us (26%)
  starting transfers between devices  59.5 us (25%)
  blocking collectives  55.4 us (23%)
  waiting for transfers between devices  50.5 us (21%)
  local copies, waits for them, and re-layouts  10.8 us (4%)
    ppermute x10, waiting for transfers between devices, shift(): lax.ppermute(value, axis, [(source, source + steps) for source in range(f...  34.3 us
    all_to_all x2, blocking collectives, reduce_chips(): lax.all_to_all(value.reshape(layers, rows * CHUNK, HALF), 'layer', 0, 0,...  32.9 us
    ppermute x10, starting transfers between devices, shift(): lax.ppermute(value, axis, [(source, source + steps) for source in range(f...  30.6 us
    pallas_call x9, Pallas kernels, call(): pl.pallas_call(kernel, out_shape=tuple(out_shape), in_specs=[SMEM] * n_sm...  30.5 us
    pallas_call x2, Pallas kernels, window_call(): pl.pallas_call(lambda *refs: window_kernel(iteration, *refs), out_shape=(...  26.1 us
    all_to_all x1, blocking collectives, finish_tile(): return (tile, lax.all_to_all(sent, CHIPS, 0, 0, tiled=True), losses)  22.5 us
    all_to_all x2, starting transfers between devices, reduce_rows(): lax.all_to_all(part.reshape(rows, CHUNK, HALF), 'row', 0, 0, tiled=True)  15.2 us
    unnamed x36, local copies, waits for them, and re-layouts  9.56 us
  transfers between devices with their start and end apart: 17, of which 10 were waited for; matrix products, arithmetic and copies ran while one was open for 0% of the time, Pallas kernels for 12%

profile of v3, /device:TPU:1, one launch (start us, length us, event | category | flops | bytes accessed | tf_op | source)
XLA Modules:
  0.0 238.7 jit_solution(12270764097958901140)
XLA Ops:
  0.6 1.3 fusion
  1.9 1.3 collective-permute-start
  3.2 3.3 %collective-permute-start.2 = (f32[2,256,256]{2,1,0:T(8,128)S(1)}, f32[2,256,256]{2,1,0:T(8,128)S(1)}, u32[]{:S(2)}, u32[]{:S(2)}) collective-permute-start(f32[2,256,256]{2,1,0:T(8,128)S(1)} %get-tuple-element.84), channel_id=1, source_target_pairs={{1,0},{2,1},{3,2},{4,3},{5,4},{6,5},{7,6},{9,8},{10,9},{11,10},{12... | collective-permute-start | bytes 1572872 | tf_op jit(solution)/shard_map/ppermute | solution.py:442
  6.6 1.3 collective-permute-start.1
  7.9 9.3 %collective-permute-done.refs_3_.below0 = f32[2,256,256]{2,1,0:T(8,128)S(1)} collective-permute-done((f32[2,256,256]{2,1,0:T(8,128)S(1)}, f32[2,256,256]{2,1,0:T(8,128)S(1)}, u32[]{:S(2)}, u32[]{:S(2)}) %collective-permute-start) | collective-permute-done | bytes 524320 | tf_op jit(solution)/shard_map/ppermute | solution.py:442
  17.2 4.8 %collective-permute-start.3 = (f32[2,256,256]{2,1,0:T(8,128)S(1)}, f32[2,256,256]{2,1,0:T(8,128)S(1)}, u32[]{:S(2)}, u32[]{:S(2)}) collective-permute-start(f32[2,256,256]{2,1,0:T(8,128)S(1)} %collective-permute-done.refs_3_.below0), channel_id=1, source_target_pairs={{1,0},{2,1},{3,2},{4,3},{5,4},{6,5},{7,6},{9,8},{10,9},{11,10},{12... | collective-permute-start | bytes 1572872 | tf_op jit(solution)/shard_map/ppermute | solution.py:442
  22.0 6.5 %collective-permute-done.1.refs_4_.below1 = f32[2,256,256]{2,1,0:T(8,128)S(1)} collective-permute-done((f32[2,256,256]{2,1,0:T(8,128)S(1)}, f32[2,256,256]{2,1,0:T(8,128)S(1)}, u32[]{:S(2)}, u32[]{:S(2)}) %collective-permute-start.1) | collective-permute-done | bytes 524320 | tf_op jit(solution)/shard_map/ppermute | solution.py:442
  28.4 0.0 collective-permute-done.2.refs_5_.rim
  28.4 2.0 collective-permute-done.3.refs_6_.diag
  30.4 0.8 copy-done.15
  31.2 13.2 %shard_map.94 = (f32[2,2,264,256]{3,2,1,0:T(8,128)}, f32[6,256,128]{2,1,0:T(8,128)}, f32[6,256,128]{2,1,0:T(8,128)}, f32[8,128]{1,0:T(8,128)}) custom-call(s32[2,2,2]{2,1,0:T(2,128)} %bitcast.14, s32[2]{0:T(128)} %bitcast.22, f32[2,256,512]{2,1,0:T(8,128)} %refs_3_.1, f32[2,256,256]{2,1,0:T(8,128)} %copy-done.12, f32[2,256,256]{2,1,0:T(8,128)} %copy-done.14, ...), custom_call_target="tpu_custom_call" | custom-call | flops 8000000000 | bytes 12000000 | tf_op jit(solution)/shard_map/pallas_call | solution.py:296
  44.4 0.1 collective-permute-start.4
  44.5 1.3 collective-permute-start.6
  45.8 4.1 %collective-permute-start.5 = (f32[2,2,264,256]{3,2,1,0:T(8,128)}, f32[2,2,264,256]{3,2,1,0:T(8,128)S(1)}, u32[]{:S(2)}, u32[]{:S(2)}) collective-permute-start(f32[2,2,264,256]{3,2,1,0:T(8,128)} %get-tuple-element.46.refs_0_), channel_id=1, source_target_pairs={{0,8},{8,16},{16,24},{24,32},{32,40},{40,48},{48,56},{56,64},{64,7... | collective-permute-start | bytes 3244040 | tf_op jit(solution)/shard_map/ppermute | solution.py:442
  49.9 0.0 collective-permute-done.4.other
  49.9 0.9 copy-done.10
  50.8 2.3 shard_map.95
  53.1 16.7 %all_to_all.30.parts = f32[4,384,128]{2,1,0:T(8,128)} all-to-all(f32[4,384,128]{2,1,0:T(8,128)} %bitcast.10), channel_id=1, replica_groups=mesh['row'=16,'layer'=4,'core'=2] {'layer'}, dimensions={0} | all-to-all | bytes 1572864 | tf_op jit(solution)/shard_map/all_to_all | solution.py:468
  69.8 1.9 shard_map.96
  71.6 10.7 %all-to-all-start.1 = ((f32[16,24,128]{2,1,0:T(8,128)}), f32[16,24,128]{2,1,0:T(8,128)S(1)}, u32[]{:S(2)}, u32[]{:S(2)}) async-start(f32[16,24,128]{2,1,0:T(8,128)} %bitcast.12), calls=%async_computation.1 | async-start | bytes 393216 | tf_op jit(solution)/shard_map/all_to_all | solution.py:472
  82.4 0.0 collective-permute-done.6.refs_2_
  82.4 0.0 collective-permute-done.5.refs_1_
  82.4 0.0 copy-start.3
  82.4 1.0 copy-done.2
  83.4 0.3 copy-done.3
  83.7 4.8 %shard_map.97 = (f32[2,2,256,256]{3,2,1,0:T(8,128)}, f32[2,2,256,256]{3,2,1,0:T(8,128)}, f32[2,2,256,256]{3,2,1,0:T(8,128)}) custom-call(f32[2,2,264,256]{3,2,1,0:T(8,128)} %get-tuple-element.46.refs_0_, f32[2,2,264,256]{3,2,1,0:T(8,128)} %copy-done.3, f32[2,2,264,256]{3,2,1,0:T(8,128)} %copy-done.2, f32[8,128]{1,0:T(8,128)} %get-tuple-element.47.refs_3_), custom_call_target="tpu_custom_call" | custom-call | flops 10000000 | bytes 6393856 | tf_op jit(solution)/shard_map/pallas_call | solution.py:279
  88.4 1.0 all-to-all-done.1.parts
  89.4 5.4 %collective-permute-start.7 = (f32[2,2,256,256]{3,2,1,0:T(8,128)}, f32[2,2,256,256]{3,2,1,0:T(8,128)S(1)}, u32[]{:S(2)}, u32[]{:S(2)}) collective-permute-start(f32[2,2,256,256]{3,2,1,0:T(8,128)} %get-tuple-element.53.block2), channel_id=1, source_target_pairs={{0,1},{1,2},{2,3},{3,4},{4,5},{5,6},{6,7},{8,9},{9,10},{10,11},{11... | collective-permute-start | bytes 3145736 | tf_op jit(solution)/shard_map/ppermute | solution.py:442
  94.9 1.9 collective-permute-start.8
  96.8 10.1 %collective-permute-done.7.from_left.left = f32[2,2,256,256]{3,2,1,0:T(8,128)S(1)} collective-permute-done((f32[2,2,256,256]{3,2,1,0:T(8,128)}, f32[2,2,256,256]{3,2,1,0:T(8,128)S(1)}, u32[]{:S(2)}, u32[]{:S(2)}) %collective-permute-start.7) | collective-permute-done | bytes 1048608 | tf_op jit(solution)/shard_map/ppermute | solution.py:442
  106.9 1.0 copy-done
  107.9 3.5 %shard_map.98 = (f32[2,256,512]{2,1,0:T(8,128)}, f32[64,32,128]{2,1,0:T(8,128)}, f32[1,2]{1,0:T(1,128)}) custom-call(f32[2,2,256,256]{3,2,1,0:T(8,128)} %get-tuple-element.51.block0, f32[2,2,256,256]{3,2,1,0:T(8,128)} %get-tuple-element.52.block1, f32[2,2,256,256]{3,2,1,0:T(8,128)} %copy-done, f32[16,24,128]{2,1,0:T(8,128)} %copy-done.8, ...), custom_call_target="tpu_custom_call" | custom-call | flops 10000000 | bytes 5447688 | tf_op jit(solution)/shard_map/pallas_call | solution.py:279
  111.4 7.1 %all-to-all-start.2 = ((f32[64,32,128]{2,1,0:T(8,128)}), f32[64,32,128]{2,1,0:T(8,128)S(1)}, u32[]{:S(2)}, u32[]{:S(2)}) async-start(f32[64,32,128]{2,1,0:T(8,128)} %get-tuple-element.56), calls=%async_computation.2 | async-start | bytes 2097152 | tf_op jit(solution)/shard_map/all_to_all | solution.py:478
  118.5 0.0 collective-permute-done.8.right
  118.5 1.0 copy-done.5
  119.5 7.6 %shard_map.99 = (f32[2,2,256,256]{3,2,1,0:T(8,128)}, f32[2,2,256,256]{3,2,1,0:T(8,128)}) custom-call(s32[2,2,2]{2,1,0:T(2,128)} %bitcast.15, f32[2,256,512]{2,1,0:T(8,128)} %refs_3_.1, f32[2,256,256]{2,1,0:T(8,128)} %copy-done.12, f32[2,256,256]{2,1,0:T(8,128)} %copy-done.14, f32[2,256,256]{2,1,0:T(8,128)} %copy-done.13, f32[2,256,256]{2,1,0:T(8,128)} %copy-done.15, ...), custom_call_target="tpu_custom_call" | custom-call | flops 10000000 | bytes 10485792 | tf_op jit(solution)/shard_map/pallas_call | solution.py:279
  127.1 8.1 %all-to-all-done.2.refs_2_ = f32[64,32,128]{2,1,0:T(8,128)S(1)} async-done(((f32[64,32,128]{2,1,0:T(8,128)}), f32[64,32,128]{2,1,0:T(8,128)S(1)}, u32[]{:S(2)}, u32[]{:S(2)}) %all-to-all-start.2) | async-done | bytes 1048608 | tf_op jit(solution)/shard_map/all_to_all | solution.py:478
  135.1 3.0 %collective-permute-start.9 = (f32[64,32,128]{2,1,0:T(8,128)S(1)}, f32[64,32,128]{2,1,0:T(8,128)S(1)}, u32[]{:S(2)}, u32[]{:S(2)}) collective-permute-start(f32[64,32,128]{2,1,0:T(8,128)S(1)} %all-to-all-done.2.refs_2_), channel_id=1, source_target_pairs={{0,1},{1,0},{2,3},{3,2},{4,5},{5,4},{6,7},{7,6},{8,9},{9,8},{10,11... | collective-permute-start | bytes 3145736 | tf_op jit(solution)/shard_map/ppermute | solution.py:464
  138.2 2.3 collective-permute-done.9.refs_3_
  140.5 1.0 copy-done.17
  141.4 12.9 %shard_map.100 = (f32[2,2,264,256]{3,2,1,0:T(8,128)}, f32[6,256,128]{2,1,0:T(8,128)}, f32[6,256,128]{2,1,0:T(8,128)}, f32[6,256,256]{2,1,0:T(8,128)}, f32[8,128]{1,0:T(8,128)}, /*index=5*/f32[8,128]{1,0:T(8,128)}) custom-call(s32[2,2,2]{2,1,0:T(2,128)} %bitcast.16, s32[2]{0:T(128)} %bitcast.23, f32[64,32,128]{2,1,0:T(8,128)} %copy-done.6, ...), custom_call_target="tpu_custom_call" | custom-call | flops 8000000000 | bytes 12000000 | tf_op jit(solution)/shard_map/pallas_call | solution.py:296
  154.4 0.5 collective-permute-start.10
  154.8 2.4 %collective-permute-start.11 = (f32[2,2,264,256]{3,2,1,0:T(8,128)}, f32[2,2,264,256]{3,2,1,0:T(8,128)S(1)}, u32[]{:S(2)}, u32[]{:S(2)}) collective-permute-start(f32[2,2,264,256]{3,2,1,0:T(8,128)} %get-tuple-element.66.refs_0_), channel_id=1, source_target_pairs={{0,8},{8,16},{16,24},{24,32},{32,40},{40,48},{48,56},{56,64},{64,7... | collective-permute-start | bytes 3244040 | tf_op jit(solution)/shard_map/ppermute | solution.py:442
  157.3 0.0 collective-permute-done.10.other
  157.3 0.0 copy-start.11
  157.3 0.9 copy-done.11
  158.2 2.3 shard_map.101
  160.5 16.2 %all_to_all.31.parts = f32[4,384,128]{2,1,0:T(8,128)} all-to-all(f32[4,384,128]{2,1,0:T(8,128)} %bitcast.11), channel_id=1, replica_groups=mesh['row'=16,'layer'=4,'core'=2] {'layer'}, dimensions={0} | all-to-all | bytes 1572864 | tf_op jit(solution)/shard_map/all_to_all | solution.py:468
  176.7 1.8 shard_map.102
  178.5 4.5 %all-to-all-start.4 = ((f32[16,24,128]{2,1,0:T(8,128)}), f32[16,24,128]{2,1,0:T(8,128)S(1)}, u32[]{:S(2)}, u32[]{:S(2)}) async-start(f32[16,24,128]{2,1,0:T(8,128)} %bitcast.13), calls=%async_computation.4 | async-start | bytes 393216 | tf_op jit(solution)/shard_map/all_to_all | solution.py:472
  183.0 0.0 collective-permute-done.11.refs_1_
  183.0 1.0 copy-done.4
  184.0 3.3 %shard_map.103 = (f32[1,2,256,256]{3,2,1,0:T(8,128)}, f32[1,2,256,256]{3,2,1,0:T(8,128)}, f32[1,2,256,256]{3,2,1,0:T(8,128)}) custom-call(f32[2,2,264,256]{3,2,1,0:T(8,128)} %get-tuple-element.66.refs_0_, f32[2,2,264,256]{3,2,1,0:T(8,128)} %copy-done.4, f32[8,128]{1,0:T(8,128)} %get-tuple-element.67.refs_2_), custom_call_target="tpu_custom_call" | custom-call | flops 10000000 | bytes 3739648 | tf_op jit(solution)/shard_map/pallas_call | solution.py:279
  187.4 2.6 %all-to-all-done.4.parts = f32[16,24,128]{2,1,0:T(8,128)S(1)} async-done(((f32[16,24,128]{2,1,0:T(8,128)}), f32[16,24,128]{2,1,0:T(8,128)S(1)}, u32[]{:S(2)}, u32[]{:S(2)}) %all-to-all-start.4) | async-done | bytes 196640 | tf_op jit(solution)/shard_map/all_to_all | solution.py:472
  189.9 4.8 %collective-permute-start.12 = (f32[1,2,256,256]{3,2,1,0:T(8,128)}, f32[1,2,256,256]{3,2,1,0:T(8,128)S(1)}, u32[]{:S(2)}, u32[]{:S(2)}) collective-permute-start(f32[1,2,256,256]{3,2,1,0:T(8,128)} %get-tuple-element.73), channel_id=1, source_target_pairs={{0,1},{1,2},{2,3},{3,4},{4,5},{5,6},{6,7},{8,9},{9,10},{10,11},{11... | collective-permute-start | bytes 1572872 | tf_op jit(solution)/shard_map/ppermute | solution.py:442
  194.7 6.4 %collective-permute-done.12.from_left = f32[1,2,256,256]{3,2,1,0:T(8,128)S(1)} collective-permute-done((f32[1,2,256,256]{3,2,1,0:T(8,128)}, f32[1,2,256,256]{3,2,1,0:T(8,128)S(1)}, u32[]{:S(2)}, u32[]{:S(2)}) %collective-permute-start.12) | collective-permute-done | bytes 524320 | tf_op jit(solution)/shard_map/ppermute | solution.py:442
  201.1 0.0 copy-done.9
  201.1 0.8 copy-done.16
  201.9 3.0 %shard_map.104 = (f32[2,256,512]{2,1,0:T(8,128)}, f32[64,32,128]{2,1,0:T(8,128)}, f32[1,2]{1,0:T(1,128)}) custom-call(f32[1,2,256,256]{3,2,1,0:T(8,128)} %get-tuple-element.71.block0, f32[1,2,256,256]{3,2,1,0:T(8,128)} %get-tuple-element.72.block1, f32[1,2,256,256]{3,2,1,0:T(8,128)} %copy-done.16, f32[16,24,128]{2,1,0:T(8,128)} %copy-done.9, ...), custom_call_target="tpu_custom_call" | custom-call | flops 10000000 | bytes 3874824 | tf_op jit(solution)/shard_map/pallas_call | solution.py:279
  204.9 22.5 %all_to_all.32.refs_0_ = f32[64,32,128]{2,1,0:T(8,128)S(1)} all-to-all(f32[64,32,128]{2,1,0:T(8,128)} %get-tuple-element.76), channel_id=1, replica_groups=mesh['row'=16,'layer'=4,'core'=2] {'layer','row'}, dimensions={0} | all-to-all | bytes 2097152 | tf_op jit(solution)/shard_map/all_to_all | solution.py:478
  227.4 3.0 %collective-permute-start.13 = (f32[64,32,128]{2,1,0:T(8,128)S(1)}, f32[64,32,128]{2,1,0:T(8,128)S(1)}, u32[]{:S(2)}, u32[]{:S(2)}) collective-permute-start(f32[64,32,128]{2,1,0:T(8,128)S(1)} %all_to_all.32.refs_0_), channel_id=1, source_target_pairs={{0,1},{1,0},{2,3},{3,2},{4,5},{5,4},{6,7},{7,6},{8,9},{9,8},{10,11... | collective-permute-start | bytes 3145736 | tf_op jit(solution)/shard_map/ppermute | solution.py:464
  230.4 2.3 collective-permute-done.13.refs_1_
  232.7 1.0 copy-done.7
  233.7 4.8 %shard_map.105 = (f32[2,256,512]{2,1,0:T(8,128)}, f32[6,256,256]{2,1,0:T(8,128)}) custom-call(f32[8,128]{1,0:T(8,128)} %get-tuple-element.62.rate_first, f32[64,32,128]{2,1,0:T(8,128)} %copy-done.1, f32[64,32,128]{2,1,0:T(8,128)} %copy-done.7, f32[6,256,256]{2,1,0:T(8,128)} %get-tuple-element.77.refs_2_, f32[2,256,512]{2,1,0:T(8,128)} %refs_3_.1, ...), custom_call_target="tpu_custom_call" | custom-call | flops 10000000 | bytes 9000000 | tf_op jit(solution)/shard_map/pallas_call | solution.py:423
  (22 shorter events, 0.0 us)
Async XLA Ops:
  1.9 15.3 %collective-permute-start = (f32[2,256,256]{2,1,0:T(8,128)S(1)}, f32[2,256,256]{2,1,0:T(8,128)S(1)}, u32[]{:S(2)}, u32[]{:S(2)}) collective-permute-start(f32[2,256,256]{2,1,0:T(8,128)S(1)} %get-tuple-element.84), channel_id=1, source_target_pairs={{8,0},{16,8},{24,16},{32,24},{40,32},{48,40},{56,48},{64,56},{72,6... | collective-permute-start | bytes 1572872 | tf_op jit(solution)/shard_map/ppermute | solution.py:442
  3.2 25.2 %collective-permute-start.2 = (f32[2,256,256]{2,1,0:T(8,128)S(1)}, f32[2,256,256]{2,1,0:T(8,128)S(1)}, u32[]{:S(2)}, u32[]{:S(2)}) collective-permute-start(f32[2,256,256]{2,1,0:T(8,128)S(1)} %get-tuple-element.84), channel_id=1, source_target_pairs={{1,0},{2,1},{3,2},{4,3},{5,4},{6,5},{7,6},{9,8},{10,9},{11,10},{12... | collective-permute-start | bytes 1572872 | tf_op jit(solution)/shard_map/ppermute | solution.py:442
  6.6 21.9 %collective-permute-start.1 = (f32[2,256,256]{2,1,0:T(8,128)S(1)}, f32[2,256,256]{2,1,0:T(8,128)S(1)}, u32[]{:S(2)}, u32[]{:S(2)}) collective-permute-start(f32[2,256,256]{2,1,0:T(8,128)S(1)} %get-tuple-element.83), channel_id=1, source_target_pairs={{8,0},{16,8},{24,16},{32,24},{40,32},{48,40},{56,48},{64,56},{72,6... | collective-permute-start | bytes 1572872 | tf_op jit(solution)/shard_map/ppermute | solution.py:442
  17.2 13.2 %copy-start.12 = (f32[2,256,256]{2,1,0:T(8,128)}, f32[2,256,256]{2,1,0:T(8,128)S(1)}, u32[]{:S(2)}) copy-start(f32[2,256,256]{2,1,0:T(8,128)S(1)} %collective-permute-done.refs_3_.below0) | copy-start | bytes 1572868
  17.2 13.2 %collective-permute-start.3 = (f32[2,256,256]{2,1,0:T(8,128)S(1)}, f32[2,256,256]{2,1,0:T(8,128)S(1)}, u32[]{:S(2)}, u32[]{:S(2)}) collective-permute-start(f32[2,256,256]{2,1,0:T(8,128)S(1)} %collective-permute-done.refs_3_.below0), channel_id=1, source_target_pairs={{1,0},{2,1},{3,2},{4,3},{5,4},{6,5},{7,6},{9,8},{10,9},{11,10},{12... | collective-permute-start | bytes 1572872 | tf_op jit(solution)/shard_map/ppermute | solution.py:442
  28.4 2.0 copy-start.14
  28.4 2.0 copy-start.13
  30.4 0.8 copy-start.15
  44.4 5.5 %collective-permute-start.4 = (f32[6,256,128]{2,1,0:T(8,128)}, f32[6,256,128]{2,1,0:T(8,128)S(1)}, u32[]{:S(2)}, u32[]{:S(2)}) collective-permute-start(f32[6,256,128]{2,1,0:T(8,128)} %get-tuple-element.44), channel_id=1, source_target_pairs={{0,1},{1,0},{2,3},{3,2},{4,5},{5,4},{6,7},{7,6},{8,9},{9,8},{10,11... | collective-permute-start | bytes 2359304 | tf_op jit(solution)/shard_map/ppermute | solution.py:464
  44.5 37.9 %collective-permute-start.6 = (f32[2,2,264,256]{3,2,1,0:T(8,128)}, f32[2,2,264,256]{3,2,1,0:T(8,128)S(1)}, u32[]{:S(2)}, u32[]{:S(2)}) collective-permute-start(f32[2,2,264,256]{3,2,1,0:T(8,128)} %get-tuple-element.46.refs_0_), channel_id=1, source_target_pairs={{8,0},{16,8},{24,16},{32,24},{40,32},{48,40},{56,48},{64,56},{72,6... | collective-permute-start | bytes 3244040 | tf_op jit(solution)/shard_map/ppermute | solution.py:442
  45.8 36.6 %collective-permute-start.5 = (f32[2,2,264,256]{3,2,1,0:T(8,128)}, f32[2,2,264,256]{3,2,1,0:T(8,128)S(1)}, u32[]{:S(2)}, u32[]{:S(2)}) collective-permute-start(f32[2,2,264,256]{3,2,1,0:T(8,128)} %get-tuple-element.46.refs_0_), channel_id=1, source_target_pairs={{0,8},{8,16},{16,24},{24,32},{32,40},{40,48},{48,56},{56,64},{64,7... | collective-permute-start | bytes 3244040 | tf_op jit(solution)/shard_map/ppermute | solution.py:442
  49.9 0.9 copy-start.10
  71.6 17.8 %all-to-all-start.1 = ((f32[16,24,128]{2,1,0:T(8,128)}), f32[16,24,128]{2,1,0:T(8,128)S(1)}, u32[]{:S(2)}, u32[]{:S(2)}) async-start(f32[16,24,128]{2,1,0:T(8,128)} %bitcast.12), calls=%async_computation.1 | async-start | bytes 393216 | tf_op jit(solution)/shard_map/all_to_all | solution.py:472
  82.4 1.0 copy-start.2
  82.4 1.3 copy-start.3
  89.4 17.5 %copy-start.8 = (f32[16,24,128]{2,1,0:T(8,128)}, f32[16,24,128]{2,1,0:T(8,128)S(1)}, u32[]{:S(2)}) copy-start(f32[16,24,128]{2,1,0:T(8,128)S(1)} %all-to-all-done.1.parts) | copy-start | bytes 589828
  89.4 17.5 %collective-permute-start.7 = (f32[2,2,256,256]{3,2,1,0:T(8,128)}, f32[2,2,256,256]{3,2,1,0:T(8,128)S(1)}, u32[]{:S(2)}, u32[]{:S(2)}) collective-permute-start(f32[2,2,256,256]{3,2,1,0:T(8,128)} %get-tuple-element.53.block2), channel_id=1, source_target_pairs={{0,1},{1,2},{2,3},{3,4},{4,5},{5,6},{6,7},{8,9},{9,10},{10,11},{11... | collective-permute-start | bytes 3145736 | tf_op jit(solution)/shard_map/ppermute | solution.py:442
  94.9 23.6 %collective-permute-start.8 = (f32[2,2,256,256]{3,2,1,0:T(8,128)}, f32[2,2,256,256]{3,2,1,0:T(8,128)S(1)}, u32[]{:S(2)}, u32[]{:S(2)}) collective-permute-start(f32[2,2,256,256]{3,2,1,0:T(8,128)} %get-tuple-element.51.block0), channel_id=1, source_target_pairs={{1,0},{2,1},{3,2},{4,3},{5,4},{6,5},{7,6},{9,8},{10,9},{11,10},{12... | collective-permute-start | bytes 3145736 | tf_op jit(solution)/shard_map/ppermute | solution.py:442
  106.9 1.0 copy-start
  111.4 23.7 %all-to-all-start.2 = ((f32[64,32,128]{2,1,0:T(8,128)}), f32[64,32,128]{2,1,0:T(8,128)S(1)}, u32[]{:S(2)}, u32[]{:S(2)}) async-start(f32[64,32,128]{2,1,0:T(8,128)} %get-tuple-element.56), calls=%async_computation.2 | async-start | bytes 2097152 | tf_op jit(solution)/shard_map/all_to_all | solution.py:478
  118.5 1.0 copy-start.5
  135.1 5.3 %copy-start.6 = (f32[64,32,128]{2,1,0:T(8,128)}, f32[64,32,128]{2,1,0:T(8,128)S(1)}, u32[]{:S(2)}) copy-start(f32[64,32,128]{2,1,0:T(8,128)S(1)} %all-to-all-done.2.refs_2_) | copy-start | bytes 3145732
  135.1 5.3 %collective-permute-start.9 = (f32[64,32,128]{2,1,0:T(8,128)S(1)}, f32[64,32,128]{2,1,0:T(8,128)S(1)}, u32[]{:S(2)}, u32[]{:S(2)}) collective-permute-start(f32[64,32,128]{2,1,0:T(8,128)S(1)} %all-to-all-done.2.refs_2_), channel_id=1, source_target_pairs={{0,1},{1,0},{2,3},{3,2},{4,5},{5,4},{6,7},{7,6},{8,9},{9,8},{10,11... | collective-permute-start | bytes 3145736 | tf_op jit(solution)/shard_map/ppermute | solution.py:464
  140.5 1.0 copy-start.17
  154.4 2.9 %collective-permute-start.10 = (f32[6,256,128]{2,1,0:T(8,128)}, f32[6,256,128]{2,1,0:T(8,128)S(1)}, u32[]{:S(2)}, u32[]{:S(2)}) collective-permute-start(f32[6,256,128]{2,1,0:T(8,128)} %get-tuple-element.64), channel_id=1, source_target_pairs={{0,1},{1,0},{2,3},{3,2},{4,5},{5,4},{6,7},{7,6},{8,9},{9,8},{10,11... | collective-permute-start | bytes 2359304 | tf_op jit(solution)/shard_map/ppermute | solution.py:464
  154.8 28.2 %collective-permute-start.11 = (f32[2,2,264,256]{3,2,1,0:T(8,128)}, f32[2,2,264,256]{3,2,1,0:T(8,128)S(1)}, u32[]{:S(2)}, u32[]{:S(2)}) collective-permute-start(f32[2,2,264,256]{3,2,1,0:T(8,128)} %get-tuple-element.66.refs_0_), channel_id=1, source_target_pairs={{0,8},{8,16},{16,24},{24,32},{32,40},{40,48},{48,56},{56,64},{64,7... | collective-permute-start | bytes 3244040 | tf_op jit(solution)/shard_map/ppermute | solution.py:442
  157.3 0.9 copy-start.11
  178.5 11.4 %all-to-all-start.4 = ((f32[16,24,128]{2,1,0:T(8,128)}), f32[16,24,128]{2,1,0:T(8,128)S(1)}, u32[]{:S(2)}, u32[]{:S(2)}) async-start(f32[16,24,128]{2,1,0:T(8,128)} %bitcast.13), calls=%async_computation.4 | async-start | bytes 393216 | tf_op jit(solution)/shard_map/all_to_all | solution.py:472
  183.0 1.0 copy-start.4
  189.9 11.2 %copy-start.9 = (f32[16,24,128]{2,1,0:T(8,128)}, f32[16,24,128]{2,1,0:T(8,128)S(1)}, u32[]{:S(2)}) copy-start(f32[16,24,128]{2,1,0:T(8,128)S(1)} %all-to-all-done.4.parts) | copy-start | bytes 589828
  189.9 11.2 %collective-permute-start.12 = (f32[1,2,256,256]{3,2,1,0:T(8,128)}, f32[1,2,256,256]{3,2,1,0:T(8,128)S(1)}, u32[]{:S(2)}, u32[]{:S(2)}) collective-permute-start(f32[1,2,256,256]{3,2,1,0:T(8,128)} %get-tuple-element.73), channel_id=1, source_target_pairs={{0,1},{1,2},{2,3},{3,4},{4,5},{5,6},{6,7},{8,9},{9,10},{10,11},{11... | collective-permute-start | bytes 1572872 | tf_op jit(solution)/shard_map/ppermute | solution.py:442
  201.1 0.8 copy-start.16
  227.4 5.3 %copy-start.1 = (f32[64,32,128]{2,1,0:T(8,128)}, f32[64,32,128]{2,1,0:T(8,128)S(1)}, u32[]{:S(2)}) copy-start(f32[64,32,128]{2,1,0:T(8,128)S(1)} %all_to_all.32.refs_0_) | copy-start | bytes 3145732
  227.4 5.3 %collective-permute-start.13 = (f32[64,32,128]{2,1,0:T(8,128)S(1)}, f32[64,32,128]{2,1,0:T(8,128)S(1)}, u32[]{:S(2)}, u32[]{:S(2)}) collective-permute-start(f32[64,32,128]{2,1,0:T(8,128)S(1)} %all_to_all.32.refs_0_), channel_id=1, source_target_pairs={{0,1},{1,0},{2,3},{3,2},{4,5},{5,4},{6,7},{7,6},{8,9},{9,8},{10,11... | collective-permute-start | bytes 3145736 | tf_op jit(solution)/shard_map/ppermute | solution.py:464
  232.7 1.0 copy-start.7

commit v4 on v3

--- a/solution.py
+++ b/solution.py
@@ -274,14 +274,14 @@
         mid_copy.wait()
 
 
-def call(kernel, args, out_shape, n_smem):
+def call(kernel, args, out_shape, n_smem, limit=60):
     size = sum(math.prod(a.shape) * a.dtype.itemsize for a in (*args, *out_shape))
     return pl.pallas_call(
         kernel,
         out_shape=tuple(out_shape),
         in_specs=[SMEM] * n_smem + [VMEM] * (len(args) - n_smem),
         out_specs=tuple([VMEM] * len(out_shape)),
-        compiler_params=pltpu.CompilerParams(vmem_limit_bytes=60 * MEGA),
+        compiler_params=pltpu.CompilerParams(vmem_limit_bytes=limit * MEGA),
         cost_estimate=pl.CostEstimate(flops=10_000_000, bytes_accessed=size, transcendentals=0),
     )(*args)
 
@@ -311,7 +311,7 @@
             pltpu.SemaphoreType.DMA((1,)),
             *[pltpu.VMEM(value.shape, value.dtype) for value in big],
         ],
-        compiler_params=pltpu.CompilerParams(vmem_limit_bytes=60 * MEGA),
+        compiler_params=pltpu.CompilerParams(vmem_limit_bytes=(60 if iteration else 48) * MEGA),
         cost_estimate=pl.CostEstimate(flops=8_000_000_000, bytes_accessed=12_000_000, transcendentals=0),
     )(corners, counts, *big)
 
@@ -431,7 +431,7 @@
             pltpu.SemaphoreType.DMA((2,)),
             pltpu.SemaphoreType.DMA((2 * MODES,)),
         ],
-        compiler_params=pltpu.CompilerParams(vmem_limit_bytes=60 * MEGA),
+        compiler_params=pltpu.CompilerParams(vmem_limit_bytes=48 * MEGA),
         cost_estimate=pl.CostEstimate(flops=10_000_000, bytes_accessed=9_000_000, transcendentals=0),
     )(rate_first, *data)
 
@@ -456,7 +456,8 @@
     first_cols = object_field[:, :, :WIN]
     below0 = shift(first_cols, "row", -1)
     rim = shift(first_cols, COL, -1)
-    below1 = shift(object_field[:, :, WIN:], "row", -1)
+    first_cols, again = lax.optimization_barrier((first_cols, object_field))
+    below1 = shift(again[:, :, WIN:], "row", -1)
     diag = shift(below0, COL, -1)
     rims = (below0, below1, rim, diag)
 
@@ -464,9 +465,9 @@
         return lax.ppermute(value, "core", [(0, 1), (1, 0)])
 
     def reduce_chips(keep, send):
-        (value,) = call(add_kernel, [keep, swap(send)], [f32(*keep.shape)], 0)
+        (value,) = call(add_kernel, [keep, swap(send)], [f32(*keep.shape)], 0, 48)
         parts = lax.all_to_all(value.reshape(layers, rows * CHUNK, HALF), "layer", 0, 0, tiled=True)
-        return call(sum_kernel, [parts], [f32(rows * CHUNK, HALF), f32(8, HALF)], 0)
+        return call(sum_kernel, [parts], [f32(rows * CHUNK, HALF), f32(8, HALF)], 0, 48)
 
     def reduce_rows(part):
         return lax.all_to_all(part.reshape(rows, CHUNK, HALF), "row", 0, 0, tiled=True)
@@ -474,13 +475,13 @@
     def finish_tile(sums, from_left, chunk, loss, loss_before):
         outs = [f32(2, WIN, 2 * WIN), f32(layers * rows, SENT, HALF), f32(1, 2)]
         args = [sums[0], sums[1], from_left, chunk, loss, loss_before]
-        tile, sent, losses = call(tile_kernel, args, outs, 0)
+        tile, sent, losses = call(tile_kernel, args, outs, 0, 48)
         return tile, lax.all_to_all(sent, CHIPS, 0, 0, tiled=True), losses
 
     def fold(*windows, token):
         both = len(windows) == 3
         strip = f32(1 + both, 2, WIN, WIN)
-        return call(lambda *refs: fold_kernel(both, *refs), [*windows, token], [strip] * 3, 0)
+        return call(lambda *refs: fold_kernel(both, *refs), [*windows, token], [strip] * 3, 0, 48)
 
     grads, keep, send, loss_first = window_call(
         0, corners, counts, [object_field, *rims, tables[0], probe], amplitude, tables

time: 240 us -> 227 us (0.946)
  Pallas kernels: 61.4 us -> 44.8 us
  waiting for transfers between devices: 50.5 us -> 54.6 us
  starting transfers between devices: 59.5 us -> 62.8 us
  blocking collectives: 55.4 us -> 52.9 us
    pallas_call x9, Pallas kernels: 30.5 us -> 14.4 us  [call(): pl.pallas_call(kernel, out_shape=tuple(out_shape), in_specs=[SMEM] * n_sm...]
    all_to_all x1, starting transfers between devices: 7.11 us -> 10.9 us  [finish_tile(): return (tile, lax.all_to_all(sent, CHIPS, 0, 0, tiled=True), losses)]
    ppermute x10, waiting for transfers between devices: 34.3 us -> 36.8 us  [shift(): lax.ppermute(value, axis, [(source, source + steps) for source in range(f...]
    unnamed x36 -> x54, local copies, waits for them, and re-layouts: 9.56 us -> 8.36 us
  transfers between devices with their start and end apart: 17 -> 17, of which waited for: 10 -> 11; matrix products, arithmetic and copies ran while one was open for 0% -> 0% of each run, Pallas kernels for 12% -> 6%
where the time goes in v4:
time: 227 us; the launch traced here: 226 us
  starting transfers between devices  62.8 us (28%)
  waiting for transfers between devices  54.6 us (24%)
  blocking collectives  52.9 us (23%)
  Pallas kernels  44.8 us (20%)
  local copies, waits for them, and re-layouts  9.6 us (4%)
    ppermute x10, waiting for transfers between devices, shift(): lax.ppermute(value, axis, [(source, source + steps) for source in range(f...  36.8 us
    all_to_all x2, blocking collectives, reduce_chips(): lax.all_to_all(value.reshape(layers, rows * CHUNK, HALF), 'layer', 0, 0,...  30.6 us
    ppermute x10, starting transfers between devices, shift(): lax.ppermute(value, axis, [(source, source + steps) for source in range(f...  30 us
    pallas_call x2, Pallas kernels, window_call(): pl.pallas_call(lambda *refs: window_kernel(iteration, *refs), out_shape=(...  27.1 us
    all_to_all x1, blocking collectives, finish_tile(): return (tile, lax.all_to_all(sent, CHIPS, 0, 0, tiled=True), losses)  22.4 us
    all_to_all x2, starting transfers between devices, reduce_rows(): lax.all_to_all(part.reshape(rows, CHUNK, HALF), 'row', 0, 0, tiled=True)  15.3 us
    pallas_call x9, Pallas kernels, call(): pl.pallas_call(kernel, out_shape=tuple(out_shape), in_specs=[SMEM] * n_sm...  14.4 us
    all_to_all x1, starting transfers between devices, finish_tile(): return (tile, lax.all_to_all(sent, CHIPS, 0, 0, tiled=True), losses)  10.9 us
  transfers between devices with their start and end apart: 17, of which 11 were waited for; matrix products, arithmetic and copies ran while one was open for 0% of the time, Pallas kernels for 6%

profile of v4, /device:TPU:1, one launch (start us, length us, event | category | flops | bytes accessed | tf_op | source)
XLA Modules:
  0.0 225.9 jit_solution(1378023117258443331)
XLA Ops:
  0.6 0.0 copy-start
  0.6 0.0 copy-start.24
  0.7 0.0 copy-start.21
  0.7 0.0 copy-start.23
  0.7 0.0 copy-start.20
  0.7 1.2 slice.6
  1.9 1.3 collective-permute-start
  3.2 3.3 %collective-permute-start.2 = (f32[2,256,256]{2,1,0:T(8,128)S(1)}, f32[2,256,256]{2,1,0:T(8,128)S(1)}, u32[]{:S(2)}, u32[]{:S(2)}) collective-permute-start(f32[2,256,256]{2,1,0:T(8,128)S(1)} %slice.6), channel_id=1, source_target_pairs={{1,0},{2,1},{3,2},{4,3},{5,4},{6,5},{7,6},{9,8},{10,9},{11,10},{12... | collective-permute-start | bytes 1572872 | tf_op jit(solution)/shard_map/ppermute | solution.py:442
  6.6 1.3 collective-permute-start.1
  7.9 9.3 %collective-permute-done.refs_3_.below0 = f32[2,256,256]{2,1,0:T(8,128)S(1)} collective-permute-done((f32[2,256,256]{2,1,0:T(8,128)S(1)}, f32[2,256,256]{2,1,0:T(8,128)S(1)}, u32[]{:S(2)}, u32[]{:S(2)}) %collective-permute-start) | collective-permute-done | bytes 524320 | tf_op jit(solution)/shard_map/ppermute | solution.py:442
  17.2 4.8 %collective-permute-start.3 = (f32[2,256,256]{2,1,0:T(8,128)S(1)}, f32[2,256,256]{2,1,0:T(8,128)S(1)}, u32[]{:S(2)}, u32[]{:S(2)}) collective-permute-start(f32[2,256,256]{2,1,0:T(8,128)S(1)} %collective-permute-done.refs_3_.below0), channel_id=1, source_target_pairs={{1,0},{2,1},{3,2},{4,3},{5,4},{6,5},{7,6},{9,8},{10,9},{11,10},{12... | collective-permute-start | bytes 1572872 | tf_op jit(solution)/shard_map/ppermute | solution.py:442
  21.9 6.5 %collective-permute-done.1.refs_4_.below1 = f32[2,256,256]{2,1,0:T(8,128)S(1)} collective-permute-done((f32[2,256,256]{2,1,0:T(8,128)S(1)}, f32[2,256,256]{2,1,0:T(8,128)S(1)}, u32[]{:S(2)}, u32[]{:S(2)}) %collective-permute-start.1) | collective-permute-done | bytes 524320 | tf_op jit(solution)/shard_map/ppermute | solution.py:442
  28.4 0.0 collective-permute-done.2.refs_5_.rim
  28.4 2.0 collective-permute-done.3.refs_6_.diag
  30.4 14.2 %shard_map.94 = (f32[2,2,264,256]{3,2,1,0:T(8,128)}, f32[6,256,128]{2,1,0:T(8,128)S(1)}, f32[6,256,128]{2,1,0:T(8,128)S(1)}, f32[8,128]{1,0:T(8,128)S(1)}) custom-call(s32[2,2,2]{2,1,0:T(2,128)S(1)} %bitcast.14, s32[2]{0:T(128)S(1)} %bitcast.18, f32[2,256,512]{2,1,0:T(8,128)S(1)} %copy-done, f32[2,256,256]{2,1,0:T(8,128)S(1)} %collective-permute-done.refs_3_.below0, ...), custom_call_target="tpu_custom_call" | custom-call | flops 8000000000 | bytes 12000000 | tf_op jit(solution)/shard_map/pallas_call | solution.py:296
  44.6 0.1 collective-permute-start.4
  44.7 1.3 collective-permute-start.6
  46.0 4.1 %collective-permute-start.5 = (f32[2,2,264,256]{3,2,1,0:T(8,128)}, f32[2,2,264,256]{3,2,1,0:T(8,128)S(1)}, u32[]{:S(2)}, u32[]{:S(2)}) collective-permute-start(f32[2,2,264,256]{3,2,1,0:T(8,128)} %get-tuple-element.48.refs_0_), channel_id=1, source_target_pairs={{0,8},{8,16},{16,24},{24,32},{32,40},{40,48},{48,56},{56,64},{64,7... | collective-permute-start | bytes 3244040 | tf_op jit(solution)/shard_map/ppermute | solution.py:442
  50.1 0.1 shard_map.95
  50.2 0.0 copy-start.5
  50.2 16.0 %all_to_all.30.parts = f32[4,384,128]{2,1,0:T(8,128)S(1)} all-to-all(f32[4,384,128]{2,1,0:T(8,128)S(1)} %bitcast.10), channel_id=1, replica_groups=mesh['row'=16,'layer'=4,'core'=2] {'layer'}, dimensions={0} | all-to-all | bytes 1572864 | tf_op jit(solution)/shard_map/all_to_all | solution.py:469
  66.3 0.7 shard_map.96
  67.0 10.8 %all-to-all-start.1 = ((f32[16,24,128]{2,1,0:T(8,128)}), f32[16,24,128]{2,1,0:T(8,128)S(1)}, u32[]{:S(2)}, u32[]{:S(2)}) async-start(f32[16,24,128]{2,1,0:T(8,128)} %bitcast.5), calls=%async_computation.1 | async-start | bytes 393216 | tf_op jit(solution)/shard_map/all_to_all | solution.py:473
  77.9 0.0 collective-permute-done.5.refs_1_
  77.9 1.0 copy-done.6
  78.9 1.2 copy-done.7
  80.1 2.8 %shard_map.97 = (f32[2,2,256,256]{3,2,1,0:T(8,128)S(1)}, f32[2,2,256,256]{3,2,1,0:T(8,128)S(1)}, f32[2,2,256,256]{3,2,1,0:T(8,128)S(1)}) custom-call(f32[2,2,264,256]{3,2,1,0:T(8,128)S(1)} %copy-done.5, f32[2,2,264,256]{3,2,1,0:T(8,128)S(1)} %copy-done.7, f32[2,2,264,256]{3,2,1,0:T(8,128)} %collective-permute-done.6.refs_2_, ...), custom_call_target="tpu_custom_call" | custom-call | flops 10000000 | bytes 6393856 | tf_op jit(solution)/shard_map/pallas_call | solution.py:279
  82.9 0.0 copy-start.9
  82.9 1.0 copy-done.9
  83.9 1.0 all-to-all-done.1.parts
  84.9 5.2 %collective-permute-start.7 = (f32[2,2,256,256]{3,2,1,0:T(8,128)}, f32[2,2,256,256]{3,2,1,0:T(8,128)S(1)}, u32[]{:S(2)}, u32[]{:S(2)}) collective-permute-start(f32[2,2,256,256]{3,2,1,0:T(8,128)} %copy-done.9), channel_id=1, source_target_pairs={{0,1},{1,2},{2,3},{3,4},{4,5},{5,6},{6,7},{8,9},{9,10},{10,11},{11... | collective-permute-start | bytes 3145736 | tf_op jit(solution)/shard_map/ppermute | solution.py:442
  90.2 1.9 collective-permute-start.8
  92.1 10.1 %collective-permute-done.7.from_left.left = f32[2,2,256,256]{3,2,1,0:T(8,128)S(1)} collective-permute-done((f32[2,2,256,256]{3,2,1,0:T(8,128)}, f32[2,2,256,256]{3,2,1,0:T(8,128)S(1)}, u32[]{:S(2)}, u32[]{:S(2)}) %collective-permute-start.7) | collective-permute-done | bytes 1048608 | tf_op jit(solution)/shard_map/ppermute | solution.py:442
  102.2 0.9 shard_map.98
  103.1 0.2 copy-done.4
  103.2 1.0 copy-done.10
  104.2 1.0 copy-done.11
  105.2 10.9 %all-to-all-start.2 = ((f32[64,32,128]{2,1,0:T(8,128)}), f32[64,32,128]{2,1,0:T(8,128)S(1)}, u32[]{:S(2)}, u32[]{:S(2)}) async-start(f32[64,32,128]{2,1,0:T(8,128)} %copy-done.10), calls=%async_computation.2 | async-start | bytes 2097152 | tf_op jit(solution)/shard_map/all_to_all | solution.py:479
  116.1 7.6 %shard_map.99 = (f32[2,2,256,256]{3,2,1,0:T(8,128)}, f32[2,2,256,256]{3,2,1,0:T(8,128)}) custom-call(s32[2,2,2]{2,1,0:T(2,128)} %bitcast.12, f32[2,256,512]{2,1,0:T(8,128)} %refs_3_.1, f32[2,256,256]{2,1,0:T(8,128)} %copy-done.14, f32[2,256,256]{2,1,0:T(8,128)} %copy-done.16, f32[2,256,256]{2,1,0:T(8,128)} %copy-done.15, f32[2,256,256]{2,1,0:T(8,128)} %copy-done.17, ...), custom_call_target="tpu_custom_call" | custom-call | flops 10000000 | bytes 10485792 | tf_op jit(solution)/shard_map/pallas_call | solution.py:279
  123.7 9.0 %all-to-all-done.2.refs_2_ = f32[64,32,128]{2,1,0:T(8,128)S(1)} async-done(((f32[64,32,128]{2,1,0:T(8,128)}), f32[64,32,128]{2,1,0:T(8,128)S(1)}, u32[]{:S(2)}, u32[]{:S(2)}) %all-to-all-start.2) | async-done | bytes 1048608 | tf_op jit(solution)/shard_map/all_to_all | solution.py:479
  132.7 3.0 %collective-permute-start.9 = (f32[64,32,128]{2,1,0:T(8,128)S(1)}, f32[64,32,128]{2,1,0:T(8,128)S(1)}, u32[]{:S(2)}, u32[]{:S(2)}) collective-permute-start(f32[64,32,128]{2,1,0:T(8,128)S(1)} %all-to-all-done.2.refs_2_), channel_id=1, source_target_pairs={{0,1},{1,0},{2,3},{3,2},{4,5},{5,4},{6,7},{7,6},{8,9},{9,8},{10,11... | collective-permute-start | bytes 3145736 | tf_op jit(solution)/shard_map/ppermute | solution.py:465
  135.8 2.3 %collective-permute-done.9.refs_3_ = f32[64,32,128]{2,1,0:T(8,128)S(1)} collective-permute-done((f32[64,32,128]{2,1,0:T(8,128)S(1)}, f32[64,32,128]{2,1,0:T(8,128)S(1)}, u32[]{:S(2)}, u32[]{:S(2)}) %collective-permute-start.9) | collective-permute-done | bytes 1048608 | tf_op jit(solution)/shard_map/ppermute | solution.py:465
  138.1 1.0 copy-done.26
  139.1 12.9 %shard_map.100 = (f32[2,2,264,256]{3,2,1,0:T(8,128)}, f32[6,256,128]{2,1,0:T(8,128)}, f32[6,256,128]{2,1,0:T(8,128)}, f32[6,256,256]{2,1,0:T(8,128)}, f32[8,128]{1,0:T(8,128)}, /*index=5*/f32[8,128]{1,0:T(8,128)}) custom-call(s32[2,2,2]{2,1,0:T(2,128)} %bitcast.13, s32[2]{0:T(128)} %bitcast.17, f32[64,32,128]{2,1,0:T(8,128)} %copy-done.25, ...), custom_call_target="tpu_custom_call" | custom-call | flops 8000000000 | bytes 12000000 | tf_op jit(solution)/shard_map/pallas_call | solution.py:296
  152.0 0.5 collective-permute-start.10
  152.5 2.4 %collective-permute-start.11 = (f32[2,2,264,256]{3,2,1,0:T(8,128)}, f32[2,2,264,256]{3,2,1,0:T(8,128)S(1)}, u32[]{:S(2)}, u32[]{:S(2)}) collective-permute-start(f32[2,2,264,256]{3,2,1,0:T(8,128)} %get-tuple-element.68.refs_0_), channel_id=1, source_target_pairs={{0,8},{8,16},{16,24},{24,32},{32,40},{40,48},{48,56},{56,64},{64,7... | collective-permute-start | bytes 3244040 | tf_op jit(solution)/shard_map/ppermute | solution.py:442
  154.9 1.1 copy-done.13
  156.0 0.1 shard_map.101
  156.1 0.0 copy-start.8
  156.1 14.5 %all_to_all.31.parts = f32[4,384,128]{2,1,0:T(8,128)S(1)} all-to-all(f32[4,384,128]{2,1,0:T(8,128)S(1)} %bitcast.11), channel_id=1, replica_groups=mesh['row'=16,'layer'=4,'core'=2] {'layer'}, dimensions={0} | all-to-all | bytes 1572864 | tf_op jit(solution)/shard_map/all_to_all | solution.py:469
  170.6 0.7 shard_map.102
  171.3 4.4 %all-to-all-start.4 = ((f32[16,24,128]{2,1,0:T(8,128)}), f32[16,24,128]{2,1,0:T(8,128)S(1)}, u32[]{:S(2)}, u32[]{:S(2)}) async-start(f32[16,24,128]{2,1,0:T(8,128)} %bitcast.7), calls=%async_computation.4 | async-start | bytes 393216 | tf_op jit(solution)/shard_map/all_to_all | solution.py:473
  175.8 2.5 %collective-permute-done.11.refs_1_ = f32[2,2,264,256]{3,2,1,0:T(8,128)S(1)} collective-permute-done((f32[2,2,264,256]{3,2,1,0:T(8,128)}, f32[2,2,264,256]{3,2,1,0:T(8,128)S(1)}, u32[]{:S(2)}, u32[]{:S(2)}) %collective-permute-start.11) | collective-permute-done | bytes 1081376 | tf_op jit(solution)/shard_map/ppermute | solution.py:442
  178.3 0.8 shard_map.103
  179.1 0.0 copy-start.22
  179.1 0.8 copy-done.22
  179.9 3.2 %all-to-all-done.4.parts = f32[16,24,128]{2,1,0:T(8,128)S(1)} async-done(((f32[16,24,128]{2,1,0:T(8,128)}), f32[16,24,128]{2,1,0:T(8,128)S(1)}, u32[]{:S(2)}, u32[]{:S(2)}) %all-to-all-start.4) | async-done | bytes 196640 | tf_op jit(solution)/shard_map/all_to_all | solution.py:473
  183.1 4.4 %collective-permute-start.12 = (f32[1,2,256,256]{3,2,1,0:T(8,128)}, f32[1,2,256,256]{3,2,1,0:T(8,128)S(1)}, u32[]{:S(2)}, u32[]{:S(2)}) collective-permute-start(f32[1,2,256,256]{3,2,1,0:T(8,128)} %copy-done.22), channel_id=1, source_target_pairs={{0,1},{1,2},{2,3},{3,4},{4,5},{5,6},{6,7},{8,9},{9,10},{10,11},{11... | collective-permute-start | bytes 1572872 | tf_op jit(solution)/shard_map/ppermute | solution.py:442
  187.5 6.4 %collective-permute-done.12.from_left = f32[1,2,256,256]{3,2,1,0:T(8,128)S(1)} collective-permute-done((f32[1,2,256,256]{3,2,1,0:T(8,128)}, f32[1,2,256,256]{3,2,1,0:T(8,128)S(1)}, u32[]{:S(2)}, u32[]{:S(2)}) %collective-permute-start.12) | collective-permute-done | bytes 524320 | tf_op jit(solution)/shard_map/ppermute | solution.py:442
  193.9 0.8 shard_map.104
  194.7 22.4 %all_to_all.32.refs_0_ = f32[64,32,128]{2,1,0:T(8,128)S(1)} all-to-all(f32[64,32,128]{2,1,0:T(8,128)S(1)} %get-tuple-element.78), channel_id=1, replica_groups=mesh['row'=16,'layer'=4,'core'=2] {'layer','row'}, dimensions={0} | all-to-all | bytes 2097152 | tf_op jit(solution)/shard_map/all_to_all | solution.py:479
  217.1 3.0 %collective-permute-start.13 = (f32[64,32,128]{2,1,0:T(8,128)S(1)}, f32[64,32,128]{2,1,0:T(8,128)S(1)}, u32[]{:S(2)}, u32[]{:S(2)}) collective-permute-start(f32[64,32,128]{2,1,0:T(8,128)S(1)} %all_to_all.32.refs_0_), channel_id=1, source_target_pairs={{0,1},{1,0},{2,3},{3,2},{4,5},{5,4},{6,7},{7,6},{8,9},{9,8},{10,11... | collective-permute-start | bytes 3145736 | tf_op jit(solution)/shard_map/ppermute | solution.py:465
  220.2 2.3 %collective-permute-done.13.refs_1_ = f32[64,32,128]{2,1,0:T(8,128)S(1)} collective-permute-done((f32[64,32,128]{2,1,0:T(8,128)S(1)}, f32[64,32,128]{2,1,0:T(8,128)S(1)}, u32[]{:S(2)}, u32[]{:S(2)}) %collective-permute-start.13) | collective-permute-done | bytes 1048608 | tf_op jit(solution)/shard_map/ppermute | solution.py:465
  222.4 3.3 %shard_map.105 = (f32[2,256,512]{2,1,0:T(8,128)}, f32[6,256,256]{2,1,0:T(8,128)}) custom-call(f32[8,128]{1,0:T(8,128)S(1)} %copy-done.18, f32[64,32,128]{2,1,0:T(8,128)S(1)} %all_to_all.32.refs_0_, f32[64,32,128]{2,1,0:T(8,128)S(1)} %collective-permute-done.13.refs_1_, f32[6,256,256]{2,1,0:T(8,128)} %get-tuple-element.79.refs_2_, ...), custom_call_target="tpu_custom_call" | custom-call | flops 10000000 | bytes 9000000 | tf_op jit(solution)/shard_map/pallas_call | solution.py:423
  (41 shorter events, 0.1 us)
Async XLA Ops:
  0.6 5.9 %copy-start = (f32[2,256,512]{2,1,0:T(8,128)S(1)}, f32[2,256,512]{2,1,0:T(8,128)}, u32[]{:S(2)}) copy-start(f32[2,256,512]{2,1,0:T(8,128)} %refs_3_.1) | copy-start | bytes 3145732
  0.6 29.7 %copy-start.24 = (bf16[2,256,256]{2,1,0:T(8,128)(2,1)S(1)}, bf16[2,256,256]{2,1,0:T(8,128)(2,1)}, u32[]{:S(2)}) copy-start(bf16[2,256,256]{2,1,0:T(8,128)(2,1)} %constant.5.clone.refs_10_.refs_9_) | copy-start | bytes 786436
  0.7 29.7 %copy-start.21 = (bf16[2,1,1,2,256,256]{5,4,3,2,1,0:T(8,128)(2,1)S(1)}, bf16[2,1,1,2,256,256]{5,4,3,2,1,0:T(8,128)(2,1)}, u32[]{:S(2)}) copy-start(bf16[2,1,1,2,256,256]{5,4,3,2,1,0:T(8,128)(2,1)} %param.11) | copy-start | bytes 1572868
  0.7 29.7 %copy-start.23 = (s32[2,1,1]{0,2,1:T(1,128)S(1)}, s32[2,1,1]{0,2,1:T(1,128)}, u32[]{:S(2)}) copy-start(s32[2,1,1]{0,2,1:T(1,128)} %param.10) | copy-start | bytes 28
  0.7 29.7 %copy-start.20 = (s32[2,1,1,2,2]{4,3,2,1,0:T(2,128)S(1)}, s32[2,1,1,2,2]{4,3,2,1,0:T(2,128)}, u32[]{:S(2)}) copy-start(s32[2,1,1,2,2]{4,3,2,1,0:T(2,128)} %param.9) | copy-start | bytes 100
  1.9 15.3 %collective-permute-start = (f32[2,256,256]{2,1,0:T(8,128)S(1)}, f32[2,256,256]{2,1,0:T(8,128)S(1)}, u32[]{:S(2)}, u32[]{:S(2)}) collective-permute-start(f32[2,256,256]{2,1,0:T(8,128)S(1)} %slice.6), channel_id=1, source_target_pairs={{8,0},{16,8},{24,16},{32,24},{40,32},{48,40},{56,48},{64,56},{72,6... | collective-permute-start | bytes 1572872 | tf_op jit(solution)/shard_map/ppermute | solution.py:442
  3.2 25.2 %collective-permute-start.2 = (f32[2,256,256]{2,1,0:T(8,128)S(1)}, f32[2,256,256]{2,1,0:T(8,128)S(1)}, u32[]{:S(2)}, u32[]{:S(2)}) collective-permute-start(f32[2,256,256]{2,1,0:T(8,128)S(1)} %slice.6), channel_id=1, source_target_pairs={{1,0},{2,1},{3,2},{4,3},{5,4},{6,5},{7,6},{9,8},{10,9},{11,10},{12... | collective-permute-start | bytes 1572872 | tf_op jit(solution)/shard_map/ppermute | solution.py:442
  6.6 21.8 %collective-permute-start.1 = (f32[2,256,256]{2,1,0:T(8,128)S(1)}, f32[2,256,256]{2,1,0:T(8,128)S(1)}, u32[]{:S(2)}, u32[]{:S(2)}) collective-permute-start(f32[2,256,256]{2,1,0:T(8,128)S(1)} %slice.7), channel_id=1, source_target_pairs={{8,0},{16,8},{24,16},{32,24},{40,32},{48,40},{56,48},{64,56},{72,6... | collective-permute-start | bytes 1572872 | tf_op jit(solution)/shard_map/ppermute | solution.py:442
  17.2 27.4 %copy-start.14 = (f32[2,256,256]{2,1,0:T(8,128)}, f32[2,256,256]{2,1,0:T(8,128)S(1)}, u32[]{:S(2)}) copy-start(f32[2,256,256]{2,1,0:T(8,128)S(1)} %collective-permute-done.refs_3_.below0) | copy-start | bytes 1572868
  17.2 13.2 %collective-permute-start.3 = (f32[2,256,256]{2,1,0:T(8,128)S(1)}, f32[2,256,256]{2,1,0:T(8,128)S(1)}, u32[]{:S(2)}, u32[]{:S(2)}) collective-permute-start(f32[2,256,256]{2,1,0:T(8,128)S(1)} %collective-permute-done.refs_3_.below0), channel_id=1, source_target_pairs={{1,0},{2,1},{3,2},{4,3},{5,4},{6,5},{7,6},{9,8},{10,9},{11,10},{12... | collective-permute-start | bytes 1572872 | tf_op jit(solution)/shard_map/ppermute | solution.py:442
  28.4 16.2 %copy-start.16 = (f32[2,256,256]{2,1,0:T(8,128)}, f32[2,256,256]{2,1,0:T(8,128)S(1)}, u32[]{:S(2)}) copy-start(f32[2,256,256]{2,1,0:T(8,128)S(1)} %collective-permute-done.1.refs_4_.below1) | copy-start | bytes 1572868
  28.4 16.2 %copy-start.15 = (f32[2,256,256]{2,1,0:T(8,128)}, f32[2,256,256]{2,1,0:T(8,128)S(1)}, u32[]{:S(2)}) copy-start(f32[2,256,256]{2,1,0:T(8,128)S(1)} %collective-permute-done.2.refs_5_.rim) | copy-start | bytes 1572868
  30.4 14.3 %copy-start.17 = (f32[2,256,256]{2,1,0:T(8,128)}, f32[2,256,256]{2,1,0:T(8,128)S(1)}, u32[]{:S(2)}) copy-start(f32[2,256,256]{2,1,0:T(8,128)S(1)} %collective-permute-done.3.refs_6_.diag) | copy-start | bytes 1572868
  44.6 5.5 %collective-permute-start.4 = (f32[6,256,128]{2,1,0:T(8,128)S(1)}, f32[6,256,128]{2,1,0:T(8,128)S(1)}, u32[]{:S(2)}, u32[]{:S(2)}) collective-permute-start(f32[6,256,128]{2,1,0:T(8,128)S(1)} %get-tuple-element.46), channel_id=1, source_target_pairs={{0,1},{1,0},{2,3},{3,2},{4,5},{5,4},{6,7},{7,6},{8,9},{9,8},{10,11... | collective-permute-start | bytes 2359304 | tf_op jit(solution)/shard_map/ppermute | solution.py:465
  44.7 33.1 %collective-permute-start.6 = (f32[2,2,264,256]{3,2,1,0:T(8,128)}, f32[2,2,264,256]{3,2,1,0:T(8,128)}, u32[]{:S(2)}, u32[]{:S(2)}) collective-permute-start(f32[2,2,264,256]{3,2,1,0:T(8,128)} %get-tuple-element.48.refs_0_), channel_id=1, source_target_pairs={{8,0},{16,8},{24,16},{32,24},{40,32},{48,40},{56,48},{64,56},{72,6... | collective-permute-start | bytes 3244040 | tf_op jit(solution)/shard_map/ppermute | solution.py:442
  46.0 31.8 %collective-permute-start.5 = (f32[2,2,264,256]{3,2,1,0:T(8,128)}, f32[2,2,264,256]{3,2,1,0:T(8,128)S(1)}, u32[]{:S(2)}, u32[]{:S(2)}) collective-permute-start(f32[2,2,264,256]{3,2,1,0:T(8,128)} %get-tuple-element.48.refs_0_), channel_id=1, source_target_pairs={{0,8},{8,16},{16,24},{24,32},{32,40},{40,48},{48,56},{56,64},{64,7... | collective-permute-start | bytes 3244040 | tf_op jit(solution)/shard_map/ppermute | solution.py:442
  50.2 28.7 %copy-start.5 = (f32[2,2,264,256]{3,2,1,0:T(8,128)S(1)}, f32[2,2,264,256]{3,2,1,0:T(8,128)}, u32[]{:S(2)}) copy-start(f32[2,2,264,256]{3,2,1,0:T(8,128)} %get-tuple-element.48.refs_0_) | copy-start | bytes 3244036
  67.0 17.9 %all-to-all-start.1 = ((f32[16,24,128]{2,1,0:T(8,128)}), f32[16,24,128]{2,1,0:T(8,128)S(1)}, u32[]{:S(2)}, u32[]{:S(2)}) async-start(f32[16,24,128]{2,1,0:T(8,128)} %bitcast.5), calls=%async_computation.1 | async-start | bytes 393216 | tf_op jit(solution)/shard_map/all_to_all | solution.py:473
  77.9 1.0 copy-start.6
  78.9 1.2 copy-start.7
  82.9 1.0 copy-start.9
  83.9 19.2 %copy-start.2 = (f32[2,2,256,256]{3,2,1,0:T(8,128)}, f32[2,2,256,256]{3,2,1,0:T(8,128)S(1)}, u32[]{:S(2)}) copy-start(f32[2,2,256,256]{3,2,1,0:T(8,128)S(1)} %get-tuple-element.53.block0) | copy-start | bytes 3145732
  83.9 19.2 %copy-start.3 = (f32[2,2,256,256]{3,2,1,0:T(8,128)}, f32[2,2,256,256]{3,2,1,0:T(8,128)S(1)}, u32[]{:S(2)}) copy-start(f32[2,2,256,256]{3,2,1,0:T(8,128)S(1)} %get-tuple-element.54.block1) | copy-start | bytes 3145732
  84.9 17.3 %collective-permute-start.7 = (f32[2,2,256,256]{3,2,1,0:T(8,128)}, f32[2,2,256,256]{3,2,1,0:T(8,128)S(1)}, u32[]{:S(2)}, u32[]{:S(2)}) collective-permute-start(f32[2,2,256,256]{3,2,1,0:T(8,128)} %copy-done.9), channel_id=1, source_target_pairs={{0,1},{1,2},{2,3},{3,4},{4,5},{5,6},{6,7},{8,9},{9,10},{10,11},{11... | collective-permute-start | bytes 3145736 | tf_op jit(solution)/shard_map/ppermute | solution.py:442
  90.2 26.0 %collective-permute-start.8 = (f32[2,2,256,256]{3,2,1,0:T(8,128)S(1)}, f32[2,2,256,256]{3,2,1,0:T(8,128)}, u32[]{:S(2)}, u32[]{:S(2)}) collective-permute-start(f32[2,2,256,256]{3,2,1,0:T(8,128)S(1)} %get-tuple-element.53.block0), channel_id=1, source_target_pairs={{1,0},{2,1},{3,2},{4,3},{5,4},{6,5},{7,6},{9,8},{10,9},{11,10},{12... | collective-permute-start | bytes 3145736 | tf_op jit(solution)/shard_map/ppermute | solution.py:442
  102.2 1.1 copy-start.4
  103.2 1.0 copy-start.10
  104.2 1.0 copy-start.11
  105.2 27.5 %all-to-all-start.2 = ((f32[64,32,128]{2,1,0:T(8,128)}), f32[64,32,128]{2,1,0:T(8,128)S(1)}, u32[]{:S(2)}, u32[]{:S(2)}) async-start(f32[64,32,128]{2,1,0:T(8,128)} %copy-done.10), calls=%async_computation.2 | async-start | bytes 2097152 | tf_op jit(solution)/shard_map/all_to_all | solution.py:479
  132.7 5.3 %copy-start.25 = (f32[64,32,128]{2,1,0:T(8,128)}, f32[64,32,128]{2,1,0:T(8,128)S(1)}, u32[]{:S(2)}) copy-start(f32[64,32,128]{2,1,0:T(8,128)S(1)} %all-to-all-done.2.refs_2_) | copy-start | bytes 3145732
  132.7 5.3 %collective-permute-start.9 = (f32[64,32,128]{2,1,0:T(8,128)S(1)}, f32[64,32,128]{2,1,0:T(8,128)S(1)}, u32[]{:S(2)}, u32[]{:S(2)}) collective-permute-start(f32[64,32,128]{2,1,0:T(8,128)S(1)} %all-to-all-done.2.refs_2_), channel_id=1, source_target_pairs={{0,1},{1,0},{2,3},{3,2},{4,5},{5,4},{6,7},{7,6},{8,9},{9,8},{10,11... | collective-permute-start | bytes 3145736 | tf_op jit(solution)/shard_map/ppermute | solution.py:465
  138.1 1.0 copy-start.26
  152.0 2.9 %collective-permute-start.10 = (f32[6,256,128]{2,1,0:T(8,128)}, f32[6,256,128]{2,1,0:T(8,128)S(1)}, u32[]{:S(2)}, u32[]{:S(2)}) collective-permute-start(f32[6,256,128]{2,1,0:T(8,128)} %get-tuple-element.66), channel_id=1, source_target_pairs={{0,1},{1,0},{2,3},{3,2},{4,5},{5,4},{6,7},{7,6},{8,9},{9,8},{10,11... | collective-permute-start | bytes 2359304 | tf_op jit(solution)/shard_map/ppermute | solution.py:465
  152.5 25.8 %collective-permute-start.11 = (f32[2,2,264,256]{3,2,1,0:T(8,128)}, f32[2,2,264,256]{3,2,1,0:T(8,128)S(1)}, u32[]{:S(2)}, u32[]{:S(2)}) collective-permute-start(f32[2,2,264,256]{3,2,1,0:T(8,128)} %get-tuple-element.68.refs_0_), channel_id=1, source_target_pairs={{0,8},{8,16},{16,24},{24,32},{32,40},{40,48},{48,56},{56,64},{64,7... | collective-permute-start | bytes 3244040 | tf_op jit(solution)/shard_map/ppermute | solution.py:442
  154.9 1.1 copy-start.13
  156.1 22.2 %copy-start.8 = (f32[2,2,264,256]{3,2,1,0:T(8,128)S(1)}, f32[2,2,264,256]{3,2,1,0:T(8,128)}, u32[]{:S(2)}) copy-start(f32[2,2,264,256]{3,2,1,0:T(8,128)} %get-tuple-element.68.refs_0_) | copy-start | bytes 3244036
  171.3 11.8 %all-to-all-start.4 = ((f32[16,24,128]{2,1,0:T(8,128)}), f32[16,24,128]{2,1,0:T(8,128)S(1)}, u32[]{:S(2)}, u32[]{:S(2)}) async-start(f32[16,24,128]{2,1,0:T(8,128)} %bitcast.7), calls=%async_computation.4 | async-start | bytes 393216 | tf_op jit(solution)/shard_map/all_to_all | solution.py:473
  178.3 15.6 %copy-start.19 = (f32[8,128]{1,0:T(8,128)S(1)}, f32[8,128]{1,0:T(8,128)}, u32[]{:S(2)}) copy-start(f32[8,128]{1,0:T(8,128)} %get-tuple-element.77.loss) | copy-start | bytes 12292
  179.1 0.8 copy-start.22
  183.1 10.8 %collective-permute-start.12 = (f32[1,2,256,256]{3,2,1,0:T(8,128)}, f32[1,2,256,256]{3,2,1,0:T(8,128)S(1)}, u32[]{:S(2)}, u32[]{:S(2)}) collective-permute-start(f32[1,2,256,256]{3,2,1,0:T(8,128)} %copy-done.22), channel_id=1, source_target_pairs={{0,1},{1,2},{2,3},{3,4},{4,5},{5,6},{6,7},{8,9},{9,10},{10,11},{11... | collective-permute-start | bytes 1572872 | tf_op jit(solution)/shard_map/ppermute | solution.py:442
  194.7 27.7 %copy-start.1 = (f32[2,256,512]{2,1,0:T(8,128)S(1)}, f32[2,256,512]{2,1,0:T(8,128)}, u32[]{:S(2)}) copy-start(f32[2,256,512]{2,1,0:T(8,128)} %refs_3_.1) | copy-start | bytes 3145732
  194.7 27.7 %copy-start.12 = (f32[2,256,512]{2,1,0:T(8,128)S(1)}, f32[2,256,512]{2,1,0:T(8,128)}, u32[]{:S(2)}) copy-start(f32[2,256,512]{2,1,0:T(8,128)} %copy-done.11) | copy-start | bytes 3145732
  194.7 27.7 %copy-start.18 = (f32[8,128]{1,0:T(8,128)S(1)}, f32[8,128]{1,0:T(8,128)}, u32[]{:S(2)}) copy-start(f32[8,128]{1,0:T(8,128)} %get-tuple-element.64.rate_first) | copy-start | bytes 12292
  217.1 5.3 %collective-permute-start.13 = (f32[64,32,128]{2,1,0:T(8,128)S(1)}, f32[64,32,128]{2,1,0:T(8,128)S(1)}, u32[]{:S(2)}, u32[]{:S(2)}) collective-permute-start(f32[64,32,128]{2,1,0:T(8,128)S(1)} %all_to_all.32.refs_0_), channel_id=1, source_target_pairs={{0,1},{1,0},{2,3},{3,2},{4,5},{5,4},{6,7},{7,6},{8,9},{9,8},{10,11... | collective-permute-start | bytes 3145736 | tf_op jit(solution)/shard_map/ppermute | solution.py:465

commit v5 on v4

--- a/solution.py
+++ b/solution.py
@@ -311,7 +311,7 @@
             pltpu.SemaphoreType.DMA((1,)),
             *[pltpu.VMEM(value.shape, value.dtype) for value in big],
         ],
-        compiler_params=pltpu.CompilerParams(vmem_limit_bytes=(60 if iteration else 48) * MEGA),
+        compiler_params=pltpu.CompilerParams(vmem_limit_bytes=48 * MEGA),
         cost_estimate=pl.CostEstimate(flops=8_000_000_000, bytes_accessed=12_000_000, transcendentals=0),
     )(corners, counts, *big)
 

time: 227 us -> 228 us (level)
    unnamed x54 -> x52, local copies, waits for them, and re-layouts: 8.36 us -> 7.34 us
where the time goes in v5:
time: 228 us; the launch traced here: 227 us
  starting transfers between devices  61.4 us (27%)
  waiting for transfers between devices  56.2 us (25%)
  blocking collectives  53.6 us (24%)
  Pallas kernels  45.9 us (20%)
  local copies, waits for them, and re-layouts  8.58 us (4%)
    ppermute x10, waiting for transfers between devices, shift(): lax.ppermute(value, axis, [(source, source + steps) for source in range(f...  38.2 us
    all_to_all x2, blocking collectives, reduce_chips(): lax.all_to_all(value.reshape(layers, rows * CHUNK, HALF), 'layer', 0, 0,...  30.5 us
    ppermute x10, starting transfers between devices, shift(): lax.ppermute(value, axis, [(source, source + steps) for source in range(f...  28.5 us
    pallas_call x2, Pallas kernels, window_call(): pl.pallas_call(lambda *refs: window_kernel(iteration, *refs), out_shape=(...  28 us
    all_to_all x1, blocking collectives, finish_tile(): return (tile, lax.all_to_all(sent, CHIPS, 0, 0, tiled=True), losses)  23.1 us
    all_to_all x2, starting transfers between devices, reduce_rows(): lax.all_to_all(part.reshape(rows, CHUNK, HALF), 'row', 0, 0, tiled=True)  15.3 us
    pallas_call x9, Pallas kernels, call(): pl.pallas_call(kernel, out_shape=tuple(out_shape), in_specs=[SMEM] * n_sm...  14.5 us
    all_to_all x1, starting transfers between devices, finish_tile(): return (tile, lax.all_to_all(sent, CHIPS, 0, 0, tiled=True), losses)  10.8 us
  transfers between devices with their start and end apart: 17, of which 11 were waited for; matrix products, arithmetic and copies ran while one was open for 0% of the time, Pallas kernels for 6%

profile of v5, /device:TPU:1, one launch (start us, length us, event | category | flops | bytes accessed | tf_op | source)
XLA Modules:
  0.0 226.9 jit_solution(5089283074921898160)
XLA Ops:
  0.6 0.0 copy-start
  0.6 0.0 copy-start.24
  0.7 0.0 copy-start.20
  0.7 0.0 copy-start.17
  0.7 1.2 slice.6
  1.9 1.3 collective-permute-start
  3.2 3.3 %collective-permute-start.2 = (f32[2,256,256]{2,1,0:T(8,128)S(1)}, f32[2,256,256]{2,1,0:T(8,128)S(1)}, u32[]{:S(2)}, u32[]{:S(2)}) collective-permute-start(f32[2,256,256]{2,1,0:T(8,128)S(1)} %slice.6), channel_id=1, source_target_pairs={{1,0},{2,1},{3,2},{4,3},{5,4},{6,5},{7,6},{9,8},{10,9},{11,10},{12... | collective-permute-start | bytes 1572872 | tf_op jit(solution)/shard_map/ppermute | solution.py:442
  6.6 1.3 collective-permute-start.1
  7.9 9.3 %collective-permute-done.refs_3_.below0 = f32[2,256,256]{2,1,0:T(8,128)S(1)} collective-permute-done((f32[2,256,256]{2,1,0:T(8,128)S(1)}, f32[2,256,256]{2,1,0:T(8,128)S(1)}, u32[]{:S(2)}, u32[]{:S(2)}) %collective-permute-start) | collective-permute-done | bytes 524320 | tf_op jit(solution)/shard_map/ppermute | solution.py:442
  17.2 4.8 %collective-permute-start.3 = (f32[2,256,256]{2,1,0:T(8,128)S(1)}, f32[2,256,256]{2,1,0:T(8,128)S(1)}, u32[]{:S(2)}, u32[]{:S(2)}) collective-permute-start(f32[2,256,256]{2,1,0:T(8,128)S(1)} %collective-permute-done.refs_3_.below0), channel_id=1, source_target_pairs={{1,0},{2,1},{3,2},{4,3},{5,4},{6,5},{7,6},{9,8},{10,9},{11,10},{12... | collective-permute-start | bytes 1572872 | tf_op jit(solution)/shard_map/ppermute | solution.py:442
  21.9 6.5 %collective-permute-done.1.refs_4_.below1 = f32[2,256,256]{2,1,0:T(8,128)S(1)} collective-permute-done((f32[2,256,256]{2,1,0:T(8,128)S(1)}, f32[2,256,256]{2,1,0:T(8,128)S(1)}, u32[]{:S(2)}, u32[]{:S(2)}) %collective-permute-start.1) | collective-permute-done | bytes 524320 | tf_op jit(solution)/shard_map/ppermute | solution.py:442
  28.4 0.0 collective-permute-done.2.refs_5_.rim
  28.4 2.0 collective-permute-done.3.refs_6_.diag
  30.4 14.2 %shard_map.94 = (f32[2,2,264,256]{3,2,1,0:T(8,128)}, f32[6,256,128]{2,1,0:T(8,128)S(1)}, f32[6,256,128]{2,1,0:T(8,128)S(1)}, f32[8,128]{1,0:T(8,128)S(1)}) custom-call(s32[2,2,2]{2,1,0:T(2,128)S(1)} %bitcast.13, s32[2]{0:T(128)S(1)} %bitcast.17, f32[2,256,512]{2,1,0:T(8,128)S(1)} %copy-done, f32[2,256,256]{2,1,0:T(8,128)S(1)} %collective-permute-done.refs_3_.below0, ...), custom_call_target="tpu_custom_call" | custom-call | flops 8000000000 | bytes 12000000 | tf_op jit(solution)/shard_map/pallas_call | solution.py:296
  44.6 0.1 collective-permute-start.4
  44.7 1.3 collective-permute-start.6
  46.0 4.1 %collective-permute-start.5 = (f32[2,2,264,256]{3,2,1,0:T(8,128)}, f32[2,2,264,256]{3,2,1,0:T(8,128)S(1)}, u32[]{:S(2)}, u32[]{:S(2)}) collective-permute-start(f32[2,2,264,256]{3,2,1,0:T(8,128)} %get-tuple-element.48.refs_0_), channel_id=1, source_target_pairs={{0,8},{8,16},{16,24},{24,32},{32,40},{40,48},{48,56},{56,64},{64,7... | collective-permute-start | bytes 3244040 | tf_op jit(solution)/shard_map/ppermute | solution.py:442
  50.1 0.1 shard_map.95
  50.2 0.0 copy-start.5
  50.2 16.0 %all_to_all.30.parts = f32[4,384,128]{2,1,0:T(8,128)S(1)} all-to-all(f32[4,384,128]{2,1,0:T(8,128)S(1)} %bitcast.10), channel_id=1, replica_groups=mesh['row'=16,'layer'=4,'core'=2] {'layer'}, dimensions={0} | all-to-all | bytes 1572864 | tf_op jit(solution)/shard_map/all_to_all | solution.py:469
  66.3 0.7 shard_map.96
  67.0 10.9 %all-to-all-start.1 = ((f32[16,24,128]{2,1,0:T(8,128)}), f32[16,24,128]{2,1,0:T(8,128)S(1)}, u32[]{:S(2)}, u32[]{:S(2)}) async-start(f32[16,24,128]{2,1,0:T(8,128)} %bitcast.5), calls=%async_computation.1 | async-start | bytes 393216 | tf_op jit(solution)/shard_map/all_to_all | solution.py:473
  77.9 1.0 copy-done.6
  78.9 1.2 copy-done.7
  80.1 2.8 %shard_map.97 = (f32[2,2,256,256]{3,2,1,0:T(8,128)S(1)}, f32[2,2,256,256]{3,2,1,0:T(8,128)S(1)}, f32[2,2,256,256]{3,2,1,0:T(8,128)S(1)}) custom-call(f32[2,2,264,256]{3,2,1,0:T(8,128)S(1)} %copy-done.5, f32[2,2,264,256]{3,2,1,0:T(8,128)S(1)} %copy-done.7, f32[2,2,264,256]{3,2,1,0:T(8,128)} %collective-permute-done.6.refs_2_, ...), custom_call_target="tpu_custom_call" | custom-call | flops 10000000 | bytes 6393856 | tf_op jit(solution)/shard_map/pallas_call | solution.py:279
  82.9 0.0 copy-start.9
  82.9 1.0 copy-done.9
  83.9 1.1 all-to-all-done.1.parts
  84.9 5.2 %collective-permute-start.7 = (f32[2,2,256,256]{3,2,1,0:T(8,128)}, f32[2,2,256,256]{3,2,1,0:T(8,128)S(1)}, u32[]{:S(2)}, u32[]{:S(2)}) collective-permute-start(f32[2,2,256,256]{3,2,1,0:T(8,128)} %copy-done.9), channel_id=1, source_target_pairs={{0,1},{1,2},{2,3},{3,4},{4,5},{5,6},{6,7},{8,9},{9,10},{10,11},{11... | collective-permute-start | bytes 3145736 | tf_op jit(solution)/shard_map/ppermute | solution.py:442
  90.2 1.9 collective-permute-start.8
  92.1 10.1 %collective-permute-done.7.from_left.left = f32[2,2,256,256]{3,2,1,0:T(8,128)S(1)} collective-permute-done((f32[2,2,256,256]{3,2,1,0:T(8,128)}, f32[2,2,256,256]{3,2,1,0:T(8,128)S(1)}, u32[]{:S(2)}, u32[]{:S(2)}) %collective-permute-start.7) | collective-permute-done | bytes 1048608 | tf_op jit(solution)/shard_map/ppermute | solution.py:442
  102.2 0.9 shard_map.98
  103.1 0.1 copy-done.4
  103.2 1.0 copy-done.10
  104.2 1.0 copy-done.11
  105.1 10.8 %all-to-all-start.2 = ((f32[64,32,128]{2,1,0:T(8,128)}), f32[64,32,128]{2,1,0:T(8,128)S(1)}, u32[]{:S(2)}, u32[]{:S(2)}) async-start(f32[64,32,128]{2,1,0:T(8,128)} %copy-done.10), calls=%async_computation.2 | async-start | bytes 2097152 | tf_op jit(solution)/shard_map/all_to_all | solution.py:479
  116.0 0.0 copy-start.18
  116.0 0.0 copy-start.21
  116.0 0.0 copy-start.25
  116.0 7.7 %shard_map.99 = (f32[2,2,256,256]{3,2,1,0:T(8,128)}, f32[2,2,256,256]{3,2,1,0:T(8,128)}) custom-call(s32[2,2,2]{2,1,0:T(2,128)} %bitcast.12, f32[2,256,512]{2,1,0:T(8,128)} %refs_3_.1, f32[2,256,256]{2,1,0:T(8,128)} %copy-done.13, f32[2,256,256]{2,1,0:T(8,128)} %copy-done.15, f32[2,256,256]{2,1,0:T(8,128)} %copy-done.14, f32[2,256,256]{2,1,0:T(8,128)} %copy-done.16, ...), custom_call_target="tpu_custom_call" | custom-call | flops 10000000 | bytes 10485792 | tf_op jit(solution)/shard_map/pallas_call | solution.py:279
  123.7 8.9 %all-to-all-done.2.refs_2_ = f32[64,32,128]{2,1,0:T(8,128)S(1)} async-done(((f32[64,32,128]{2,1,0:T(8,128)}), f32[64,32,128]{2,1,0:T(8,128)S(1)}, u32[]{:S(2)}, u32[]{:S(2)}) %all-to-all-start.2) | async-done | bytes 1048608 | tf_op jit(solution)/shard_map/all_to_all | solution.py:479
  132.6 3.0 %collective-permute-start.9 = (f32[64,32,128]{2,1,0:T(8,128)S(1)}, f32[64,32,128]{2,1,0:T(8,128)S(1)}, u32[]{:S(2)}, u32[]{:S(2)}) collective-permute-start(f32[64,32,128]{2,1,0:T(8,128)S(1)} %all-to-all-done.2.refs_2_), channel_id=1, source_target_pairs={{0,1},{1,0},{2,3},{3,2},{4,5},{5,4},{6,7},{7,6},{8,9},{9,8},{10,11... | collective-permute-start | bytes 3145736 | tf_op jit(solution)/shard_map/ppermute | solution.py:465
  135.6 2.3 %collective-permute-done.9.refs_3_ = f32[64,32,128]{2,1,0:T(8,128)S(1)} collective-permute-done((f32[64,32,128]{2,1,0:T(8,128)S(1)}, f32[64,32,128]{2,1,0:T(8,128)S(1)}, u32[]{:S(2)}, u32[]{:S(2)}) %collective-permute-start.9) | collective-permute-done | bytes 1048608 | tf_op jit(solution)/shard_map/ppermute | solution.py:465
  137.9 1.2 copy-done.19
  139.2 13.8 %shard_map.100 = (f32[2,2,264,256]{3,2,1,0:T(8,128)}, f32[6,256,128]{2,1,0:T(8,128)S(1)}, f32[6,256,128]{2,1,0:T(8,128)S(1)}, f32[6,256,256]{2,1,0:T(8,128)}, f3...) custom-call(s32[2,2,2]{2,1,0:T(2,128)S(1)} %bitcast.14, s32[2]{0:T(128)S(1)} %bitcast.18, ...), custom_call_target="tpu_custom_call" | custom-call | flops 8000000000 | bytes 12000000 | tf_op jit(solution)/shard_map/pallas_call | solution.py:296
  153.0 0.4 collective-permute-start.10
  153.4 2.4 %collective-permute-start.11 = (f32[2,2,264,256]{3,2,1,0:T(8,128)}, f32[2,2,264,256]{3,2,1,0:T(8,128)S(1)}, u32[]{:S(2)}, u32[]{:S(2)}) collective-permute-start(f32[2,2,264,256]{3,2,1,0:T(8,128)} %get-tuple-element.68.refs_0_), channel_id=1, source_target_pairs={{0,8},{8,16},{16,24},{24,32},{32,40},{40,48},{48,56},{56,64},{64,7... | collective-permute-start | bytes 3244040 | tf_op jit(solution)/shard_map/ppermute | solution.py:442
  155.9 0.1 shard_map.101
  156.0 0.0 copy-start.8
  156.0 14.5 %all_to_all.31.parts = f32[4,384,128]{2,1,0:T(8,128)S(1)} all-to-all(f32[4,384,128]{2,1,0:T(8,128)S(1)} %bitcast.11), channel_id=1, replica_groups=mesh['row'=16,'layer'=4,'core'=2] {'layer'}, dimensions={0} | all-to-all | bytes 1572864 | tf_op jit(solution)/shard_map/all_to_all | solution.py:469
  170.5 0.7 shard_map.102
  171.2 4.5 %all-to-all-start.4 = ((f32[16,24,128]{2,1,0:T(8,128)}), f32[16,24,128]{2,1,0:T(8,128)S(1)}, u32[]{:S(2)}, u32[]{:S(2)}) async-start(f32[16,24,128]{2,1,0:T(8,128)} %bitcast.7), calls=%async_computation.4 | async-start | bytes 393216 | tf_op jit(solution)/shard_map/all_to_all | solution.py:473
  175.7 3.9 %collective-permute-done.11.refs_1_ = f32[2,2,264,256]{3,2,1,0:T(8,128)S(1)} collective-permute-done((f32[2,2,264,256]{3,2,1,0:T(8,128)}, f32[2,2,264,256]{3,2,1,0:T(8,128)S(1)}, u32[]{:S(2)}, u32[]{:S(2)}) %collective-permute-start.11) | collective-permute-done | bytes 1081376 | tf_op jit(solution)/shard_map/ppermute | solution.py:442
  179.6 0.8 shard_map.103
  180.4 0.0 copy-start.22
  180.4 0.8 copy-done.22
  181.2 3.4 %all-to-all-done.4.parts = f32[16,24,128]{2,1,0:T(8,128)S(1)} async-done(((f32[16,24,128]{2,1,0:T(8,128)}), f32[16,24,128]{2,1,0:T(8,128)S(1)}, u32[]{:S(2)}, u32[]{:S(2)}) %all-to-all-start.4) | async-done | bytes 196640 | tf_op jit(solution)/shard_map/all_to_all | solution.py:473
  184.7 2.9 %collective-permute-start.12 = (f32[1,2,256,256]{3,2,1,0:T(8,128)}, f32[1,2,256,256]{3,2,1,0:T(8,128)S(1)}, u32[]{:S(2)}, u32[]{:S(2)}) collective-permute-start(f32[1,2,256,256]{3,2,1,0:T(8,128)} %copy-done.22), channel_id=1, source_target_pairs={{0,1},{1,2},{2,3},{3,4},{4,5},{5,6},{6,7},{8,9},{9,10},{10,11},{11... | collective-permute-start | bytes 1572872 | tf_op jit(solution)/shard_map/ppermute | solution.py:442
  187.5 6.4 %collective-permute-done.12.from_left = f32[1,2,256,256]{3,2,1,0:T(8,128)S(1)} collective-permute-done((f32[1,2,256,256]{3,2,1,0:T(8,128)}, f32[1,2,256,256]{3,2,1,0:T(8,128)S(1)}, u32[]{:S(2)}, u32[]{:S(2)}) %collective-permute-start.12) | collective-permute-done | bytes 524320 | tf_op jit(solution)/shard_map/ppermute | solution.py:442
  193.9 0.8 shard_map.104
  194.8 23.1 %all_to_all.32.refs_0_ = f32[64,32,128]{2,1,0:T(8,128)S(1)} all-to-all(f32[64,32,128]{2,1,0:T(8,128)S(1)} %get-tuple-element.78), channel_id=1, replica_groups=mesh['row'=16,'layer'=4,'core'=2] {'layer','row'}, dimensions={0} | all-to-all | bytes 2097152 | tf_op jit(solution)/shard_map/all_to_all | solution.py:479
  217.8 3.3 %collective-permute-start.13 = (f32[64,32,128]{2,1,0:T(8,128)S(1)}, f32[64,32,128]{2,1,0:T(8,128)S(1)}, u32[]{:S(2)}, u32[]{:S(2)}) collective-permute-start(f32[64,32,128]{2,1,0:T(8,128)S(1)} %all_to_all.32.refs_0_), channel_id=1, source_target_pairs={{0,1},{1,0},{2,3},{3,2},{4,5},{5,4},{6,7},{7,6},{8,9},{9,8},{10,11... | collective-permute-start | bytes 3145736 | tf_op jit(solution)/shard_map/ppermute | solution.py:465
  221.1 2.3 %collective-permute-done.13.refs_1_ = f32[64,32,128]{2,1,0:T(8,128)S(1)} collective-permute-done((f32[64,32,128]{2,1,0:T(8,128)S(1)}, f32[64,32,128]{2,1,0:T(8,128)S(1)}, u32[]{:S(2)}, u32[]{:S(2)}) %collective-permute-start.13) | collective-permute-done | bytes 1048608 | tf_op jit(solution)/shard_map/ppermute | solution.py:465
  223.4 3.3 %shard_map.105 = (f32[2,256,512]{2,1,0:T(8,128)}, f32[6,256,256]{2,1,0:T(8,128)}) custom-call(f32[8,128]{1,0:T(8,128)S(1)} %get-tuple-element.64.rate_first, f32[64,32,128]{2,1,0:T(8,128)S(1)} %all_to_all.32.refs_0_, f32[64,32,128]{2,1,0:T(8,128)S(1)} %collective-permute-done.13.refs_1_, f32[6,256,256]{2,1,0:T(8,128)} %get-tuple-element.79.refs_2_, ...), custom_call_target="tpu_custom_call" | custom-call | flops 10000000 | bytes 9000000 | tf_op jit(solution)/shard_map/pallas_call | solution.py:423
  (39 shorter events, 0.1 us)
Async XLA Ops:
  0.6 5.9 %copy-start = (f32[2,256,512]{2,1,0:T(8,128)S(1)}, f32[2,256,512]{2,1,0:T(8,128)}, u32[]{:S(2)}) copy-start(f32[2,256,512]{2,1,0:T(8,128)} %refs_3_.1) | copy-start | bytes 3145732
  0.6 29.7 %copy-start.24 = (bf16[2,256,256]{2,1,0:T(8,128)(2,1)S(1)}, bf16[2,256,256]{2,1,0:T(8,128)(2,1)}, u32[]{:S(2)}) copy-start(bf16[2,256,256]{2,1,0:T(8,128)(2,1)} %constant.5.clone.refs_10_.refs_9_) | copy-start | bytes 786436
  0.7 29.7 %copy-start.20 = (bf16[2,1,1,2,256,256]{5,4,3,2,1,0:T(8,128)(2,1)S(1)}, bf16[2,1,1,2,256,256]{5,4,3,2,1,0:T(8,128)(2,1)}, u32[]{:S(2)}) copy-start(bf16[2,1,1,2,256,256]{5,4,3,2,1,0:T(8,128)(2,1)} %param.11) | copy-start | bytes 1572868
  0.7 29.7 %copy-start.23 = (s32[2,1,1]{0,2,1:T(1,128)S(1)}, s32[2,1,1]{0,2,1:T(1,128)}, u32[]{:S(2)}) copy-start(s32[2,1,1]{0,2,1:T(1,128)} %param.10) | copy-start | bytes 28
  0.7 29.7 %copy-start.17 = (s32[2,1,1,2,2]{4,3,2,1,0:T(2,128)S(1)}, s32[2,1,1,2,2]{4,3,2,1,0:T(2,128)}, u32[]{:S(2)}) copy-start(s32[2,1,1,2,2]{4,3,2,1,0:T(2,128)} %param.9) | copy-start | bytes 100
  1.9 15.3 %collective-permute-start = (f32[2,256,256]{2,1,0:T(8,128)S(1)}, f32[2,256,256]{2,1,0:T(8,128)S(1)}, u32[]{:S(2)}, u32[]{:S(2)}) collective-permute-start(f32[2,256,256]{2,1,0:T(8,128)S(1)} %slice.6), channel_id=1, source_target_pairs={{8,0},{16,8},{24,16},{32,24},{40,32},{48,40},{56,48},{64,56},{72,6... | collective-permute-start | bytes 1572872 | tf_op jit(solution)/shard_map/ppermute | solution.py:442
  3.2 25.2 %collective-permute-start.2 = (f32[2,256,256]{2,1,0:T(8,128)S(1)}, f32[2,256,256]{2,1,0:T(8,128)S(1)}, u32[]{:S(2)}, u32[]{:S(2)}) collective-permute-start(f32[2,256,256]{2,1,0:T(8,128)S(1)} %slice.6), channel_id=1, source_target_pairs={{1,0},{2,1},{3,2},{4,3},{5,4},{6,5},{7,6},{9,8},{10,9},{11,10},{12... | collective-permute-start | bytes 1572872 | tf_op jit(solution)/shard_map/ppermute | solution.py:442
  6.6 21.8 %collective-permute-start.1 = (f32[2,256,256]{2,1,0:T(8,128)S(1)}, f32[2,256,256]{2,1,0:T(8,128)S(1)}, u32[]{:S(2)}, u32[]{:S(2)}) collective-permute-start(f32[2,256,256]{2,1,0:T(8,128)S(1)} %slice.7), channel_id=1, source_target_pairs={{8,0},{16,8},{24,16},{32,24},{40,32},{48,40},{56,48},{64,56},{72,6... | collective-permute-start | bytes 1572872 | tf_op jit(solution)/shard_map/ppermute | solution.py:442
  17.2 27.4 %copy-start.13 = (f32[2,256,256]{2,1,0:T(8,128)}, f32[2,256,256]{2,1,0:T(8,128)S(1)}, u32[]{:S(2)}) copy-start(f32[2,256,256]{2,1,0:T(8,128)S(1)} %collective-permute-done.refs_3_.below0) | copy-start | bytes 1572868
  17.2 13.2 %collective-permute-start.3 = (f32[2,256,256]{2,1,0:T(8,128)S(1)}, f32[2,256,256]{2,1,0:T(8,128)S(1)}, u32[]{:S(2)}, u32[]{:S(2)}) collective-permute-start(f32[2,256,256]{2,1,0:T(8,128)S(1)} %collective-permute-done.refs_3_.below0), channel_id=1, source_target_pairs={{1,0},{2,1},{3,2},{4,3},{5,4},{6,5},{7,6},{9,8},{10,9},{11,10},{12... | collective-permute-start | bytes 1572872 | tf_op jit(solution)/shard_map/ppermute | solution.py:442
  28.4 16.2 %copy-start.15 = (f32[2,256,256]{2,1,0:T(8,128)}, f32[2,256,256]{2,1,0:T(8,128)S(1)}, u32[]{:S(2)}) copy-start(f32[2,256,256]{2,1,0:T(8,128)S(1)} %collective-permute-done.1.refs_4_.below1) | copy-start | bytes 1572868
  28.4 16.2 %copy-start.14 = (f32[2,256,256]{2,1,0:T(8,128)}, f32[2,256,256]{2,1,0:T(8,128)S(1)}, u32[]{:S(2)}) copy-start(f32[2,256,256]{2,1,0:T(8,128)S(1)} %collective-permute-done.2.refs_5_.rim) | copy-start | bytes 1572868
  30.4 14.3 %copy-start.16 = (f32[2,256,256]{2,1,0:T(8,128)}, f32[2,256,256]{2,1,0:T(8,128)S(1)}, u32[]{:S(2)}) copy-start(f32[2,256,256]{2,1,0:T(8,128)S(1)} %collective-permute-done.3.refs_6_.diag) | copy-start | bytes 1572868
  44.6 5.5 %collective-permute-start.4 = (f32[6,256,128]{2,1,0:T(8,128)S(1)}, f32[6,256,128]{2,1,0:T(8,128)S(1)}, u32[]{:S(2)}, u32[]{:S(2)}) collective-permute-start(f32[6,256,128]{2,1,0:T(8,128)S(1)} %get-tuple-element.46), channel_id=1, source_target_pairs={{0,1},{1,0},{2,3},{3,2},{4,5},{5,4},{6,7},{7,6},{8,9},{9,8},{10,11... | collective-permute-start | bytes 2359304 | tf_op jit(solution)/shard_map/ppermute | solution.py:465
  44.7 33.1 %collective-permute-start.6 = (f32[2,2,264,256]{3,2,1,0:T(8,128)}, f32[2,2,264,256]{3,2,1,0:T(8,128)}, u32[]{:S(2)}, u32[]{:S(2)}) collective-permute-start(f32[2,2,264,256]{3,2,1,0:T(8,128)} %get-tuple-element.48.refs_0_), channel_id=1, source_target_pairs={{8,0},{16,8},{24,16},{32,24},{40,32},{48,40},{56,48},{64,56},{72,6... | collective-permute-start | bytes 3244040 | tf_op jit(solution)/shard_map/ppermute | solution.py:442
  46.0 31.9 %collective-permute-start.5 = (f32[2,2,264,256]{3,2,1,0:T(8,128)}, f32[2,2,264,256]{3,2,1,0:T(8,128)S(1)}, u32[]{:S(2)}, u32[]{:S(2)}) collective-permute-start(f32[2,2,264,256]{3,2,1,0:T(8,128)} %get-tuple-element.48.refs_0_), channel_id=1, source_target_pairs={{0,8},{8,16},{16,24},{24,32},{32,40},{40,48},{48,56},{56,64},{64,7... | collective-permute-start | bytes 3244040 | tf_op jit(solution)/shard_map/ppermute | solution.py:442
  50.2 28.7 %copy-start.5 = (f32[2,2,264,256]{3,2,1,0:T(8,128)S(1)}, f32[2,2,264,256]{3,2,1,0:T(8,128)}, u32[]{:S(2)}) copy-start(f32[2,2,264,256]{3,2,1,0:T(8,128)} %get-tuple-element.48.refs_0_) | copy-start | bytes 3244036
  67.0 17.9 %all-to-all-start.1 = ((f32[16,24,128]{2,1,0:T(8,128)}), f32[16,24,128]{2,1,0:T(8,128)S(1)}, u32[]{:S(2)}, u32[]{:S(2)}) async-start(f32[16,24,128]{2,1,0:T(8,128)} %bitcast.5), calls=%async_computation.1 | async-start | bytes 393216 | tf_op jit(solution)/shard_map/all_to_all | solution.py:473
  77.9 1.0 copy-start.6
  78.9 1.2 copy-start.7
  82.9 1.0 copy-start.9
  83.9 19.2 %copy-start.2 = (f32[2,2,256,256]{3,2,1,0:T(8,128)}, f32[2,2,256,256]{3,2,1,0:T(8,128)S(1)}, u32[]{:S(2)}) copy-start(f32[2,2,256,256]{3,2,1,0:T(8,128)S(1)} %get-tuple-element.53.block0) | copy-start | bytes 3145732
  83.9 19.2 %copy-start.3 = (f32[2,2,256,256]{3,2,1,0:T(8,128)}, f32[2,2,256,256]{3,2,1,0:T(8,128)S(1)}, u32[]{:S(2)}) copy-start(f32[2,2,256,256]{3,2,1,0:T(8,128)S(1)} %get-tuple-element.54.block1) | copy-start | bytes 3145732
  84.9 17.3 %collective-permute-start.7 = (f32[2,2,256,256]{3,2,1,0:T(8,128)}, f32[2,2,256,256]{3,2,1,0:T(8,128)S(1)}, u32[]{:S(2)}, u32[]{:S(2)}) collective-permute-start(f32[2,2,256,256]{3,2,1,0:T(8,128)} %copy-done.9), channel_id=1, source_target_pairs={{0,1},{1,2},{2,3},{3,4},{4,5},{5,6},{6,7},{8,9},{9,10},{10,11},{11... | collective-permute-start | bytes 3145736 | tf_op jit(solution)/shard_map/ppermute | solution.py:442
  90.2 25.8 %collective-permute-start.8 = (f32[2,2,256,256]{3,2,1,0:T(8,128)S(1)}, f32[2,2,256,256]{3,2,1,0:T(8,128)}, u32[]{:S(2)}, u32[]{:S(2)}) collective-permute-start(f32[2,2,256,256]{3,2,1,0:T(8,128)S(1)} %get-tuple-element.53.block0), channel_id=1, source_target_pairs={{1,0},{2,1},{3,2},{4,3},{5,4},{6,5},{7,6},{9,8},{10,9},{11,10},{12... | collective-permute-start | bytes 3145736 | tf_op jit(solution)/shard_map/ppermute | solution.py:442
  102.2 1.0 copy-start.4
  103.2 1.0 copy-start.10
  104.2 1.0 copy-start.11
  105.1 27.5 %all-to-all-start.2 = ((f32[64,32,128]{2,1,0:T(8,128)}), f32[64,32,128]{2,1,0:T(8,128)S(1)}, u32[]{:S(2)}, u32[]{:S(2)}) async-start(f32[64,32,128]{2,1,0:T(8,128)} %copy-done.10), calls=%async_computation.2 | async-start | bytes 2097152 | tf_op jit(solution)/shard_map/all_to_all | solution.py:479
  116.0 22.0 %copy-start.18 = (s32[2,1,1,2,2]{4,3,2,1,0:T(2,128)S(1)}, s32[2,1,1,2,2]{4,3,2,1,0:T(2,128)}, u32[]{:S(2)}) copy-start(s32[2,1,1,2,2]{4,3,2,1,0:T(2,128)} %param.9) | copy-start | bytes 100
  116.0 21.9 %copy-start.21 = (bf16[2,1,1,2,256,256]{5,4,3,2,1,0:T(8,128)(2,1)S(1)}, bf16[2,1,1,2,256,256]{5,4,3,2,1,0:T(8,128)(2,1)}, u32[]{:S(2)}) copy-start(bf16[2,1,1,2,256,256]{5,4,3,2,1,0:T(8,128)(2,1)} %param.11) | copy-start | bytes 1572868
  116.0 21.9 %copy-start.25 = (bf16[2,256,256]{2,1,0:T(8,128)(2,1)S(1)}, bf16[2,256,256]{2,1,0:T(8,128)(2,1)}, u32[]{:S(2)}) copy-start(bf16[2,256,256]{2,1,0:T(8,128)(2,1)} %constant.5.clone.refs_10_.refs_9_) | copy-start | bytes 786436
  132.6 5.3 %collective-permute-start.9 = (f32[64,32,128]{2,1,0:T(8,128)S(1)}, f32[64,32,128]{2,1,0:T(8,128)S(1)}, u32[]{:S(2)}, u32[]{:S(2)}) collective-permute-start(f32[64,32,128]{2,1,0:T(8,128)S(1)} %all-to-all-done.2.refs_2_), channel_id=1, source_target_pairs={{0,1},{1,0},{2,3},{3,2},{4,5},{5,4},{6,7},{7,6},{8,9},{9,8},{10,11... | collective-permute-start | bytes 3145736 | tf_op jit(solution)/shard_map/ppermute | solution.py:465
  137.9 1.2 copy-start.19
  153.0 2.9 %collective-permute-start.10 = (f32[6,256,128]{2,1,0:T(8,128)S(1)}, f32[6,256,128]{2,1,0:T(8,128)S(1)}, u32[]{:S(2)}, u32[]{:S(2)}) collective-permute-start(f32[6,256,128]{2,1,0:T(8,128)S(1)} %get-tuple-element.66), channel_id=1, source_target_pairs={{0,1},{1,0},{2,3},{3,2},{4,5},{5,4},{6,7},{7,6},{8,9},{9,8},{10,11... | collective-permute-start | bytes 2359304 | tf_op jit(solution)/shard_map/ppermute | solution.py:465
  153.4 26.2 %collective-permute-start.11 = (f32[2,2,264,256]{3,2,1,0:T(8,128)}, f32[2,2,264,256]{3,2,1,0:T(8,128)S(1)}, u32[]{:S(2)}, u32[]{:S(2)}) collective-permute-start(f32[2,2,264,256]{3,2,1,0:T(8,128)} %get-tuple-element.68.refs_0_), channel_id=1, source_target_pairs={{0,8},{8,16},{16,24},{24,32},{32,40},{40,48},{48,56},{56,64},{64,7... | collective-permute-start | bytes 3244040 | tf_op jit(solution)/shard_map/ppermute | solution.py:442
  156.0 23.6 %copy-start.8 = (f32[2,2,264,256]{3,2,1,0:T(8,128)S(1)}, f32[2,2,264,256]{3,2,1,0:T(8,128)}, u32[]{:S(2)}) copy-start(f32[2,2,264,256]{3,2,1,0:T(8,128)} %get-tuple-element.68.refs_0_) | copy-start | bytes 3244036
  171.2 13.4 %all-to-all-start.4 = ((f32[16,24,128]{2,1,0:T(8,128)}), f32[16,24,128]{2,1,0:T(8,128)S(1)}, u32[]{:S(2)}, u32[]{:S(2)}) async-start(f32[16,24,128]{2,1,0:T(8,128)} %bitcast.7), calls=%async_computation.4 | async-start | bytes 393216 | tf_op jit(solution)/shard_map/all_to_all | solution.py:473
  180.4 0.8 copy-start.22
  184.7 9.3 %collective-permute-start.12 = (f32[1,2,256,256]{3,2,1,0:T(8,128)}, f32[1,2,256,256]{3,2,1,0:T(8,128)S(1)}, u32[]{:S(2)}, u32[]{:S(2)}) collective-permute-start(f32[1,2,256,256]{3,2,1,0:T(8,128)} %copy-done.22), channel_id=1, source_target_pairs={{0,1},{1,2},{2,3},{3,4},{4,5},{5,6},{6,7},{8,9},{9,10},{10,11},{11... | collective-permute-start | bytes 1572872 | tf_op jit(solution)/shard_map/ppermute | solution.py:442
  194.7 28.7 %copy-start.1 = (f32[2,256,512]{2,1,0:T(8,128)S(1)}, f32[2,256,512]{2,1,0:T(8,128)}, u32[]{:S(2)}) copy-start(f32[2,256,512]{2,1,0:T(8,128)} %refs_3_.1) | copy-start | bytes 3145732
  194.8 28.7 %copy-start.12 = (f32[2,256,512]{2,1,0:T(8,128)S(1)}, f32[2,256,512]{2,1,0:T(8,128)}, u32[]{:S(2)}) copy-start(f32[2,256,512]{2,1,0:T(8,128)} %copy-done.11) | copy-start | bytes 3145732
  217.8 5.6 %collective-permute-start.13 = (f32[64,32,128]{2,1,0:T(8,128)S(1)}, f32[64,32,128]{2,1,0:T(8,128)S(1)}, u32[]{:S(2)}, u32[]{:S(2)}) collective-permute-start(f32[64,32,128]{2,1,0:T(8,128)S(1)} %all_to_all.32.refs_0_), channel_id=1, source_target_pairs={{0,1},{1,0},{2,3},{3,2},{4,5},{5,4},{6,7},{7,6},{8,9},{9,8},{10,11... | collective-permute-start | bytes 3145736 | tf_op jit(solution)/shard_map/ppermute | solution.py:465

commit v6 on v4

--- a/solution.py
+++ b/solution.py
@@ -129,15 +129,17 @@
         out_mid, out_rate = refs[:2]
         refs = refs[2:]
     out_loss, obj, field, lhs, factor, total_probe, grads, sems, out_sems, probe_sems, mid_sem = refs[:11]
-    held = refs[11:]
-    fetch = [pltpu.make_async_copy(src, dst, sems.at[k]) for k, (src, dst) in enumerate(zip(sources, held))]
+    direct = 5 if iteration == 0 else 0
+    held = [*sources[:direct], *refs[11:]]
+    fetch = [pltpu.make_async_copy(src, dst, sems.at[k]) for k, (src, dst) in enumerate(zip(sources[direct:], refs[11:]))]
     for copy in fetch:
         copy.start()
+    fetch = [None] * direct + fetch
     if iteration == 0:
         tile, below0, below1, rim, diag, tables, probe_ref, amp_ref, shuffle = held
     else:
         mine, other, probe_ref, patch, patch_grad, tables, amp_ref, shuffle = held
-    for copy in fetch[: 5 if iteration == 0 else 3]:
+    for copy in fetch[direct : 5 if iteration == 0 else 3]:
         copy.wait()
 
     if iteration:
@@ -293,10 +295,11 @@
         outs += [f32(2 * MODES, WIN, WIN), f32(8, HALF)]
         out_specs += [ANY, VMEM]
     big = [*data, amplitude, tables[1]]
+    direct = 5 if iteration == 0 else 0
     return pl.pallas_call(
         lambda *refs: window_kernel(iteration, *refs),
         out_shape=(*outs, f32(8, HALF)),
-        in_specs=[SMEM] * 2 + [ANY] * len(big),
+        in_specs=[SMEM] * 2 + [VMEM] * direct + [ANY] * (len(big) - direct),
         out_specs=(*out_specs, VMEM),
         scratch_shapes=[
             pltpu.VMEM((2, WIN, WIN), F32),
@@ -309,7 +312,7 @@
             pltpu.SemaphoreType.DMA((CAP,)),
             pltpu.SemaphoreType.DMA((4 * MODES,)),
             pltpu.SemaphoreType.DMA((1,)),
-            *[pltpu.VMEM(value.shape, value.dtype) for value in big],
+            *[pltpu.VMEM(value.shape, value.dtype) for value in big[direct:]],
         ],
         compiler_params=pltpu.CompilerParams(vmem_limit_bytes=(60 if iteration else 48) * MEGA),
         cost_estimate=pl.CostEstimate(flops=8_000_000_000, bytes_accessed=12_000_000, transcendentals=0),

time: 227 us -> 227 us (level)
  no operation moved by 1% of the time
where the time goes in v6:
time: 227 us; the launch traced here: 226 us
  starting transfers between devices  62.8 us (28%)
  waiting for transfers between devices  54.6 us (24%)
  blocking collectives  52.9 us (23%)
  Pallas kernels  44.7 us (20%)
  local copies, waits for them, and re-layouts  9.6 us (4%)
    ppermute x10, waiting for transfers between devices, shift(): lax.ppermute(value, axis, [(source, source + steps) for source in range(f...  36.8 us
    all_to_all x2, blocking collectives, reduce_chips(): lax.all_to_all(value.reshape(layers, rows * CHUNK, HALF), 'layer', 0, 0,...  30.6 us
    ppermute x10, starting transfers between devices, shift(): lax.ppermute(value, axis, [(source, source + steps) for source in range(f...  30 us
    pallas_call x2, Pallas kernels, window_call(): pl.pallas_call(lambda *refs: window_kernel(iteration, *refs), out_shape=(...  27 us
    all_to_all x1, blocking collectives, finish_tile(): return (tile, lax.all_to_all(sent, CHIPS, 0, 0, tiled=True), losses)  22.4 us
    all_to_all x2, starting transfers between devices, reduce_rows(): lax.all_to_all(part.reshape(rows, CHUNK, HALF), 'row', 0, 0, tiled=True)  15.3 us
    pallas_call x9, Pallas kernels, call(): pl.pallas_call(kernel, out_shape=tuple(out_shape), in_specs=[SMEM] * n_sm...  14.4 us
    all_to_all x1, starting transfers between devices, finish_tile(): return (tile, lax.all_to_all(sent, CHIPS, 0, 0, tiled=True), losses)  10.9 us
  transfers between devices with their start and end apart: 17, of which 11 were waited for; matrix products, arithmetic and copies ran while one was open for 0% of the time, Pallas kernels for 6%

profile of v6, /device:TPU:1, one launch (start us, length us, event | category | flops | bytes accessed | tf_op | source)
XLA Modules:
  0.0 225.7 jit_solution(12585007383232820716)
XLA Ops:
  0.6 0.0 copy-start
  0.6 0.0 copy-start.24
  0.7 0.0 copy-start.21
  0.7 0.0 copy-start.23
  0.7 0.0 copy-start.20
  0.7 1.2 slice.6
  1.9 1.3 collective-permute-start
  3.2 3.3 %collective-permute-start.2 = (f32[2,256,256]{2,1,0:T(8,128)S(1)}, f32[2,256,256]{2,1,0:T(8,128)S(1)}, u32[]{:S(2)}, u32[]{:S(2)}) collective-permute-start(f32[2,256,256]{2,1,0:T(8,128)S(1)} %slice.6), channel_id=1, source_target_pairs={{1,0},{2,1},{3,2},{4,3},{5,4},{6,5},{7,6},{9,8},{10,9},{11,10},{12... | collective-permute-start | bytes 1572872 | tf_op jit(solution)/shard_map/ppermute | solution.py:445
  6.6 1.3 collective-permute-start.1
  7.9 9.3 %collective-permute-done.refs_3_.below0 = f32[2,256,256]{2,1,0:T(8,128)S(1)} collective-permute-done((f32[2,256,256]{2,1,0:T(8,128)S(1)}, f32[2,256,256]{2,1,0:T(8,128)S(1)}, u32[]{:S(2)}, u32[]{:S(2)}) %collective-permute-start) | collective-permute-done | bytes 524320 | tf_op jit(solution)/shard_map/ppermute | solution.py:445
  17.2 4.8 %collective-permute-start.3 = (f32[2,256,256]{2,1,0:T(8,128)S(1)}, f32[2,256,256]{2,1,0:T(8,128)S(1)}, u32[]{:S(2)}, u32[]{:S(2)}) collective-permute-start(f32[2,256,256]{2,1,0:T(8,128)S(1)} %collective-permute-done.refs_3_.below0), channel_id=1, source_target_pairs={{1,0},{2,1},{3,2},{4,3},{5,4},{6,5},{7,6},{9,8},{10,9},{11,10},{12... | collective-permute-start | bytes 1572872 | tf_op jit(solution)/shard_map/ppermute | solution.py:445
  21.9 6.5 %collective-permute-done.1.refs_4_.below1 = f32[2,256,256]{2,1,0:T(8,128)S(1)} collective-permute-done((f32[2,256,256]{2,1,0:T(8,128)S(1)}, f32[2,256,256]{2,1,0:T(8,128)S(1)}, u32[]{:S(2)}, u32[]{:S(2)}) %collective-permute-start.1) | collective-permute-done | bytes 524320 | tf_op jit(solution)/shard_map/ppermute | solution.py:445
  28.4 0.0 collective-permute-done.2.refs_5_.rim
  28.4 2.0 collective-permute-done.3.refs_6_.diag
  30.4 14.0 %shard_map.94 = (f32[2,2,264,256]{3,2,1,0:T(8,128)}, f32[6,256,128]{2,1,0:T(8,128)S(1)}, f32[6,256,128]{2,1,0:T(8,128)S(1)}, f32[8,128]{1,0:T(8,128)S(1)}) custom-call(s32[2,2,2]{2,1,0:T(2,128)S(1)} %bitcast.14, s32[2]{0:T(128)S(1)} %bitcast.18, f32[2,256,512]{2,1,0:T(8,128)S(1)} %copy-done, f32[2,256,256]{2,1,0:T(8,128)S(1)} %collective-permute-done.refs_3_.below0, ...), custom_call_target="tpu_custom_call" | custom-call | flops 8000000000 | bytes 12000000 | tf_op jit(solution)/shard_map/pallas_call | solution.py:299
  44.5 0.1 collective-permute-start.4
  44.6 1.3 collective-permute-start.6
  45.9 4.1 %collective-permute-start.5 = (f32[2,2,264,256]{3,2,1,0:T(8,128)}, f32[2,2,264,256]{3,2,1,0:T(8,128)S(1)}, u32[]{:S(2)}, u32[]{:S(2)}) collective-permute-start(f32[2,2,264,256]{3,2,1,0:T(8,128)} %get-tuple-element.48.refs_0_), channel_id=1, source_target_pairs={{0,8},{8,16},{16,24},{24,32},{32,40},{40,48},{48,56},{56,64},{64,7... | collective-permute-start | bytes 3244040 | tf_op jit(solution)/shard_map/ppermute | solution.py:445
  49.9 0.0 collective-permute-done.4.other
  49.9 0.1 shard_map.95
  50.1 0.0 copy-start.5
  50.1 16.1 %all_to_all.30.parts = f32[4,384,128]{2,1,0:T(8,128)S(1)} all-to-all(f32[4,384,128]{2,1,0:T(8,128)S(1)} %bitcast.10), channel_id=1, replica_groups=mesh['row'=16,'layer'=4,'core'=2] {'layer'}, dimensions={0} | all-to-all | bytes 1572864 | tf_op jit(solution)/shard_map/all_to_all | solution.py:472
  66.1 0.7 shard_map.96
  66.8 10.8 %all-to-all-start.1 = ((f32[16,24,128]{2,1,0:T(8,128)}), f32[16,24,128]{2,1,0:T(8,128)S(1)}, u32[]{:S(2)}, u32[]{:S(2)}) async-start(f32[16,24,128]{2,1,0:T(8,128)} %bitcast.5), calls=%async_computation.1 | async-start | bytes 393216 | tf_op jit(solution)/shard_map/all_to_all | solution.py:476
  77.7 1.0 copy-done.6
  78.7 1.2 copy-done.7
  80.0 2.8 %shard_map.97 = (f32[2,2,256,256]{3,2,1,0:T(8,128)S(1)}, f32[2,2,256,256]{3,2,1,0:T(8,128)S(1)}, f32[2,2,256,256]{3,2,1,0:T(8,128)S(1)}) custom-call(f32[2,2,264,256]{3,2,1,0:T(8,128)S(1)} %copy-done.5, f32[2,2,264,256]{3,2,1,0:T(8,128)S(1)} %copy-done.7, f32[2,2,264,256]{3,2,1,0:T(8,128)} %collective-permute-done.6.refs_2_, ...), custom_call_target="tpu_custom_call" | custom-call | flops 10000000 | bytes 6393856 | tf_op jit(solution)/shard_map/pallas_call | solution.py:281
  82.7 0.0 copy-start.9
  82.8 1.0 copy-done.9
  83.7 1.0 all-to-all-done.1.parts
  84.7 5.2 %collective-permute-start.7 = (f32[2,2,256,256]{3,2,1,0:T(8,128)}, f32[2,2,256,256]{3,2,1,0:T(8,128)S(1)}, u32[]{:S(2)}, u32[]{:S(2)}) collective-permute-start(f32[2,2,256,256]{3,2,1,0:T(8,128)} %copy-done.9), channel_id=1, source_target_pairs={{0,1},{1,2},{2,3},{3,4},{4,5},{5,6},{6,7},{8,9},{9,10},{10,11},{11... | collective-permute-start | bytes 3145736 | tf_op jit(solution)/shard_map/ppermute | solution.py:445
  90.0 1.9 collective-permute-start.8
  91.9 10.1 %collective-permute-done.7.from_left.left = f32[2,2,256,256]{3,2,1,0:T(8,128)S(1)} collective-permute-done((f32[2,2,256,256]{3,2,1,0:T(8,128)}, f32[2,2,256,256]{3,2,1,0:T(8,128)S(1)}, u32[]{:S(2)}, u32[]{:S(2)}) %collective-permute-start.7) | collective-permute-done | bytes 1048608 | tf_op jit(solution)/shard_map/ppermute | solution.py:445
  102.0 0.9 shard_map.98
  102.9 0.2 copy-done.4
  103.1 1.0 copy-done.10
  104.0 1.0 copy-done.11
  105.0 10.9 %all-to-all-start.2 = ((f32[64,32,128]{2,1,0:T(8,128)}), f32[64,32,128]{2,1,0:T(8,128)S(1)}, u32[]{:S(2)}, u32[]{:S(2)}) async-start(f32[64,32,128]{2,1,0:T(8,128)} %copy-done.10), calls=%async_computation.2 | async-start | bytes 2097152 | tf_op jit(solution)/shard_map/all_to_all | solution.py:482
  115.9 7.6 %shard_map.99 = (f32[2,2,256,256]{3,2,1,0:T(8,128)}, f32[2,2,256,256]{3,2,1,0:T(8,128)}) custom-call(s32[2,2,2]{2,1,0:T(2,128)} %bitcast.12, f32[2,256,512]{2,1,0:T(8,128)} %refs_3_.1, f32[2,256,256]{2,1,0:T(8,128)} %copy-done.14, f32[2,256,256]{2,1,0:T(8,128)} %copy-done.16, f32[2,256,256]{2,1,0:T(8,128)} %copy-done.15, f32[2,256,256]{2,1,0:T(8,128)} %copy-done.17, ...), custom_call_target="tpu_custom_call" | custom-call | flops 10000000 | bytes 10485792 | tf_op jit(solution)/shard_map/pallas_call | solution.py:281
  123.5 9.0 %all-to-all-done.2.refs_2_ = f32[64,32,128]{2,1,0:T(8,128)S(1)} async-done(((f32[64,32,128]{2,1,0:T(8,128)}), f32[64,32,128]{2,1,0:T(8,128)S(1)}, u32[]{:S(2)}, u32[]{:S(2)}) %all-to-all-start.2) | async-done | bytes 1048608 | tf_op jit(solution)/shard_map/all_to_all | solution.py:482
  132.6 3.0 %collective-permute-start.9 = (f32[64,32,128]{2,1,0:T(8,128)S(1)}, f32[64,32,128]{2,1,0:T(8,128)S(1)}, u32[]{:S(2)}, u32[]{:S(2)}) collective-permute-start(f32[64,32,128]{2,1,0:T(8,128)S(1)} %all-to-all-done.2.refs_2_), channel_id=1, source_target_pairs={{0,1},{1,0},{2,3},{3,2},{4,5},{5,4},{6,7},{7,6},{8,9},{9,8},{10,11... | collective-permute-start | bytes 3145736 | tf_op jit(solution)/shard_map/ppermute | solution.py:468
  135.6 2.3 %collective-permute-done.9.refs_3_ = f32[64,32,128]{2,1,0:T(8,128)S(1)} collective-permute-done((f32[64,32,128]{2,1,0:T(8,128)S(1)}, f32[64,32,128]{2,1,0:T(8,128)S(1)}, u32[]{:S(2)}, u32[]{:S(2)}) %collective-permute-start.9) | collective-permute-done | bytes 1048608 | tf_op jit(solution)/shard_map/ppermute | solution.py:468
  137.9 1.0 copy-done.26
  138.9 12.9 %shard_map.100 = (f32[2,2,264,256]{3,2,1,0:T(8,128)}, f32[6,256,128]{2,1,0:T(8,128)}, f32[6,256,128]{2,1,0:T(8,128)}, f32[6,256,256]{2,1,0:T(8,128)}, f32[8,128]{1,0:T(8,128)}, /*index=5*/f32[8,128]{1,0:T(8,128)}) custom-call(s32[2,2,2]{2,1,0:T(2,128)} %bitcast.13, s32[2]{0:T(128)} %bitcast.17, f32[64,32,128]{2,1,0:T(8,128)} %copy-done.25, ...), custom_call_target="tpu_custom_call" | custom-call | flops 8000000000 | bytes 12000000 | tf_op jit(solution)/shard_map/pallas_call | solution.py:299
  151.8 0.5 collective-permute-start.10
  152.3 2.4 %collective-permute-start.11 = (f32[2,2,264,256]{3,2,1,0:T(8,128)}, f32[2,2,264,256]{3,2,1,0:T(8,128)S(1)}, u32[]{:S(2)}, u32[]{:S(2)}) collective-permute-start(f32[2,2,264,256]{3,2,1,0:T(8,128)} %get-tuple-element.68.refs_0_), channel_id=1, source_target_pairs={{0,8},{8,16},{16,24},{24,32},{32,40},{40,48},{48,56},{56,64},{64,7... | collective-permute-start | bytes 3244040 | tf_op jit(solution)/shard_map/ppermute | solution.py:445
  154.7 1.1 copy-done.13
  155.8 0.1 shard_map.101
  155.9 0.0 copy-start.8
  155.9 14.5 %all_to_all.31.parts = f32[4,384,128]{2,1,0:T(8,128)S(1)} all-to-all(f32[4,384,128]{2,1,0:T(8,128)S(1)} %bitcast.11), channel_id=1, replica_groups=mesh['row'=16,'layer'=4,'core'=2] {'layer'}, dimensions={0} | all-to-all | bytes 1572864 | tf_op jit(solution)/shard_map/all_to_all | solution.py:472
  170.4 0.7 shard_map.102
  171.2 4.4 %all-to-all-start.4 = ((f32[16,24,128]{2,1,0:T(8,128)}), f32[16,24,128]{2,1,0:T(8,128)S(1)}, u32[]{:S(2)}, u32[]{:S(2)}) async-start(f32[16,24,128]{2,1,0:T(8,128)} %bitcast.7), calls=%async_computation.4 | async-start | bytes 393216 | tf_op jit(solution)/shard_map/all_to_all | solution.py:476
  175.6 2.5 %collective-permute-done.11.refs_1_ = f32[2,2,264,256]{3,2,1,0:T(8,128)S(1)} collective-permute-done((f32[2,2,264,256]{3,2,1,0:T(8,128)}, f32[2,2,264,256]{3,2,1,0:T(8,128)S(1)}, u32[]{:S(2)}, u32[]{:S(2)}) %collective-permute-start.11) | collective-permute-done | bytes 1081376 | tf_op jit(solution)/shard_map/ppermute | solution.py:445
  178.1 0.8 shard_map.103
  178.9 0.0 copy-start.22
  178.9 0.8 copy-done.22
  179.7 3.2 %all-to-all-done.4.parts = f32[16,24,128]{2,1,0:T(8,128)S(1)} async-done(((f32[16,24,128]{2,1,0:T(8,128)}), f32[16,24,128]{2,1,0:T(8,128)S(1)}, u32[]{:S(2)}, u32[]{:S(2)}) %all-to-all-start.4) | async-done | bytes 196640 | tf_op jit(solution)/shard_map/all_to_all | solution.py:476
  182.9 4.4 %collective-permute-start.12 = (f32[1,2,256,256]{3,2,1,0:T(8,128)}, f32[1,2,256,256]{3,2,1,0:T(8,128)S(1)}, u32[]{:S(2)}, u32[]{:S(2)}) collective-permute-start(f32[1,2,256,256]{3,2,1,0:T(8,128)} %copy-done.22), channel_id=1, source_target_pairs={{0,1},{1,2},{2,3},{3,4},{4,5},{5,6},{6,7},{8,9},{9,10},{10,11},{11... | collective-permute-start | bytes 1572872 | tf_op jit(solution)/shard_map/ppermute | solution.py:445
  187.3 6.4 %collective-permute-done.12.from_left = f32[1,2,256,256]{3,2,1,0:T(8,128)S(1)} collective-permute-done((f32[1,2,256,256]{3,2,1,0:T(8,128)}, f32[1,2,256,256]{3,2,1,0:T(8,128)S(1)}, u32[]{:S(2)}, u32[]{:S(2)}) %collective-permute-start.12) | collective-permute-done | bytes 524320 | tf_op jit(solution)/shard_map/ppermute | solution.py:445
  193.7 0.8 shard_map.104
  194.5 22.4 %all_to_all.32.refs_0_ = f32[64,32,128]{2,1,0:T(8,128)S(1)} all-to-all(f32[64,32,128]{2,1,0:T(8,128)S(1)} %get-tuple-element.78), channel_id=1, replica_groups=mesh['row'=16,'layer'=4,'core'=2] {'layer','row'}, dimensions={0} | all-to-all | bytes 2097152 | tf_op jit(solution)/shard_map/all_to_all | solution.py:482
  216.9 3.0 %collective-permute-start.13 = (f32[64,32,128]{2,1,0:T(8,128)S(1)}, f32[64,32,128]{2,1,0:T(8,128)S(1)}, u32[]{:S(2)}, u32[]{:S(2)}) collective-permute-start(f32[64,32,128]{2,1,0:T(8,128)S(1)} %all_to_all.32.refs_0_), channel_id=1, source_target_pairs={{0,1},{1,0},{2,3},{3,2},{4,5},{5,4},{6,7},{7,6},{8,9},{9,8},{10,11... | collective-permute-start | bytes 3145736 | tf_op jit(solution)/shard_map/ppermute | solution.py:468
  220.0 2.3 %collective-permute-done.13.refs_1_ = f32[64,32,128]{2,1,0:T(8,128)S(1)} collective-permute-done((f32[64,32,128]{2,1,0:T(8,128)S(1)}, f32[64,32,128]{2,1,0:T(8,128)S(1)}, u32[]{:S(2)}, u32[]{:S(2)}) %collective-permute-start.13) | collective-permute-done | bytes 1048608 | tf_op jit(solution)/shard_map/ppermute | solution.py:468
  222.3 3.3 %shard_map.105 = (f32[2,256,512]{2,1,0:T(8,128)}, f32[6,256,256]{2,1,0:T(8,128)}) custom-call(f32[8,128]{1,0:T(8,128)S(1)} %copy-done.18, f32[64,32,128]{2,1,0:T(8,128)S(1)} %all_to_all.32.refs_0_, f32[64,32,128]{2,1,0:T(8,128)S(1)} %collective-permute-done.13.refs_1_, f32[6,256,256]{2,1,0:T(8,128)} %get-tuple-element.79.refs_2_, ...), custom_call_target="tpu_custom_call" | custom-call | flops 10000000 | bytes 9000000 | tf_op jit(solution)/shard_map/pallas_call | solution.py:426
  (41 shorter events, 0.1 us)
Async XLA Ops:
  0.6 5.9 %copy-start = (f32[2,256,512]{2,1,0:T(8,128)S(1)}, f32[2,256,512]{2,1,0:T(8,128)}, u32[]{:S(2)}) copy-start(f32[2,256,512]{2,1,0:T(8,128)} %refs_3_.1) | copy-start | bytes 3145732
  0.6 29.7 %copy-start.24 = (bf16[2,256,256]{2,1,0:T(8,128)(2,1)S(1)}, bf16[2,256,256]{2,1,0:T(8,128)(2,1)}, u32[]{:S(2)}) copy-start(bf16[2,256,256]{2,1,0:T(8,128)(2,1)} %constant.5.clone.refs_10_.refs_9_) | copy-start | bytes 786436
  0.7 29.7 %copy-start.21 = (bf16[2,1,1,2,256,256]{5,4,3,2,1,0:T(8,128)(2,1)S(1)}, bf16[2,1,1,2,256,256]{5,4,3,2,1,0:T(8,128)(2,1)}, u32[]{:S(2)}) copy-start(bf16[2,1,1,2,256,256]{5,4,3,2,1,0:T(8,128)(2,1)} %param.11) | copy-start | bytes 1572868
  0.7 29.7 %copy-start.23 = (s32[2,1,1]{0,2,1:T(1,128)S(1)}, s32[2,1,1]{0,2,1:T(1,128)}, u32[]{:S(2)}) copy-start(s32[2,1,1]{0,2,1:T(1,128)} %param.10) | copy-start | bytes 28
  0.7 29.7 %copy-start.20 = (s32[2,1,1,2,2]{4,3,2,1,0:T(2,128)S(1)}, s32[2,1,1,2,2]{4,3,2,1,0:T(2,128)}, u32[]{:S(2)}) copy-start(s32[2,1,1,2,2]{4,3,2,1,0:T(2,128)} %param.9) | copy-start | bytes 100
  1.9 15.3 %collective-permute-start = (f32[2,256,256]{2,1,0:T(8,128)S(1)}, f32[2,256,256]{2,1,0:T(8,128)S(1)}, u32[]{:S(2)}, u32[]{:S(2)}) collective-permute-start(f32[2,256,256]{2,1,0:T(8,128)S(1)} %slice.6), channel_id=1, source_target_pairs={{8,0},{16,8},{24,16},{32,24},{40,32},{48,40},{56,48},{64,56},{72,6... | collective-permute-start | bytes 1572872 | tf_op jit(solution)/shard_map/ppermute | solution.py:445
  3.2 25.2 %collective-permute-start.2 = (f32[2,256,256]{2,1,0:T(8,128)S(1)}, f32[2,256,256]{2,1,0:T(8,128)S(1)}, u32[]{:S(2)}, u32[]{:S(2)}) collective-permute-start(f32[2,256,256]{2,1,0:T(8,128)S(1)} %slice.6), channel_id=1, source_target_pairs={{1,0},{2,1},{3,2},{4,3},{5,4},{6,5},{7,6},{9,8},{10,9},{11,10},{12... | collective-permute-start | bytes 1572872 | tf_op jit(solution)/shard_map/ppermute | solution.py:445
  6.6 21.8 %collective-permute-start.1 = (f32[2,256,256]{2,1,0:T(8,128)S(1)}, f32[2,256,256]{2,1,0:T(8,128)S(1)}, u32[]{:S(2)}, u32[]{:S(2)}) collective-permute-start(f32[2,256,256]{2,1,0:T(8,128)S(1)} %slice.7), channel_id=1, source_target_pairs={{8,0},{16,8},{24,16},{32,24},{40,32},{48,40},{56,48},{64,56},{72,6... | collective-permute-start | bytes 1572872 | tf_op jit(solution)/shard_map/ppermute | solution.py:445
  17.2 27.3 %copy-start.14 = (f32[2,256,256]{2,1,0:T(8,128)}, f32[2,256,256]{2,1,0:T(8,128)S(1)}, u32[]{:S(2)}) copy-start(f32[2,256,256]{2,1,0:T(8,128)S(1)} %collective-permute-done.refs_3_.below0) | copy-start | bytes 1572868
  17.2 13.2 %collective-permute-start.3 = (f32[2,256,256]{2,1,0:T(8,128)S(1)}, f32[2,256,256]{2,1,0:T(8,128)S(1)}, u32[]{:S(2)}, u32[]{:S(2)}) collective-permute-start(f32[2,256,256]{2,1,0:T(8,128)S(1)} %collective-permute-done.refs_3_.below0), channel_id=1, source_target_pairs={{1,0},{2,1},{3,2},{4,3},{5,4},{6,5},{7,6},{9,8},{10,9},{11,10},{12... | collective-permute-start | bytes 1572872 | tf_op jit(solution)/shard_map/ppermute | solution.py:445
  28.4 16.1 %copy-start.16 = (f32[2,256,256]{2,1,0:T(8,128)}, f32[2,256,256]{2,1,0:T(8,128)S(1)}, u32[]{:S(2)}) copy-start(f32[2,256,256]{2,1,0:T(8,128)S(1)} %collective-permute-done.1.refs_4_.below1) | copy-start | bytes 1572868
  28.4 16.1 %copy-start.15 = (f32[2,256,256]{2,1,0:T(8,128)}, f32[2,256,256]{2,1,0:T(8,128)S(1)}, u32[]{:S(2)}) copy-start(f32[2,256,256]{2,1,0:T(8,128)S(1)} %collective-permute-done.2.refs_5_.rim) | copy-start | bytes 1572868
  30.4 14.1 %copy-start.17 = (f32[2,256,256]{2,1,0:T(8,128)}, f32[2,256,256]{2,1,0:T(8,128)S(1)}, u32[]{:S(2)}) copy-start(f32[2,256,256]{2,1,0:T(8,128)S(1)} %collective-permute-done.3.refs_6_.diag) | copy-start | bytes 1572868
  44.5 5.5 %collective-permute-start.4 = (f32[6,256,128]{2,1,0:T(8,128)S(1)}, f32[6,256,128]{2,1,0:T(8,128)S(1)}, u32[]{:S(2)}, u32[]{:S(2)}) collective-permute-start(f32[6,256,128]{2,1,0:T(8,128)S(1)} %get-tuple-element.46), channel_id=1, source_target_pairs={{0,1},{1,0},{2,3},{3,2},{4,5},{5,4},{6,7},{7,6},{8,9},{9,8},{10,11... | collective-permute-start | bytes 2359304 | tf_op jit(solution)/shard_map/ppermute | solution.py:468
  44.6 33.1 %collective-permute-start.6 = (f32[2,2,264,256]{3,2,1,0:T(8,128)}, f32[2,2,264,256]{3,2,1,0:T(8,128)}, u32[]{:S(2)}, u32[]{:S(2)}) collective-permute-start(f32[2,2,264,256]{3,2,1,0:T(8,128)} %get-tuple-element.48.refs_0_), channel_id=1, source_target_pairs={{8,0},{16,8},{24,16},{32,24},{40,32},{48,40},{56,48},{64,56},{72,6... | collective-permute-start | bytes 3244040 | tf_op jit(solution)/shard_map/ppermute | solution.py:445
  45.9 31.8 %collective-permute-start.5 = (f32[2,2,264,256]{3,2,1,0:T(8,128)}, f32[2,2,264,256]{3,2,1,0:T(8,128)S(1)}, u32[]{:S(2)}, u32[]{:S(2)}) collective-permute-start(f32[2,2,264,256]{3,2,1,0:T(8,128)} %get-tuple-element.48.refs_0_), channel_id=1, source_target_pairs={{0,8},{8,16},{16,24},{24,32},{32,40},{40,48},{48,56},{56,64},{64,7... | collective-permute-start | bytes 3244040 | tf_op jit(solution)/shard_map/ppermute | solution.py:445
  50.1 28.7 %copy-start.5 = (f32[2,2,264,256]{3,2,1,0:T(8,128)S(1)}, f32[2,2,264,256]{3,2,1,0:T(8,128)}, u32[]{:S(2)}) copy-start(f32[2,2,264,256]{3,2,1,0:T(8,128)} %get-tuple-element.48.refs_0_) | copy-start | bytes 3244036
  66.8 17.9 %all-to-all-start.1 = ((f32[16,24,128]{2,1,0:T(8,128)}), f32[16,24,128]{2,1,0:T(8,128)S(1)}, u32[]{:S(2)}, u32[]{:S(2)}) async-start(f32[16,24,128]{2,1,0:T(8,128)} %bitcast.5), calls=%async_computation.1 | async-start | bytes 393216 | tf_op jit(solution)/shard_map/all_to_all | solution.py:476
  77.7 1.0 copy-start.6
  78.7 1.2 copy-start.7
  82.7 1.0 copy-start.9
  83.7 19.2 %copy-start.2 = (f32[2,2,256,256]{3,2,1,0:T(8,128)}, f32[2,2,256,256]{3,2,1,0:T(8,128)S(1)}, u32[]{:S(2)}) copy-start(f32[2,2,256,256]{3,2,1,0:T(8,128)S(1)} %get-tuple-element.53.block0) | copy-start | bytes 3145732
  83.7 19.2 %copy-start.3 = (f32[2,2,256,256]{3,2,1,0:T(8,128)}, f32[2,2,256,256]{3,2,1,0:T(8,128)S(1)}, u32[]{:S(2)}) copy-start(f32[2,2,256,256]{3,2,1,0:T(8,128)S(1)} %get-tuple-element.54.block1) | copy-start | bytes 3145732
  84.7 17.3 %collective-permute-start.7 = (f32[2,2,256,256]{3,2,1,0:T(8,128)}, f32[2,2,256,256]{3,2,1,0:T(8,128)S(1)}, u32[]{:S(2)}, u32[]{:S(2)}) collective-permute-start(f32[2,2,256,256]{3,2,1,0:T(8,128)} %copy-done.9), channel_id=1, source_target_pairs={{0,1},{1,2},{2,3},{3,4},{4,5},{5,6},{6,7},{8,9},{9,10},{10,11},{11... | collective-permute-start | bytes 3145736 | tf_op jit(solution)/shard_map/ppermute | solution.py:445
  90.0 26.0 %collective-permute-start.8 = (f32[2,2,256,256]{3,2,1,0:T(8,128)S(1)}, f32[2,2,256,256]{3,2,1,0:T(8,128)}, u32[]{:S(2)}, u32[]{:S(2)}) collective-permute-start(f32[2,2,256,256]{3,2,1,0:T(8,128)S(1)} %get-tuple-element.53.block0), channel_id=1, source_target_pairs={{1,0},{2,1},{3,2},{4,3},{5,4},{6,5},{7,6},{9,8},{10,9},{11,10},{12... | collective-permute-start | bytes 3145736 | tf_op jit(solution)/shard_map/ppermute | solution.py:445
  102.0 1.1 copy-start.4
  103.1 1.0 copy-start.10
  104.0 1.0 copy-start.11
  105.0 27.5 %all-to-all-start.2 = ((f32[64,32,128]{2,1,0:T(8,128)}), f32[64,32,128]{2,1,0:T(8,128)S(1)}, u32[]{:S(2)}, u32[]{:S(2)}) async-start(f32[64,32,128]{2,1,0:T(8,128)} %copy-done.10), calls=%async_computation.2 | async-start | bytes 2097152 | tf_op jit(solution)/shard_map/all_to_all | solution.py:482
  132.6 5.3 %copy-start.25 = (f32[64,32,128]{2,1,0:T(8,128)}, f32[64,32,128]{2,1,0:T(8,128)S(1)}, u32[]{:S(2)}) copy-start(f32[64,32,128]{2,1,0:T(8,128)S(1)} %all-to-all-done.2.refs_2_) | copy-start | bytes 3145732
  132.6 5.3 %collective-permute-start.9 = (f32[64,32,128]{2,1,0:T(8,128)S(1)}, f32[64,32,128]{2,1,0:T(8,128)S(1)}, u32[]{:S(2)}, u32[]{:S(2)}) collective-permute-start(f32[64,32,128]{2,1,0:T(8,128)S(1)} %all-to-all-done.2.refs_2_), channel_id=1, source_target_pairs={{0,1},{1,0},{2,3},{3,2},{4,5},{5,4},{6,7},{7,6},{8,9},{9,8},{10,11... | collective-permute-start | bytes 3145736 | tf_op jit(solution)/shard_map/ppermute | solution.py:468
  137.9 1.0 copy-start.26
  151.8 2.9 %collective-permute-start.10 = (f32[6,256,128]{2,1,0:T(8,128)}, f32[6,256,128]{2,1,0:T(8,128)S(1)}, u32[]{:S(2)}, u32[]{:S(2)}) collective-permute-start(f32[6,256,128]{2,1,0:T(8,128)} %get-tuple-element.66), channel_id=1, source_target_pairs={{0,1},{1,0},{2,3},{3,2},{4,5},{5,4},{6,7},{7,6},{8,9},{9,8},{10,11... | collective-permute-start | bytes 2359304 | tf_op jit(solution)/shard_map/ppermute | solution.py:468
  152.3 25.8 %collective-permute-start.11 = (f32[2,2,264,256]{3,2,1,0:T(8,128)}, f32[2,2,264,256]{3,2,1,0:T(8,128)S(1)}, u32[]{:S(2)}, u32[]{:S(2)}) collective-permute-start(f32[2,2,264,256]{3,2,1,0:T(8,128)} %get-tuple-element.68.refs_0_), channel_id=1, source_target_pairs={{0,8},{8,16},{16,24},{24,32},{32,40},{40,48},{48,56},{56,64},{64,7... | collective-permute-start | bytes 3244040 | tf_op jit(solution)/shard_map/ppermute | solution.py:445
  154.7 1.1 copy-start.13
  155.9 22.2 %copy-start.8 = (f32[2,2,264,256]{3,2,1,0:T(8,128)S(1)}, f32[2,2,264,256]{3,2,1,0:T(8,128)}, u32[]{:S(2)}) copy-start(f32[2,2,264,256]{3,2,1,0:T(8,128)} %get-tuple-element.68.refs_0_) | copy-start | bytes 3244036
  171.2 11.8 %all-to-all-start.4 = ((f32[16,24,128]{2,1,0:T(8,128)}), f32[16,24,128]{2,1,0:T(8,128)S(1)}, u32[]{:S(2)}, u32[]{:S(2)}) async-start(f32[16,24,128]{2,1,0:T(8,128)} %bitcast.7), calls=%async_computation.4 | async-start | bytes 393216 | tf_op jit(solution)/shard_map/all_to_all | solution.py:476
  178.1 15.6 %copy-start.19 = (f32[8,128]{1,0:T(8,128)S(1)}, f32[8,128]{1,0:T(8,128)}, u32[]{:S(2)}) copy-start(f32[8,128]{1,0:T(8,128)} %get-tuple-element.77.loss) | copy-start | bytes 12292
  178.9 0.8 copy-start.22
  182.9 10.8 %collective-permute-start.12 = (f32[1,2,256,256]{3,2,1,0:T(8,128)}, f32[1,2,256,256]{3,2,1,0:T(8,128)S(1)}, u32[]{:S(2)}, u32[]{:S(2)}) collective-permute-start(f32[1,2,256,256]{3,2,1,0:T(8,128)} %copy-done.22), channel_id=1, source_target_pairs={{0,1},{1,2},{2,3},{3,4},{4,5},{5,6},{6,7},{8,9},{9,10},{10,11},{11... | collective-permute-start | bytes 1572872 | tf_op jit(solution)/shard_map/ppermute | solution.py:445
  194.5 27.7 %copy-start.1 = (f32[2,256,512]{2,1,0:T(8,128)S(1)}, f32[2,256,512]{2,1,0:T(8,128)}, u32[]{:S(2)}) copy-start(f32[2,256,512]{2,1,0:T(8,128)} %refs_3_.1) | copy-start | bytes 3145732
  194.5 27.7 %copy-start.12 = (f32[2,256,512]{2,1,0:T(8,128)S(1)}, f32[2,256,512]{2,1,0:T(8,128)}, u32[]{:S(2)}) copy-start(f32[2,256,512]{2,1,0:T(8,128)} %copy-done.11) | copy-start | bytes 3145732
  194.5 27.7 %copy-start.18 = (f32[8,128]{1,0:T(8,128)S(1)}, f32[8,128]{1,0:T(8,128)}, u32[]{:S(2)}) copy-start(f32[8,128]{1,0:T(8,128)} %get-tuple-element.64.rate_first) | copy-start | bytes 12292
  216.9 5.3 %collective-permute-start.13 = (f32[64,32,128]{2,1,0:T(8,128)S(1)}, f32[64,32,128]{2,1,0:T(8,128)S(1)}, u32[]{:S(2)}, u32[]{:S(2)}) collective-permute-start(f32[64,32,128]{2,1,0:T(8,128)S(1)} %all_to_all.32.refs_0_), channel_id=1, source_target_pairs={{0,1},{1,0},{2,3},{3,2},{4,5},{5,4},{6,7},{7,6},{8,9},{9,8},{10,11... | collective-permute-start | bytes 3145736 | tf_op jit(solution)/shard_map/ppermute | solution.py:468

commit v7 on v6

--- a/solution.py
+++ b/solution.py
@@ -132,6 +132,14 @@
     direct = 5 if iteration == 0 else 0
     held = [*sources[:direct], *refs[11:]]
     fetch = [pltpu.make_async_copy(src, dst, sems.at[k]) for k, (src, dst) in enumerate(zip(sources[direct:], refs[11:]))]
+    by_mode = []
+    if iteration == 0:
+        for mode in range(MODES):
+            planes = pl.ds(2 * mode, 2)
+            by_mode.append(
+                pltpu.make_async_copy(sources[6].at[planes], held[6].at[planes], sems.at[len(fetch) + mode])
+            )
+        fetch[1:2] = by_mode
     for copy in fetch:
         copy.start()
     fetch = [None] * direct + fetch
@@ -175,9 +183,11 @@
                 obj[part] = patch[slot, part] - wide * patch_grad[slot, part]
 
         if slot == 0:
-            for copy in fetch[5:-2]:
+            for copy in fetch[5 : -2 - len(by_mode)]:
                 copy.wait()
         for mode in range(MODES):
+            if slot == 0 and by_mode:
+                by_mode[mode].wait()
             probe_re, probe_im = probe_ref[2 * mode], probe_ref[2 * mode + 1]
             exit_re = probe_re * obj[0] - probe_im * obj[1]
             exit_im = probe_re * obj[1] + probe_im * obj[0]
@@ -308,7 +318,7 @@
             pltpu.VMEM((2, WIN, HALF), F32),
             pltpu.VMEM((4 * MODES, WIN, HALF), F32),
             pltpu.VMEM((CAP, 2, WIN + INFO, WIN), F32),
-            pltpu.SemaphoreType.DMA((len(big),)),
+            pltpu.SemaphoreType.DMA((len(big) + MODES,)),
             pltpu.SemaphoreType.DMA((CAP,)),
             pltpu.SemaphoreType.DMA((4 * MODES,)),
             pltpu.SemaphoreType.DMA((1,)),

time: 227 us -> 227 us (level)
  no operation moved by 1% of the time
where the time goes in v7:
time: 227 us; the launch traced here: 226 us
  starting transfers between devices  62.8 us (28%)
  waiting for transfers between devices  54.6 us (24%)
  blocking collectives  53 us (23%)
  Pallas kernels  44.8 us (20%)
  local copies, waits for them, and re-layouts  9.6 us (4%)
    ppermute x10, waiting for transfers between devices, shift(): lax.ppermute(value, axis, [(source, source + steps) for source in range(f...  36.8 us
    all_to_all x2, blocking collectives, reduce_chips(): lax.all_to_all(value.reshape(layers, rows * CHUNK, HALF), 'layer', 0, 0,...  30.6 us
    ppermute x10, starting transfers between devices, shift(): lax.ppermute(value, axis, [(source, source + steps) for source in range(f...  30 us
    pallas_call x2, Pallas kernels, window_call(): pl.pallas_call(lambda *refs: window_kernel(iteration, *refs), out_shape=(...  27.1 us
    all_to_all x1, blocking collectives, finish_tile(): return (tile, lax.all_to_all(sent, CHIPS, 0, 0, tiled=True), losses)  22.4 us
    all_to_all x2, starting transfers between devices, reduce_rows(): lax.all_to_all(part.reshape(rows, CHUNK, HALF), 'row', 0, 0, tiled=True)  15.3 us
    pallas_call x9, Pallas kernels, call(): pl.pallas_call(kernel, out_shape=tuple(out_shape), in_specs=[SMEM] * n_sm...  14.4 us
    all_to_all x1, starting transfers between devices, finish_tile(): return (tile, lax.all_to_all(sent, CHIPS, 0, 0, tiled=True), losses)  10.9 us
  transfers between devices with their start and end apart: 17, of which 11 were waited for; matrix products, arithmetic and copies ran while one was open for 0% of the time, Pallas kernels for 6%

profile of v7, /device:TPU:1, one launch (start us, length us, event | category | flops | bytes accessed | tf_op | source)
XLA Modules:
  0.0 225.8 jit_solution(15693986701135065883)
XLA Ops:
  0.6 0.0 copy-start
  0.6 0.0 copy-start.24
  0.7 0.0 copy-start.21
  0.7 0.0 copy-start.23
  0.7 0.0 copy-start.20
  0.7 1.2 slice.6
  1.9 1.3 collective-permute-start
  3.2 3.3 %collective-permute-start.2 = (f32[2,256,256]{2,1,0:T(8,128)S(1)}, f32[2,256,256]{2,1,0:T(8,128)S(1)}, u32[]{:S(2)}, u32[]{:S(2)}) collective-permute-start(f32[2,256,256]{2,1,0:T(8,128)S(1)} %slice.6), channel_id=1, source_target_pairs={{1,0},{2,1},{3,2},{4,3},{5,4},{6,5},{7,6},{9,8},{10,9},{11,10},{12... | collective-permute-start | bytes 1572872 | tf_op jit(solution)/shard_map/ppermute | solution.py:455
  6.6 1.3 collective-permute-start.1
  7.9 9.3 %collective-permute-done.refs_3_.below0 = f32[2,256,256]{2,1,0:T(8,128)S(1)} collective-permute-done((f32[2,256,256]{2,1,0:T(8,128)S(1)}, f32[2,256,256]{2,1,0:T(8,128)S(1)}, u32[]{:S(2)}, u32[]{:S(2)}) %collective-permute-start) | collective-permute-done | bytes 524320 | tf_op jit(solution)/shard_map/ppermute | solution.py:455
  17.2 4.8 %collective-permute-start.3 = (f32[2,256,256]{2,1,0:T(8,128)S(1)}, f32[2,256,256]{2,1,0:T(8,128)S(1)}, u32[]{:S(2)}, u32[]{:S(2)}) collective-permute-start(f32[2,256,256]{2,1,0:T(8,128)S(1)} %collective-permute-done.refs_3_.below0), channel_id=1, source_target_pairs={{1,0},{2,1},{3,2},{4,3},{5,4},{6,5},{7,6},{9,8},{10,9},{11,10},{12... | collective-permute-start | bytes 1572872 | tf_op jit(solution)/shard_map/ppermute | solution.py:455
  21.9 6.5 %collective-permute-done.1.refs_4_.below1 = f32[2,256,256]{2,1,0:T(8,128)S(1)} collective-permute-done((f32[2,256,256]{2,1,0:T(8,128)S(1)}, f32[2,256,256]{2,1,0:T(8,128)S(1)}, u32[]{:S(2)}, u32[]{:S(2)}) %collective-permute-start.1) | collective-permute-done | bytes 524320 | tf_op jit(solution)/shard_map/ppermute | solution.py:455
  28.4 0.0 collective-permute-done.2.refs_5_.rim
  28.4 2.0 collective-permute-done.3.refs_6_.diag
  30.4 14.1 %shard_map.94 = (f32[2,2,264,256]{3,2,1,0:T(8,128)}, f32[6,256,128]{2,1,0:T(8,128)S(1)}, f32[6,256,128]{2,1,0:T(8,128)S(1)}, f32[8,128]{1,0:T(8,128)S(1)}) custom-call(s32[2,2,2]{2,1,0:T(2,128)S(1)} %bitcast.14, s32[2]{0:T(128)S(1)} %bitcast.18, f32[2,256,512]{2,1,0:T(8,128)S(1)} %copy-done, f32[2,256,256]{2,1,0:T(8,128)S(1)} %collective-permute-done.refs_3_.below0, ...), custom_call_target="tpu_custom_call" | custom-call | flops 8000000000 | bytes 12000000 | tf_op jit(solution)/shard_map/pallas_call | solution.py:309
  44.6 0.1 collective-permute-start.4
  44.7 1.3 collective-permute-start.6
  46.0 4.1 %collective-permute-start.5 = (f32[2,2,264,256]{3,2,1,0:T(8,128)}, f32[2,2,264,256]{3,2,1,0:T(8,128)S(1)}, u32[]{:S(2)}, u32[]{:S(2)}) collective-permute-start(f32[2,2,264,256]{3,2,1,0:T(8,128)} %get-tuple-element.48.refs_0_), channel_id=1, source_target_pairs={{0,8},{8,16},{16,24},{24,32},{32,40},{40,48},{48,56},{56,64},{64,7... | collective-permute-start | bytes 3244040 | tf_op jit(solution)/shard_map/ppermute | solution.py:455
  50.0 0.0 collective-permute-done.4.other
  50.0 0.1 shard_map.95
  50.1 0.0 copy-start.5
  50.2 16.1 %all_to_all.30.parts = f32[4,384,128]{2,1,0:T(8,128)S(1)} all-to-all(f32[4,384,128]{2,1,0:T(8,128)S(1)} %bitcast.10), channel_id=1, replica_groups=mesh['row'=16,'layer'=4,'core'=2] {'layer'}, dimensions={0} | all-to-all | bytes 1572864 | tf_op jit(solution)/shard_map/all_to_all | solution.py:482
  66.2 0.7 shard_map.96
  66.9 10.8 %all-to-all-start.1 = ((f32[16,24,128]{2,1,0:T(8,128)}), f32[16,24,128]{2,1,0:T(8,128)S(1)}, u32[]{:S(2)}, u32[]{:S(2)}) async-start(f32[16,24,128]{2,1,0:T(8,128)} %bitcast.5), calls=%async_computation.1 | async-start | bytes 393216 | tf_op jit(solution)/shard_map/all_to_all | solution.py:486
  77.8 1.0 copy-done.6
  78.8 1.2 copy-done.7
  80.1 2.8 %shard_map.97 = (f32[2,2,256,256]{3,2,1,0:T(8,128)S(1)}, f32[2,2,256,256]{3,2,1,0:T(8,128)S(1)}, f32[2,2,256,256]{3,2,1,0:T(8,128)S(1)}) custom-call(f32[2,2,264,256]{3,2,1,0:T(8,128)S(1)} %copy-done.5, f32[2,2,264,256]{3,2,1,0:T(8,128)S(1)} %copy-done.7, f32[2,2,264,256]{3,2,1,0:T(8,128)} %collective-permute-done.6.refs_2_, ...), custom_call_target="tpu_custom_call" | custom-call | flops 10000000 | bytes 6393856 | tf_op jit(solution)/shard_map/pallas_call | solution.py:291
  82.8 0.0 copy-start.9
  82.9 1.0 copy-done.9
  83.8 1.0 all-to-all-done.1.parts
  84.8 5.2 %collective-permute-start.7 = (f32[2,2,256,256]{3,2,1,0:T(8,128)}, f32[2,2,256,256]{3,2,1,0:T(8,128)S(1)}, u32[]{:S(2)}, u32[]{:S(2)}) collective-permute-start(f32[2,2,256,256]{3,2,1,0:T(8,128)} %copy-done.9), channel_id=1, source_target_pairs={{0,1},{1,2},{2,3},{3,4},{4,5},{5,6},{6,7},{8,9},{9,10},{10,11},{11... | collective-permute-start | bytes 3145736 | tf_op jit(solution)/shard_map/ppermute | solution.py:455
  90.1 1.9 collective-permute-start.8
  92.0 10.1 %collective-permute-done.7.from_left.left = f32[2,2,256,256]{3,2,1,0:T(8,128)S(1)} collective-permute-done((f32[2,2,256,256]{3,2,1,0:T(8,128)}, f32[2,2,256,256]{3,2,1,0:T(8,128)S(1)}, u32[]{:S(2)}, u32[]{:S(2)}) %collective-permute-start.7) | collective-permute-done | bytes 1048608 | tf_op jit(solution)/shard_map/ppermute | solution.py:455
  102.1 0.9 shard_map.98
  103.0 0.2 copy-done.4
  103.2 1.0 copy-done.10
  104.1 1.0 copy-done.11
  105.1 10.9 %all-to-all-start.2 = ((f32[64,32,128]{2,1,0:T(8,128)}), f32[64,32,128]{2,1,0:T(8,128)S(1)}, u32[]{:S(2)}, u32[]{:S(2)}) async-start(f32[64,32,128]{2,1,0:T(8,128)} %copy-done.10), calls=%async_computation.2 | async-start | bytes 2097152 | tf_op jit(solution)/shard_map/all_to_all | solution.py:492
  116.0 7.6 %shard_map.99 = (f32[2,2,256,256]{3,2,1,0:T(8,128)}, f32[2,2,256,256]{3,2,1,0:T(8,128)}) custom-call(s32[2,2,2]{2,1,0:T(2,128)} %bitcast.12, f32[2,256,512]{2,1,0:T(8,128)} %refs_3_.1, f32[2,256,256]{2,1,0:T(8,128)} %copy-done.14, f32[2,256,256]{2,1,0:T(8,128)} %copy-done.16, f32[2,256,256]{2,1,0:T(8,128)} %copy-done.15, f32[2,256,256]{2,1,0:T(8,128)} %copy-done.17, ...), custom_call_target="tpu_custom_call" | custom-call | flops 10000000 | bytes 10485792 | tf_op jit(solution)/shard_map/pallas_call | solution.py:291
  123.6 9.0 %all-to-all-done.2.refs_2_ = f32[64,32,128]{2,1,0:T(8,128)S(1)} async-done(((f32[64,32,128]{2,1,0:T(8,128)}), f32[64,32,128]{2,1,0:T(8,128)S(1)}, u32[]{:S(2)}, u32[]{:S(2)}) %all-to-all-start.2) | async-done | bytes 1048608 | tf_op jit(solution)/shard_map/all_to_all | solution.py:492
  132.6 3.0 %collective-permute-start.9 = (f32[64,32,128]{2,1,0:T(8,128)S(1)}, f32[64,32,128]{2,1,0:T(8,128)S(1)}, u32[]{:S(2)}, u32[]{:S(2)}) collective-permute-start(f32[64,32,128]{2,1,0:T(8,128)S(1)} %all-to-all-done.2.refs_2_), channel_id=1, source_target_pairs={{0,1},{1,0},{2,3},{3,2},{4,5},{5,4},{6,7},{7,6},{8,9},{9,8},{10,11... | collective-permute-start | bytes 3145736 | tf_op jit(solution)/shard_map/ppermute | solution.py:478
  135.7 2.3 %collective-permute-done.9.refs_3_ = f32[64,32,128]{2,1,0:T(8,128)S(1)} collective-permute-done((f32[64,32,128]{2,1,0:T(8,128)S(1)}, f32[64,32,128]{2,1,0:T(8,128)S(1)}, u32[]{:S(2)}, u32[]{:S(2)}) %collective-permute-start.9) | collective-permute-done | bytes 1048608 | tf_op jit(solution)/shard_map/ppermute | solution.py:478
  138.0 1.0 copy-done.26
  138.9 13.0 %shard_map.100 = (f32[2,2,264,256]{3,2,1,0:T(8,128)}, f32[6,256,128]{2,1,0:T(8,128)}, f32[6,256,128]{2,1,0:T(8,128)}, f32[6,256,256]{2,1,0:T(8,128)}, f32[8,128]{1,0:T(8,128)}, /*index=5*/f32[8,128]{1,0:T(8,128)}) custom-call(s32[2,2,2]{2,1,0:T(2,128)} %bitcast.13, s32[2]{0:T(128)} %bitcast.17, f32[64,32,128]{2,1,0:T(8,128)} %copy-done.25, ...), custom_call_target="tpu_custom_call" | custom-call | flops 8000000000 | bytes 12000000 | tf_op jit(solution)/shard_map/pallas_call | solution.py:309
  151.9 0.5 collective-permute-start.10
  152.4 2.4 %collective-permute-start.11 = (f32[2,2,264,256]{3,2,1,0:T(8,128)}, f32[2,2,264,256]{3,2,1,0:T(8,128)S(1)}, u32[]{:S(2)}, u32[]{:S(2)}) collective-permute-start(f32[2,2,264,256]{3,2,1,0:T(8,128)} %get-tuple-element.68.refs_0_), channel_id=1, source_target_pairs={{0,8},{8,16},{16,24},{24,32},{32,40},{40,48},{48,56},{56,64},{64,7... | collective-permute-start | bytes 3244040 | tf_op jit(solution)/shard_map/ppermute | solution.py:455
  154.8 1.1 copy-done.13
  155.9 0.1 shard_map.101
  156.0 0.0 copy-start.8
  156.0 14.5 %all_to_all.31.parts = f32[4,384,128]{2,1,0:T(8,128)S(1)} all-to-all(f32[4,384,128]{2,1,0:T(8,128)S(1)} %bitcast.11), channel_id=1, replica_groups=mesh['row'=16,'layer'=4,'core'=2] {'layer'}, dimensions={0} | all-to-all | bytes 1572864 | tf_op jit(solution)/shard_map/all_to_all | solution.py:482
  170.5 0.7 shard_map.102
  171.2 4.4 %all-to-all-start.4 = ((f32[16,24,128]{2,1,0:T(8,128)}), f32[16,24,128]{2,1,0:T(8,128)S(1)}, u32[]{:S(2)}, u32[]{:S(2)}) async-start(f32[16,24,128]{2,1,0:T(8,128)} %bitcast.7), calls=%async_computation.4 | async-start | bytes 393216 | tf_op jit(solution)/shard_map/all_to_all | solution.py:486
  175.7 2.5 %collective-permute-done.11.refs_1_ = f32[2,2,264,256]{3,2,1,0:T(8,128)S(1)} collective-permute-done((f32[2,2,264,256]{3,2,1,0:T(8,128)}, f32[2,2,264,256]{3,2,1,0:T(8,128)S(1)}, u32[]{:S(2)}, u32[]{:S(2)}) %collective-permute-start.11) | collective-permute-done | bytes 1081376 | tf_op jit(solution)/shard_map/ppermute | solution.py:455
  178.2 0.8 shard_map.103
  179.0 0.0 copy-start.22
  179.0 0.8 copy-done.22
  179.8 3.2 %all-to-all-done.4.parts = f32[16,24,128]{2,1,0:T(8,128)S(1)} async-done(((f32[16,24,128]{2,1,0:T(8,128)}), f32[16,24,128]{2,1,0:T(8,128)S(1)}, u32[]{:S(2)}, u32[]{:S(2)}) %all-to-all-start.4) | async-done | bytes 196640 | tf_op jit(solution)/shard_map/all_to_all | solution.py:486
  183.0 4.4 %collective-permute-start.12 = (f32[1,2,256,256]{3,2,1,0:T(8,128)}, f32[1,2,256,256]{3,2,1,0:T(8,128)S(1)}, u32[]{:S(2)}, u32[]{:S(2)}) collective-permute-start(f32[1,2,256,256]{3,2,1,0:T(8,128)} %copy-done.22), channel_id=1, source_target_pairs={{0,1},{1,2},{2,3},{3,4},{4,5},{5,6},{6,7},{8,9},{9,10},{10,11},{11... | collective-permute-start | bytes 1572872 | tf_op jit(solution)/shard_map/ppermute | solution.py:455
  187.4 6.4 %collective-permute-done.12.from_left = f32[1,2,256,256]{3,2,1,0:T(8,128)S(1)} collective-permute-done((f32[1,2,256,256]{3,2,1,0:T(8,128)}, f32[1,2,256,256]{3,2,1,0:T(8,128)S(1)}, u32[]{:S(2)}, u32[]{:S(2)}) %collective-permute-start.12) | collective-permute-done | bytes 524320 | tf_op jit(solution)/shard_map/ppermute | solution.py:455
  193.8 0.8 shard_map.104
  194.6 22.4 %all_to_all.32.refs_0_ = f32[64,32,128]{2,1,0:T(8,128)S(1)} all-to-all(f32[64,32,128]{2,1,0:T(8,128)S(1)} %get-tuple-element.78), channel_id=1, replica_groups=mesh['row'=16,'layer'=4,'core'=2] {'layer','row'}, dimensions={0} | all-to-all | bytes 2097152 | tf_op jit(solution)/shard_map/all_to_all | solution.py:492
  217.0 3.0 %collective-permute-start.13 = (f32[64,32,128]{2,1,0:T(8,128)S(1)}, f32[64,32,128]{2,1,0:T(8,128)S(1)}, u32[]{:S(2)}, u32[]{:S(2)}) collective-permute-start(f32[64,32,128]{2,1,0:T(8,128)S(1)} %all_to_all.32.refs_0_), channel_id=1, source_target_pairs={{0,1},{1,0},{2,3},{3,2},{4,5},{5,4},{6,7},{7,6},{8,9},{9,8},{10,11... | collective-permute-start | bytes 3145736 | tf_op jit(solution)/shard_map/ppermute | solution.py:478
  220.1 2.3 %collective-permute-done.13.refs_1_ = f32[64,32,128]{2,1,0:T(8,128)S(1)} collective-permute-done((f32[64,32,128]{2,1,0:T(8,128)S(1)}, f32[64,32,128]{2,1,0:T(8,128)S(1)}, u32[]{:S(2)}, u32[]{:S(2)}) %collective-permute-start.13) | collective-permute-done | bytes 1048608 | tf_op jit(solution)/shard_map/ppermute | solution.py:478
  222.3 3.3 %shard_map.105 = (f32[2,256,512]{2,1,0:T(8,128)}, f32[6,256,256]{2,1,0:T(8,128)}) custom-call(f32[8,128]{1,0:T(8,128)S(1)} %copy-done.18, f32[64,32,128]{2,1,0:T(8,128)S(1)} %all_to_all.32.refs_0_, f32[64,32,128]{2,1,0:T(8,128)S(1)} %collective-permute-done.13.refs_1_, f32[6,256,256]{2,1,0:T(8,128)} %get-tuple-element.79.refs_2_, ...), custom_call_target="tpu_custom_call" | custom-call | flops 10000000 | bytes 9000000 | tf_op jit(solution)/shard_map/pallas_call | solution.py:436
  (41 shorter events, 0.1 us)
Async XLA Ops:
  0.6 5.9 %copy-start = (f32[2,256,512]{2,1,0:T(8,128)S(1)}, f32[2,256,512]{2,1,0:T(8,128)}, u32[]{:S(2)}) copy-start(f32[2,256,512]{2,1,0:T(8,128)} %refs_3_.1) | copy-start | bytes 3145732
  0.6 29.7 %copy-start.24 = (bf16[2,256,256]{2,1,0:T(8,128)(2,1)S(1)}, bf16[2,256,256]{2,1,0:T(8,128)(2,1)}, u32[]{:S(2)}) copy-start(bf16[2,256,256]{2,1,0:T(8,128)(2,1)} %constant.5.clone.refs_10_.refs_9_) | copy-start | bytes 786436
  0.7 29.7 %copy-start.21 = (bf16[2,1,1,2,256,256]{5,4,3,2,1,0:T(8,128)(2,1)S(1)}, bf16[2,1,1,2,256,256]{5,4,3,2,1,0:T(8,128)(2,1)}, u32[]{:S(2)}) copy-start(bf16[2,1,1,2,256,256]{5,4,3,2,1,0:T(8,128)(2,1)} %param.11) | copy-start | bytes 1572868
  0.7 29.7 %copy-start.23 = (s32[2,1,1]{0,2,1:T(1,128)S(1)}, s32[2,1,1]{0,2,1:T(1,128)}, u32[]{:S(2)}) copy-start(s32[2,1,1]{0,2,1:T(1,128)} %param.10) | copy-start | bytes 28
  0.7 29.7 %copy-start.20 = (s32[2,1,1,2,2]{4,3,2,1,0:T(2,128)S(1)}, s32[2,1,1,2,2]{4,3,2,1,0:T(2,128)}, u32[]{:S(2)}) copy-start(s32[2,1,1,2,2]{4,3,2,1,0:T(2,128)} %param.9) | copy-start | bytes 100
  1.9 15.3 %collective-permute-start = (f32[2,256,256]{2,1,0:T(8,128)S(1)}, f32[2,256,256]{2,1,0:T(8,128)S(1)}, u32[]{:S(2)}, u32[]{:S(2)}) collective-permute-start(f32[2,256,256]{2,1,0:T(8,128)S(1)} %slice.6), channel_id=1, source_target_pairs={{8,0},{16,8},{24,16},{32,24},{40,32},{48,40},{56,48},{64,56},{72,6... | collective-permute-start | bytes 1572872 | tf_op jit(solution)/shard_map/ppermute | solution.py:455
  3.2 25.2 %collective-permute-start.2 = (f32[2,256,256]{2,1,0:T(8,128)S(1)}, f32[2,256,256]{2,1,0:T(8,128)S(1)}, u32[]{:S(2)}, u32[]{:S(2)}) collective-permute-start(f32[2,256,256]{2,1,0:T(8,128)S(1)} %slice.6), channel_id=1, source_target_pairs={{1,0},{2,1},{3,2},{4,3},{5,4},{6,5},{7,6},{9,8},{10,9},{11,10},{12... | collective-permute-start | bytes 1572872 | tf_op jit(solution)/shard_map/ppermute | solution.py:455
  6.6 21.8 %collective-permute-start.1 = (f32[2,256,256]{2,1,0:T(8,128)S(1)}, f32[2,256,256]{2,1,0:T(8,128)S(1)}, u32[]{:S(2)}, u32[]{:S(2)}) collective-permute-start(f32[2,256,256]{2,1,0:T(8,128)S(1)} %slice.7), channel_id=1, source_target_pairs={{8,0},{16,8},{24,16},{32,24},{40,32},{48,40},{56,48},{64,56},{72,6... | collective-permute-start | bytes 1572872 | tf_op jit(solution)/shard_map/ppermute | solution.py:455
  17.2 27.4 %copy-start.14 = (f32[2,256,256]{2,1,0:T(8,128)}, f32[2,256,256]{2,1,0:T(8,128)S(1)}, u32[]{:S(2)}) copy-start(f32[2,256,256]{2,1,0:T(8,128)S(1)} %collective-permute-done.refs_3_.below0) | copy-start | bytes 1572868
  17.2 13.2 %collective-permute-start.3 = (f32[2,256,256]{2,1,0:T(8,128)S(1)}, f32[2,256,256]{2,1,0:T(8,128)S(1)}, u32[]{:S(2)}, u32[]{:S(2)}) collective-permute-start(f32[2,256,256]{2,1,0:T(8,128)S(1)} %collective-permute-done.refs_3_.below0), channel_id=1, source_target_pairs={{1,0},{2,1},{3,2},{4,3},{5,4},{6,5},{7,6},{9,8},{10,9},{11,10},{12... | collective-permute-start | bytes 1572872 | tf_op jit(solution)/shard_map/ppermute | solution.py:455
  28.4 16.1 %copy-start.16 = (f32[2,256,256]{2,1,0:T(8,128)}, f32[2,256,256]{2,1,0:T(8,128)S(1)}, u32[]{:S(2)}) copy-start(f32[2,256,256]{2,1,0:T(8,128)S(1)} %collective-permute-done.1.refs_4_.below1) | copy-start | bytes 1572868
  28.4 16.1 %copy-start.15 = (f32[2,256,256]{2,1,0:T(8,128)}, f32[2,256,256]{2,1,0:T(8,128)S(1)}, u32[]{:S(2)}) copy-start(f32[2,256,256]{2,1,0:T(8,128)S(1)} %collective-permute-done.2.refs_5_.rim) | copy-start | bytes 1572868
  30.4 14.2 %copy-start.17 = (f32[2,256,256]{2,1,0:T(8,128)}, f32[2,256,256]{2,1,0:T(8,128)S(1)}, u32[]{:S(2)}) copy-start(f32[2,256,256]{2,1,0:T(8,128)S(1)} %collective-permute-done.3.refs_6_.diag) | copy-start | bytes 1572868
  44.6 5.5 %collective-permute-start.4 = (f32[6,256,128]{2,1,0:T(8,128)S(1)}, f32[6,256,128]{2,1,0:T(8,128)S(1)}, u32[]{:S(2)}, u32[]{:S(2)}) collective-permute-start(f32[6,256,128]{2,1,0:T(8,128)S(1)} %get-tuple-element.46), channel_id=1, source_target_pairs={{0,1},{1,0},{2,3},{3,2},{4,5},{5,4},{6,7},{7,6},{8,9},{9,8},{10,11... | collective-permute-start | bytes 2359304 | tf_op jit(solution)/shard_map/ppermute | solution.py:478
  44.7 33.1 %collective-permute-start.6 = (f32[2,2,264,256]{3,2,1,0:T(8,128)}, f32[2,2,264,256]{3,2,1,0:T(8,128)}, u32[]{:S(2)}, u32[]{:S(2)}) collective-permute-start(f32[2,2,264,256]{3,2,1,0:T(8,128)} %get-tuple-element.48.refs_0_), channel_id=1, source_target_pairs={{8,0},{16,8},{24,16},{32,24},{40,32},{48,40},{56,48},{64,56},{72,6... | collective-permute-start | bytes 3244040 | tf_op jit(solution)/shard_map/ppermute | solution.py:455
  46.0 31.8 %collective-permute-start.5 = (f32[2,2,264,256]{3,2,1,0:T(8,128)}, f32[2,2,264,256]{3,2,1,0:T(8,128)S(1)}, u32[]{:S(2)}, u32[]{:S(2)}) collective-permute-start(f32[2,2,264,256]{3,2,1,0:T(8,128)} %get-tuple-element.48.refs_0_), channel_id=1, source_target_pairs={{0,8},{8,16},{16,24},{24,32},{32,40},{40,48},{48,56},{56,64},{64,7... | collective-permute-start | bytes 3244040 | tf_op jit(solution)/shard_map/ppermute | solution.py:455
  50.1 28.7 %copy-start.5 = (f32[2,2,264,256]{3,2,1,0:T(8,128)S(1)}, f32[2,2,264,256]{3,2,1,0:T(8,128)}, u32[]{:S(2)}) copy-start(f32[2,2,264,256]{3,2,1,0:T(8,128)} %get-tuple-element.48.refs_0_) | copy-start | bytes 3244036
  66.9 17.9 %all-to-all-start.1 = ((f32[16,24,128]{2,1,0:T(8,128)}), f32[16,24,128]{2,1,0:T(8,128)S(1)}, u32[]{:S(2)}, u32[]{:S(2)}) async-start(f32[16,24,128]{2,1,0:T(8,128)} %bitcast.5), calls=%async_computation.1 | async-start | bytes 393216 | tf_op jit(solution)/shard_map/all_to_all | solution.py:486
  77.8 1.0 copy-start.6
  78.8 1.2 copy-start.7
  82.8 1.0 copy-start.9
  83.8 19.1 %copy-start.2 = (f32[2,2,256,256]{3,2,1,0:T(8,128)}, f32[2,2,256,256]{3,2,1,0:T(8,128)S(1)}, u32[]{:S(2)}) copy-start(f32[2,2,256,256]{3,2,1,0:T(8,128)S(1)} %get-tuple-element.53.block0) | copy-start | bytes 3145732
  83.8 19.1 %copy-start.3 = (f32[2,2,256,256]{3,2,1,0:T(8,128)}, f32[2,2,256,256]{3,2,1,0:T(8,128)S(1)}, u32[]{:S(2)}) copy-start(f32[2,2,256,256]{3,2,1,0:T(8,128)S(1)} %get-tuple-element.54.block1) | copy-start | bytes 3145732
  84.8 17.3 %collective-permute-start.7 = (f32[2,2,256,256]{3,2,1,0:T(8,128)}, f32[2,2,256,256]{3,2,1,0:T(8,128)S(1)}, u32[]{:S(2)}, u32[]{:S(2)}) collective-permute-start(f32[2,2,256,256]{3,2,1,0:T(8,128)} %copy-done.9), channel_id=1, source_target_pairs={{0,1},{1,2},{2,3},{3,4},{4,5},{5,6},{6,7},{8,9},{9,10},{10,11},{11... | collective-permute-start | bytes 3145736 | tf_op jit(solution)/shard_map/ppermute | solution.py:455
  90.1 25.9 %collective-permute-start.8 = (f32[2,2,256,256]{3,2,1,0:T(8,128)S(1)}, f32[2,2,256,256]{3,2,1,0:T(8,128)}, u32[]{:S(2)}, u32[]{:S(2)}) collective-permute-start(f32[2,2,256,256]{3,2,1,0:T(8,128)S(1)} %get-tuple-element.53.block0), channel_id=1, source_target_pairs={{1,0},{2,1},{3,2},{4,3},{5,4},{6,5},{7,6},{9,8},{10,9},{11,10},{12... | collective-permute-start | bytes 3145736 | tf_op jit(solution)/shard_map/ppermute | solution.py:455
  102.1 1.1 copy-start.4
  103.2 1.0 copy-start.10
  104.1 1.0 copy-start.11
  105.1 27.5 %all-to-all-start.2 = ((f32[64,32,128]{2,1,0:T(8,128)}), f32[64,32,128]{2,1,0:T(8,128)S(1)}, u32[]{:S(2)}, u32[]{:S(2)}) async-start(f32[64,32,128]{2,1,0:T(8,128)} %copy-done.10), calls=%async_computation.2 | async-start | bytes 2097152 | tf_op jit(solution)/shard_map/all_to_all | solution.py:492
  132.6 5.3 %copy-start.25 = (f32[64,32,128]{2,1,0:T(8,128)}, f32[64,32,128]{2,1,0:T(8,128)S(1)}, u32[]{:S(2)}) copy-start(f32[64,32,128]{2,1,0:T(8,128)S(1)} %all-to-all-done.2.refs_2_) | copy-start | bytes 3145732
  132.6 5.3 %collective-permute-start.9 = (f32[64,32,128]{2,1,0:T(8,128)S(1)}, f32[64,32,128]{2,1,0:T(8,128)S(1)}, u32[]{:S(2)}, u32[]{:S(2)}) collective-permute-start(f32[64,32,128]{2,1,0:T(8,128)S(1)} %all-to-all-done.2.refs_2_), channel_id=1, source_target_pairs={{0,1},{1,0},{2,3},{3,2},{4,5},{5,4},{6,7},{7,6},{8,9},{9,8},{10,11... | collective-permute-start | bytes 3145736 | tf_op jit(solution)/shard_map/ppermute | solution.py:478
  138.0 1.0 copy-start.26
  151.9 2.9 %collective-permute-start.10 = (f32[6,256,128]{2,1,0:T(8,128)}, f32[6,256,128]{2,1,0:T(8,128)S(1)}, u32[]{:S(2)}, u32[]{:S(2)}) collective-permute-start(f32[6,256,128]{2,1,0:T(8,128)} %get-tuple-element.66), channel_id=1, source_target_pairs={{0,1},{1,0},{2,3},{3,2},{4,5},{5,4},{6,7},{7,6},{8,9},{9,8},{10,11... | collective-permute-start | bytes 2359304 | tf_op jit(solution)/shard_map/ppermute | solution.py:478
  152.4 25.8 %collective-permute-start.11 = (f32[2,2,264,256]{3,2,1,0:T(8,128)}, f32[2,2,264,256]{3,2,1,0:T(8,128)S(1)}, u32[]{:S(2)}, u32[]{:S(2)}) collective-permute-start(f32[2,2,264,256]{3,2,1,0:T(8,128)} %get-tuple-element.68.refs_0_), channel_id=1, source_target_pairs={{0,8},{8,16},{16,24},{24,32},{32,40},{40,48},{48,56},{56,64},{64,7... | collective-permute-start | bytes 3244040 | tf_op jit(solution)/shard_map/ppermute | solution.py:455
  154.8 1.1 copy-start.13
  156.0 22.2 %copy-start.8 = (f32[2,2,264,256]{3,2,1,0:T(8,128)S(1)}, f32[2,2,264,256]{3,2,1,0:T(8,128)}, u32[]{:S(2)}) copy-start(f32[2,2,264,256]{3,2,1,0:T(8,128)} %get-tuple-element.68.refs_0_) | copy-start | bytes 3244036
  171.2 11.7 %all-to-all-start.4 = ((f32[16,24,128]{2,1,0:T(8,128)}), f32[16,24,128]{2,1,0:T(8,128)S(1)}, u32[]{:S(2)}, u32[]{:S(2)}) async-start(f32[16,24,128]{2,1,0:T(8,128)} %bitcast.7), calls=%async_computation.4 | async-start | bytes 393216 | tf_op jit(solution)/shard_map/all_to_all | solution.py:486
  178.2 15.6 %copy-start.19 = (f32[8,128]{1,0:T(8,128)S(1)}, f32[8,128]{1,0:T(8,128)}, u32[]{:S(2)}) copy-start(f32[8,128]{1,0:T(8,128)} %get-tuple-element.77.loss) | copy-start | bytes 12292
  179.0 0.8 copy-start.22
  183.0 10.8 %collective-permute-start.12 = (f32[1,2,256,256]{3,2,1,0:T(8,128)}, f32[1,2,256,256]{3,2,1,0:T(8,128)S(1)}, u32[]{:S(2)}, u32[]{:S(2)}) collective-permute-start(f32[1,2,256,256]{3,2,1,0:T(8,128)} %copy-done.22), channel_id=1, source_target_pairs={{0,1},{1,2},{2,3},{3,4},{4,5},{5,6},{6,7},{8,9},{9,10},{10,11},{11... | collective-permute-start | bytes 1572872 | tf_op jit(solution)/shard_map/ppermute | solution.py:455
  194.6 27.7 %copy-start.1 = (f32[2,256,512]{2,1,0:T(8,128)S(1)}, f32[2,256,512]{2,1,0:T(8,128)}, u32[]{:S(2)}) copy-start(f32[2,256,512]{2,1,0:T(8,128)} %refs_3_.1) | copy-start | bytes 3145732
  194.6 27.7 %copy-start.12 = (f32[2,256,512]{2,1,0:T(8,128)S(1)}, f32[2,256,512]{2,1,0:T(8,128)}, u32[]{:S(2)}) copy-start(f32[2,256,512]{2,1,0:T(8,128)} %copy-done.11) | copy-start | bytes 3145732
  194.6 27.7 %copy-start.18 = (f32[8,128]{1,0:T(8,128)S(1)}, f32[8,128]{1,0:T(8,128)}, u32[]{:S(2)}) copy-start(f32[8,128]{1,0:T(8,128)} %get-tuple-element.64.rate_first) | copy-start | bytes 12292
  217.0 5.3 %collective-permute-start.13 = (f32[64,32,128]{2,1,0:T(8,128)S(1)}, f32[64,32,128]{2,1,0:T(8,128)S(1)}, u32[]{:S(2)}, u32[]{:S(2)}) collective-permute-start(f32[64,32,128]{2,1,0:T(8,128)S(1)} %all_to_all.32.refs_0_), channel_id=1, source_target_pairs={{0,1},{1,0},{2,3},{3,2},{4,5},{5,4},{6,7},{7,6},{8,9},{9,8},{10,11... | collective-permute-start | bytes 3145736 | tf_op jit(solution)/shard_map/ppermute | solution.py:478

commit v8 on v5

--- a/solution.py
+++ b/solution.py
@@ -311,7 +311,7 @@
             pltpu.SemaphoreType.DMA((1,)),
             *[pltpu.VMEM(value.shape, value.dtype) for value in big],
         ],
-        compiler_params=pltpu.CompilerParams(vmem_limit_bytes=48 * MEGA),
+        compiler_params=pltpu.CompilerParams(vmem_limit_bytes=60 * MEGA),
         cost_estimate=pl.CostEstimate(flops=8_000_000_000, bytes_accessed=12_000_000, transcendentals=0),
     )(corners, counts, *big)
 

time: 228 us -> 226 us (level)
  local copies, waits for them, and re-layouts: 8.58 us -> 11.4 us
    unnamed x52 -> x50, local copies, waits for them, and re-layouts: 7.34 us -> 10.2 us
where the time goes in v8:
time: 226 us; the launch traced here: 225 us
  starting transfers between devices  60.9 us (27%)
  waiting for transfers between devices  54.6 us (24%)
  blocking collectives  53.4 us (24%)
  Pallas kernels  43.8 us (19%)
  local copies, waits for them, and re-layouts  11.4 us (5%)
    ppermute x10, waiting for transfers between devices, shift(): lax.ppermute(value, axis, [(source, source + steps) for source in range(f...  36.8 us
    all_to_all x2, blocking collectives, reduce_chips(): lax.all_to_all(value.reshape(layers, rows * CHUNK, HALF), 'layer', 0, 0,...  31 us
    ppermute x10, starting transfers between devices, shift(): lax.ppermute(value, axis, [(source, source + steps) for source in range(f...  29.8 us
    pallas_call x2, Pallas kernels, window_call(): pl.pallas_call(lambda *refs: window_kernel(iteration, *refs), out_shape=(...  26.1 us
    all_to_all x1, blocking collectives, finish_tile(): return (tile, lax.all_to_all(sent, CHIPS, 0, 0, tiled=True), losses)  22.4 us
    all_to_all x2, starting transfers between devices, reduce_rows(): lax.all_to_all(part.reshape(rows, CHUNK, HALF), 'row', 0, 0, tiled=True)  15.3 us
    pallas_call x9, Pallas kernels, call(): pl.pallas_call(kernel, out_shape=tuple(out_shape), in_specs=[SMEM] * n_sm...  14.4 us
    unnamed x50, local copies, waits for them, and re-layouts  10.2 us
  transfers between devices with their start and end apart: 17, of which 11 were waited for; matrix products, arithmetic and copies ran while one was open for 0% of the time, Pallas kernels for 6%

profile of v8, /device:TPU:1, one launch (start us, length us, event | category | flops | bytes accessed | tf_op | source)
XLA Modules:
  0.0 225.2 jit_solution(14810078276256835950)
XLA Ops:
  0.6 0.0 copy-start
  0.6 1.2 slice.6
  1.8 1.3 collective-permute-start
  3.1 3.3 %collective-permute-start.2 = (f32[2,256,256]{2,1,0:T(8,128)S(1)}, f32[2,256,256]{2,1,0:T(8,128)S(1)}, u32[]{:S(2)}, u32[]{:S(2)}) collective-permute-start(f32[2,256,256]{2,1,0:T(8,128)S(1)} %slice.6), channel_id=1, source_target_pairs={{1,0},{2,1},{3,2},{4,3},{5,4},{6,5},{7,6},{9,8},{10,9},{11,10},{12... | collective-permute-start | bytes 1572872 | tf_op jit(solution)/shard_map/ppermute | solution.py:442
  6.5 1.3 collective-permute-start.1
  7.8 9.3 %collective-permute-done.refs_3_.below0 = f32[2,256,256]{2,1,0:T(8,128)S(1)} collective-permute-done((f32[2,256,256]{2,1,0:T(8,128)S(1)}, f32[2,256,256]{2,1,0:T(8,128)S(1)}, u32[]{:S(2)}, u32[]{:S(2)}) %collective-permute-start) | collective-permute-done | bytes 524320 | tf_op jit(solution)/shard_map/ppermute | solution.py:442
  17.1 4.8 %collective-permute-start.3 = (f32[2,256,256]{2,1,0:T(8,128)S(1)}, f32[2,256,256]{2,1,0:T(8,128)S(1)}, u32[]{:S(2)}, u32[]{:S(2)}) collective-permute-start(f32[2,256,256]{2,1,0:T(8,128)S(1)} %collective-permute-done.refs_3_.below0), channel_id=1, source_target_pairs={{1,0},{2,1},{3,2},{4,3},{5,4},{6,5},{7,6},{9,8},{10,9},{11,10},{12... | collective-permute-start | bytes 1572872 | tf_op jit(solution)/shard_map/ppermute | solution.py:442
  21.9 6.5 %collective-permute-done.1.refs_4_.below1 = f32[2,256,256]{2,1,0:T(8,128)S(1)} collective-permute-done((f32[2,256,256]{2,1,0:T(8,128)S(1)}, f32[2,256,256]{2,1,0:T(8,128)S(1)}, u32[]{:S(2)}, u32[]{:S(2)}) %collective-permute-start.1) | collective-permute-done | bytes 524320 | tf_op jit(solution)/shard_map/ppermute | solution.py:442
  28.3 0.0 collective-permute-done.2.refs_5_.rim
  28.3 2.0 collective-permute-done.3.refs_6_.diag
  30.3 0.8 copy-done.23
  31.1 13.2 %shard_map.94 = (f32[2,2,264,256]{3,2,1,0:T(8,128)}, f32[6,256,128]{2,1,0:T(8,128)}, f32[6,256,128]{2,1,0:T(8,128)}, f32[8,128]{1,0:T(8,128)}) custom-call(s32[2,2,2]{2,1,0:T(2,128)} %bitcast.12, s32[2]{0:T(128)} %bitcast.20, f32[2,256,512]{2,1,0:T(8,128)} %refs_3_.1, f32[2,256,256]{2,1,0:T(8,128)} %copy-done.20, f32[2,256,256]{2,1,0:T(8,128)} %copy-done.22, ...), custom_call_target="tpu_custom_call" | custom-call | flops 8000000000 | bytes 12000000 | tf_op jit(solution)/shard_map/pallas_call | solution.py:296
  44.3 0.1 collective-permute-start.4
  44.4 1.3 collective-permute-start.6
  45.7 4.1 %collective-permute-start.5 = (f32[2,2,264,256]{3,2,1,0:T(8,128)}, f32[2,2,264,256]{3,2,1,0:T(8,128)S(1)}, u32[]{:S(2)}, u32[]{:S(2)}) collective-permute-start(f32[2,2,264,256]{3,2,1,0:T(8,128)} %get-tuple-element.48.refs_0_), channel_id=1, source_target_pairs={{0,8},{8,16},{16,24},{24,32},{32,40},{40,48},{48,56},{56,64},{64,7... | collective-permute-start | bytes 3244040 | tf_op jit(solution)/shard_map/ppermute | solution.py:442
  49.8 0.0 copy-start.14
  49.8 1.1 copy-done.14
  50.9 0.1 shard_map.95
  51.0 0.0 copy-start.5
  51.0 16.5 %all_to_all.30.parts = f32[4,384,128]{2,1,0:T(8,128)S(1)} all-to-all(f32[4,384,128]{2,1,0:T(8,128)S(1)} %bitcast.10), channel_id=1, replica_groups=mesh['row'=16,'layer'=4,'core'=2] {'layer'}, dimensions={0} | all-to-all | bytes 1572864 | tf_op jit(solution)/shard_map/all_to_all | solution.py:469
  67.5 0.7 shard_map.96
  68.2 10.9 %all-to-all-start.1 = ((f32[16,24,128]{2,1,0:T(8,128)}), f32[16,24,128]{2,1,0:T(8,128)S(1)}, u32[]{:S(2)}, u32[]{:S(2)}) async-start(f32[16,24,128]{2,1,0:T(8,128)} %bitcast.5), calls=%async_computation.1 | async-start | bytes 393216 | tf_op jit(solution)/shard_map/all_to_all | solution.py:473
  79.1 0.0 collective-permute-done.6.refs_2_
  79.1 0.0 collective-permute-done.5.refs_1_
  79.2 1.0 copy-done.6
  80.2 1.2 copy-done.7
  81.4 2.8 %shard_map.97 = (f32[2,2,256,256]{3,2,1,0:T(8,128)S(1)}, f32[2,2,256,256]{3,2,1,0:T(8,128)S(1)}, f32[2,2,256,256]{3,2,1,0:T(8,128)S(1)}) custom-call(f32[2,2,264,256]{3,2,1,0:T(8,128)S(1)} %copy-done.5, f32[2,2,264,256]{3,2,1,0:T(8,128)S(1)} %copy-done.7, f32[2,2,264,256]{3,2,1,0:T(8,128)} %collective-permute-done.6.refs_2_, ...), custom_call_target="tpu_custom_call" | custom-call | flops 10000000 | bytes 6393856 | tf_op jit(solution)/shard_map/pallas_call | solution.py:279
  84.2 0.0 copy-start.9
  84.2 1.0 copy-done.9
  85.1 1.0 all-to-all-done.1.parts
  86.2 5.0 %collective-permute-start.7 = (f32[2,2,256,256]{3,2,1,0:T(8,128)}, f32[2,2,256,256]{3,2,1,0:T(8,128)S(1)}, u32[]{:S(2)}, u32[]{:S(2)}) collective-permute-start(f32[2,2,256,256]{3,2,1,0:T(8,128)} %copy-done.9), channel_id=1, source_target_pairs={{0,1},{1,2},{2,3},{3,4},{4,5},{5,6},{6,7},{8,9},{9,10},{10,11},{11... | collective-permute-start | bytes 3145736 | tf_op jit(solution)/shard_map/ppermute | solution.py:442
  91.2 1.9 collective-permute-start.8
  93.1 10.1 %collective-permute-done.7.from_left.left = f32[2,2,256,256]{3,2,1,0:T(8,128)S(1)} collective-permute-done((f32[2,2,256,256]{3,2,1,0:T(8,128)}, f32[2,2,256,256]{3,2,1,0:T(8,128)S(1)}, u32[]{:S(2)}, u32[]{:S(2)}) %collective-permute-start.7) | collective-permute-done | bytes 1048608 | tf_op jit(solution)/shard_map/ppermute | solution.py:442
  103.3 0.8 shard_map.98
  104.1 0.2 copy-done.4
  104.3 1.0 copy-done.10
  105.3 1.0 copy-done.11
  106.3 9.1 %all-to-all-start.2 = ((f32[64,32,128]{2,1,0:T(8,128)}), f32[64,32,128]{2,1,0:T(8,128)S(1)}, u32[]{:S(2)}, u32[]{:S(2)}) async-start(f32[64,32,128]{2,1,0:T(8,128)} %copy-done.10), calls=%async_computation.2 | async-start | bytes 2097152 | tf_op jit(solution)/shard_map/all_to_all | solution.py:479
  115.3 7.6 %shard_map.99 = (f32[2,2,256,256]{3,2,1,0:T(8,128)}, f32[2,2,256,256]{3,2,1,0:T(8,128)}) custom-call(s32[2,2,2]{2,1,0:T(2,128)} %bitcast.13, f32[2,256,512]{2,1,0:T(8,128)} %refs_3_.1, f32[2,256,256]{2,1,0:T(8,128)} %copy-done.20, f32[2,256,256]{2,1,0:T(8,128)} %copy-done.22, f32[2,256,256]{2,1,0:T(8,128)} %copy-done.21, f32[2,256,256]{2,1,0:T(8,128)} %copy-done.23, ...), custom_call_target="tpu_custom_call" | custom-call | flops 10000000 | bytes 10485792 | tf_op jit(solution)/shard_map/pallas_call | solution.py:279
  122.9 9.0 %all-to-all-done.2.refs_2_ = f32[64,32,128]{2,1,0:T(8,128)S(1)} async-done(((f32[64,32,128]{2,1,0:T(8,128)}), f32[64,32,128]{2,1,0:T(8,128)S(1)}, u32[]{:S(2)}, u32[]{:S(2)}) %all-to-all-start.2) | async-done | bytes 1048608 | tf_op jit(solution)/shard_map/all_to_all | solution.py:479
  132.0 3.0 %collective-permute-start.9 = (f32[64,32,128]{2,1,0:T(8,128)S(1)}, f32[64,32,128]{2,1,0:T(8,128)S(1)}, u32[]{:S(2)}, u32[]{:S(2)}) collective-permute-start(f32[64,32,128]{2,1,0:T(8,128)S(1)} %all-to-all-done.2.refs_2_), channel_id=1, source_target_pairs={{0,1},{1,0},{2,3},{3,2},{4,5},{5,4},{6,7},{7,6},{8,9},{9,8},{10,11... | collective-permute-start | bytes 3145736 | tf_op jit(solution)/shard_map/ppermute | solution.py:465
  135.0 2.3 %collective-permute-done.9.refs_3_ = f32[64,32,128]{2,1,0:T(8,128)S(1)} collective-permute-done((f32[64,32,128]{2,1,0:T(8,128)S(1)}, f32[64,32,128]{2,1,0:T(8,128)S(1)}, u32[]{:S(2)}, u32[]{:S(2)}) %collective-permute-start.9) | collective-permute-done | bytes 1048608 | tf_op jit(solution)/shard_map/ppermute | solution.py:465
  137.3 1.0 copy-done.24
  138.3 12.9 %shard_map.100 = (f32[2,2,264,256]{3,2,1,0:T(8,128)}, f32[6,256,128]{2,1,0:T(8,128)}, f32[6,256,128]{2,1,0:T(8,128)}, f32[6,256,256]{2,1,0:T(8,128)}, f32[8,128]{1,0:T(8,128)}, /*index=5*/f32[8,128]{1,0:T(8,128)}) custom-call(s32[2,2,2]{2,1,0:T(2,128)} %bitcast.14, s32[2]{0:T(128)} %bitcast.21, f32[64,32,128]{2,1,0:T(8,128)} %copy-done.19, ...), custom_call_target="tpu_custom_call" | custom-call | flops 8000000000 | bytes 12000000 | tf_op jit(solution)/shard_map/pallas_call | solution.py:296
  151.2 0.5 collective-permute-start.10
  151.7 2.4 %collective-permute-start.11 = (f32[2,2,264,256]{3,2,1,0:T(8,128)}, f32[2,2,264,256]{3,2,1,0:T(8,128)S(1)}, u32[]{:S(2)}, u32[]{:S(2)}) collective-permute-start(f32[2,2,264,256]{3,2,1,0:T(8,128)} %get-tuple-element.68.refs_0_), channel_id=1, source_target_pairs={{0,8},{8,16},{16,24},{24,32},{32,40},{40,48},{48,56},{56,64},{64,7... | collective-permute-start | bytes 3244040 | tf_op jit(solution)/shard_map/ppermute | solution.py:442
  154.1 1.1 copy-done.13
  155.3 0.1 shard_map.101
  155.4 0.0 copy-start.8
  155.4 14.5 %all_to_all.31.parts = f32[4,384,128]{2,1,0:T(8,128)S(1)} all-to-all(f32[4,384,128]{2,1,0:T(8,128)S(1)} %bitcast.11), channel_id=1, replica_groups=mesh['row'=16,'layer'=4,'core'=2] {'layer'}, dimensions={0} | all-to-all | bytes 1572864 | tf_op jit(solution)/shard_map/all_to_all | solution.py:469
  169.9 0.7 shard_map.102
  170.6 4.4 %all-to-all-start.4 = ((f32[16,24,128]{2,1,0:T(8,128)}), f32[16,24,128]{2,1,0:T(8,128)S(1)}, u32[]{:S(2)}, u32[]{:S(2)}) async-start(f32[16,24,128]{2,1,0:T(8,128)} %bitcast.7), calls=%async_computation.4 | async-start | bytes 393216 | tf_op jit(solution)/shard_map/all_to_all | solution.py:473
  175.0 2.5 %collective-permute-done.11.refs_1_ = f32[2,2,264,256]{3,2,1,0:T(8,128)S(1)} collective-permute-done((f32[2,2,264,256]{3,2,1,0:T(8,128)}, f32[2,2,264,256]{3,2,1,0:T(8,128)S(1)}, u32[]{:S(2)}, u32[]{:S(2)}) %collective-permute-start.11) | collective-permute-done | bytes 1081376 | tf_op jit(solution)/shard_map/ppermute | solution.py:442
  177.5 0.8 shard_map.103
  178.3 0.0 copy-start.18
  178.4 0.8 copy-done.18
  179.1 3.2 %all-to-all-done.4.parts = f32[16,24,128]{2,1,0:T(8,128)S(1)} async-done(((f32[16,24,128]{2,1,0:T(8,128)}), f32[16,24,128]{2,1,0:T(8,128)S(1)}, u32[]{:S(2)}, u32[]{:S(2)}) %all-to-all-start.4) | async-done | bytes 196640 | tf_op jit(solution)/shard_map/all_to_all | solution.py:473
  182.3 4.4 %collective-permute-start.12 = (f32[1,2,256,256]{3,2,1,0:T(8,128)}, f32[1,2,256,256]{3,2,1,0:T(8,128)S(1)}, u32[]{:S(2)}, u32[]{:S(2)}) collective-permute-start(f32[1,2,256,256]{3,2,1,0:T(8,128)} %copy-done.18), channel_id=1, source_target_pairs={{0,1},{1,2},{2,3},{3,4},{4,5},{5,6},{6,7},{8,9},{9,10},{10,11},{11... | collective-permute-start | bytes 1572872 | tf_op jit(solution)/shard_map/ppermute | solution.py:442
  186.7 6.4 %collective-permute-done.12.from_left = f32[1,2,256,256]{3,2,1,0:T(8,128)S(1)} collective-permute-done((f32[1,2,256,256]{3,2,1,0:T(8,128)}, f32[1,2,256,256]{3,2,1,0:T(8,128)S(1)}, u32[]{:S(2)}, u32[]{:S(2)}) %collective-permute-start.12) | collective-permute-done | bytes 524320 | tf_op jit(solution)/shard_map/ppermute | solution.py:442
  193.2 0.8 shard_map.104
  194.0 22.4 %all_to_all.32.refs_0_ = f32[64,32,128]{2,1,0:T(8,128)S(1)} all-to-all(f32[64,32,128]{2,1,0:T(8,128)S(1)} %get-tuple-element.78), channel_id=1, replica_groups=mesh['row'=16,'layer'=4,'core'=2] {'layer','row'}, dimensions={0} | all-to-all | bytes 2097152 | tf_op jit(solution)/shard_map/all_to_all | solution.py:479
  216.4 3.0 %collective-permute-start.13 = (f32[64,32,128]{2,1,0:T(8,128)S(1)}, f32[64,32,128]{2,1,0:T(8,128)S(1)}, u32[]{:S(2)}, u32[]{:S(2)}) collective-permute-start(f32[64,32,128]{2,1,0:T(8,128)S(1)} %all_to_all.32.refs_0_), channel_id=1, source_target_pairs={{0,1},{1,0},{2,3},{3,2},{4,5},{5,4},{6,7},{7,6},{8,9},{9,8},{10,11... | collective-permute-start | bytes 3145736 | tf_op jit(solution)/shard_map/ppermute | solution.py:465
  219.4 2.3 %collective-permute-done.13.refs_1_ = f32[64,32,128]{2,1,0:T(8,128)S(1)} collective-permute-done((f32[64,32,128]{2,1,0:T(8,128)S(1)}, f32[64,32,128]{2,1,0:T(8,128)S(1)}, u32[]{:S(2)}, u32[]{:S(2)}) %collective-permute-start.13) | collective-permute-done | bytes 1048608 | tf_op jit(solution)/shard_map/ppermute | solution.py:465
  221.7 3.3 %shard_map.105 = (f32[2,256,512]{2,1,0:T(8,128)}, f32[6,256,256]{2,1,0:T(8,128)}) custom-call(f32[8,128]{1,0:T(8,128)S(1)} %copy-done.16, f32[64,32,128]{2,1,0:T(8,128)S(1)} %all_to_all.32.refs_0_, f32[64,32,128]{2,1,0:T(8,128)S(1)} %collective-permute-done.13.refs_1_, f32[6,256,256]{2,1,0:T(8,128)} %get-tuple-element.79.refs_2_, ...), custom_call_target="tpu_custom_call" | custom-call | flops 10000000 | bytes 9000000 | tf_op jit(solution)/shard_map/pallas_call | solution.py:423
  (37 shorter events, 0.1 us)
Async XLA Ops:
  0.6 5.8 %copy-start = (f32[2,256,512]{2,1,0:T(8,128)S(1)}, f32[2,256,512]{2,1,0:T(8,128)}, u32[]{:S(2)}) copy-start(f32[2,256,512]{2,1,0:T(8,128)} %refs_3_.1) | copy-start | bytes 3145732
  1.8 15.3 %collective-permute-start = (f32[2,256,256]{2,1,0:T(8,128)S(1)}, f32[2,256,256]{2,1,0:T(8,128)S(1)}, u32[]{:S(2)}, u32[]{:S(2)}) collective-permute-start(f32[2,256,256]{2,1,0:T(8,128)S(1)} %slice.6), channel_id=1, source_target_pairs={{8,0},{16,8},{24,16},{32,24},{40,32},{48,40},{56,48},{64,56},{72,6... | collective-permute-start | bytes 1572872 | tf_op jit(solution)/shard_map/ppermute | solution.py:442
  3.1 25.2 %collective-permute-start.2 = (f32[2,256,256]{2,1,0:T(8,128)S(1)}, f32[2,256,256]{2,1,0:T(8,128)S(1)}, u32[]{:S(2)}, u32[]{:S(2)}) collective-permute-start(f32[2,256,256]{2,1,0:T(8,128)S(1)} %slice.6), channel_id=1, source_target_pairs={{1,0},{2,1},{3,2},{4,3},{5,4},{6,5},{7,6},{9,8},{10,9},{11,10},{12... | collective-permute-start | bytes 1572872 | tf_op jit(solution)/shard_map/ppermute | solution.py:442
  6.5 21.8 %collective-permute-start.1 = (f32[2,256,256]{2,1,0:T(8,128)S(1)}, f32[2,256,256]{2,1,0:T(8,128)S(1)}, u32[]{:S(2)}, u32[]{:S(2)}) collective-permute-start(f32[2,256,256]{2,1,0:T(8,128)S(1)} %slice.7), channel_id=1, source_target_pairs={{8,0},{16,8},{24,16},{32,24},{40,32},{48,40},{56,48},{64,56},{72,6... | collective-permute-start | bytes 1572872 | tf_op jit(solution)/shard_map/ppermute | solution.py:442
  17.1 13.2 %copy-start.20 = (f32[2,256,256]{2,1,0:T(8,128)}, f32[2,256,256]{2,1,0:T(8,128)S(1)}, u32[]{:S(2)}) copy-start(f32[2,256,256]{2,1,0:T(8,128)S(1)} %collective-permute-done.refs_3_.below0) | copy-start | bytes 1572868
  17.1 13.2 %collective-permute-start.3 = (f32[2,256,256]{2,1,0:T(8,128)S(1)}, f32[2,256,256]{2,1,0:T(8,128)S(1)}, u32[]{:S(2)}, u32[]{:S(2)}) collective-permute-start(f32[2,256,256]{2,1,0:T(8,128)S(1)} %collective-permute-done.refs_3_.below0), channel_id=1, source_target_pairs={{1,0},{2,1},{3,2},{4,3},{5,4},{6,5},{7,6},{9,8},{10,9},{11,10},{12... | collective-permute-start | bytes 1572872 | tf_op jit(solution)/shard_map/ppermute | solution.py:442
  28.3 2.0 copy-start.22
  28.3 2.0 copy-start.21
  30.3 0.8 copy-start.23
  44.3 5.5 %collective-permute-start.4 = (f32[6,256,128]{2,1,0:T(8,128)}, f32[6,256,128]{2,1,0:T(8,128)S(1)}, u32[]{:S(2)}, u32[]{:S(2)}) collective-permute-start(f32[6,256,128]{2,1,0:T(8,128)} %get-tuple-element.46), channel_id=1, source_target_pairs={{0,1},{1,0},{2,3},{3,2},{4,5},{5,4},{6,7},{7,6},{8,9},{9,8},{10,11... | collective-permute-start | bytes 2359304 | tf_op jit(solution)/shard_map/ppermute | solution.py:465
  44.4 34.7 %collective-permute-start.6 = (f32[2,2,264,256]{3,2,1,0:T(8,128)}, f32[2,2,264,256]{3,2,1,0:T(8,128)}, u32[]{:S(2)}, u32[]{:S(2)}) collective-permute-start(f32[2,2,264,256]{3,2,1,0:T(8,128)} %get-tuple-element.48.refs_0_), channel_id=1, source_target_pairs={{8,0},{16,8},{24,16},{32,24},{40,32},{48,40},{56,48},{64,56},{72,6... | collective-permute-start | bytes 3244040 | tf_op jit(solution)/shard_map/ppermute | solution.py:442
  45.7 33.5 %collective-permute-start.5 = (f32[2,2,264,256]{3,2,1,0:T(8,128)}, f32[2,2,264,256]{3,2,1,0:T(8,128)S(1)}, u32[]{:S(2)}, u32[]{:S(2)}) collective-permute-start(f32[2,2,264,256]{3,2,1,0:T(8,128)} %get-tuple-element.48.refs_0_), channel_id=1, source_target_pairs={{0,8},{8,16},{16,24},{24,32},{32,40},{40,48},{48,56},{56,64},{64,7... | collective-permute-start | bytes 3244040 | tf_op jit(solution)/shard_map/ppermute | solution.py:442
  49.8 1.1 copy-start.14
  51.0 29.2 %copy-start.5 = (f32[2,2,264,256]{3,2,1,0:T(8,128)S(1)}, f32[2,2,264,256]{3,2,1,0:T(8,128)}, u32[]{:S(2)}) copy-start(f32[2,2,264,256]{3,2,1,0:T(8,128)} %get-tuple-element.48.refs_0_) | copy-start | bytes 3244036
  68.2 18.0 %all-to-all-start.1 = ((f32[16,24,128]{2,1,0:T(8,128)}), f32[16,24,128]{2,1,0:T(8,128)S(1)}, u32[]{:S(2)}, u32[]{:S(2)}) async-start(f32[16,24,128]{2,1,0:T(8,128)} %bitcast.5), calls=%async_computation.1 | async-start | bytes 393216 | tf_op jit(solution)/shard_map/all_to_all | solution.py:473
  79.1 1.0 copy-start.6
  80.1 1.2 copy-start.7
  81.4 21.9 %copy-start.15 = (f32[8,128]{1,0:T(8,128)S(1)}, f32[8,128]{1,0:T(8,128)}, u32[]{:S(2)}) copy-start(f32[8,128]{1,0:T(8,128)} %get-tuple-element.57.loss.loss_before) | copy-start | bytes 12292
  84.2 1.0 copy-start.9
  85.1 19.0 %copy-start.2 = (f32[2,2,256,256]{3,2,1,0:T(8,128)}, f32[2,2,256,256]{3,2,1,0:T(8,128)S(1)}, u32[]{:S(2)}) copy-start(f32[2,2,256,256]{3,2,1,0:T(8,128)S(1)} %get-tuple-element.53.block0) | copy-start | bytes 3145732
  85.1 19.0 %copy-start.3 = (f32[2,2,256,256]{3,2,1,0:T(8,128)}, f32[2,2,256,256]{3,2,1,0:T(8,128)S(1)}, u32[]{:S(2)}) copy-start(f32[2,2,256,256]{3,2,1,0:T(8,128)S(1)} %get-tuple-element.54.block1) | copy-start | bytes 3145732
  86.2 17.1 %collective-permute-start.7 = (f32[2,2,256,256]{3,2,1,0:T(8,128)}, f32[2,2,256,256]{3,2,1,0:T(8,128)S(1)}, u32[]{:S(2)}, u32[]{:S(2)}) collective-permute-start(f32[2,2,256,256]{3,2,1,0:T(8,128)} %copy-done.9), channel_id=1, source_target_pairs={{0,1},{1,2},{2,3},{3,4},{4,5},{5,6},{6,7},{8,9},{9,10},{10,11},{11... | collective-permute-start | bytes 3145736 | tf_op jit(solution)/shard_map/ppermute | solution.py:442
  91.2 24.1 %collective-permute-start.8 = (f32[2,2,256,256]{3,2,1,0:T(8,128)S(1)}, f32[2,2,256,256]{3,2,1,0:T(8,128)}, u32[]{:S(2)}, u32[]{:S(2)}) collective-permute-start(f32[2,2,256,256]{3,2,1,0:T(8,128)S(1)} %get-tuple-element.53.block0), channel_id=1, source_target_pairs={{1,0},{2,1},{3,2},{4,3},{5,4},{6,5},{7,6},{9,8},{10,9},{11,10},{12... | collective-permute-start | bytes 3145736 | tf_op jit(solution)/shard_map/ppermute | solution.py:442
  103.2 1.0 copy-start.4
  104.3 1.0 copy-start.10
  105.3 1.0 copy-start.11
  106.3 25.7 %all-to-all-start.2 = ((f32[64,32,128]{2,1,0:T(8,128)}), f32[64,32,128]{2,1,0:T(8,128)S(1)}, u32[]{:S(2)}, u32[]{:S(2)}) async-start(f32[64,32,128]{2,1,0:T(8,128)} %copy-done.10), calls=%async_computation.2 | async-start | bytes 2097152 | tf_op jit(solution)/shard_map/all_to_all | solution.py:479
  132.0 5.3 %copy-start.19 = (f32[64,32,128]{2,1,0:T(8,128)}, f32[64,32,128]{2,1,0:T(8,128)S(1)}, u32[]{:S(2)}) copy-start(f32[64,32,128]{2,1,0:T(8,128)S(1)} %all-to-all-done.2.refs_2_) | copy-start | bytes 3145732
  132.0 5.3 %collective-permute-start.9 = (f32[64,32,128]{2,1,0:T(8,128)S(1)}, f32[64,32,128]{2,1,0:T(8,128)S(1)}, u32[]{:S(2)}, u32[]{:S(2)}) collective-permute-start(f32[64,32,128]{2,1,0:T(8,128)S(1)} %all-to-all-done.2.refs_2_), channel_id=1, source_target_pairs={{0,1},{1,0},{2,3},{3,2},{4,5},{5,4},{6,7},{7,6},{8,9},{9,8},{10,11... | collective-permute-start | bytes 3145736 | tf_op jit(solution)/shard_map/ppermute | solution.py:465
  137.3 1.0 copy-start.24
  151.2 2.9 %collective-permute-start.10 = (f32[6,256,128]{2,1,0:T(8,128)}, f32[6,256,128]{2,1,0:T(8,128)S(1)}, u32[]{:S(2)}, u32[]{:S(2)}) collective-permute-start(f32[6,256,128]{2,1,0:T(8,128)} %get-tuple-element.66), channel_id=1, source_target_pairs={{0,1},{1,0},{2,3},{3,2},{4,5},{5,4},{6,7},{7,6},{8,9},{9,8},{10,11... | collective-permute-start | bytes 2359304 | tf_op jit(solution)/shard_map/ppermute | solution.py:465
  151.7 25.9 %collective-permute-start.11 = (f32[2,2,264,256]{3,2,1,0:T(8,128)}, f32[2,2,264,256]{3,2,1,0:T(8,128)S(1)}, u32[]{:S(2)}, u32[]{:S(2)}) collective-permute-start(f32[2,2,264,256]{3,2,1,0:T(8,128)} %get-tuple-element.68.refs_0_), channel_id=1, source_target_pairs={{0,8},{8,16},{16,24},{24,32},{32,40},{40,48},{48,56},{56,64},{64,7... | collective-permute-start | bytes 3244040 | tf_op jit(solution)/shard_map/ppermute | solution.py:442
  154.1 1.1 copy-start.13
  155.4 22.2 %copy-start.8 = (f32[2,2,264,256]{3,2,1,0:T(8,128)S(1)}, f32[2,2,264,256]{3,2,1,0:T(8,128)}, u32[]{:S(2)}) copy-start(f32[2,2,264,256]{3,2,1,0:T(8,128)} %get-tuple-element.68.refs_0_) | copy-start | bytes 3244036
  170.6 11.7 %all-to-all-start.4 = ((f32[16,24,128]{2,1,0:T(8,128)}), f32[16,24,128]{2,1,0:T(8,128)S(1)}, u32[]{:S(2)}, u32[]{:S(2)}) async-start(f32[16,24,128]{2,1,0:T(8,128)} %bitcast.7), calls=%async_computation.4 | async-start | bytes 393216 | tf_op jit(solution)/shard_map/all_to_all | solution.py:473
  177.5 15.6 %copy-start.17 = (f32[8,128]{1,0:T(8,128)S(1)}, f32[8,128]{1,0:T(8,128)}, u32[]{:S(2)}) copy-start(f32[8,128]{1,0:T(8,128)} %get-tuple-element.77.loss) | copy-start | bytes 12292
  178.3 0.8 copy-start.18
  182.3 10.8 %collective-permute-start.12 = (f32[1,2,256,256]{3,2,1,0:T(8,128)}, f32[1,2,256,256]{3,2,1,0:T(8,128)S(1)}, u32[]{:S(2)}, u32[]{:S(2)}) collective-permute-start(f32[1,2,256,256]{3,2,1,0:T(8,128)} %copy-done.18), channel_id=1, source_target_pairs={{0,1},{1,2},{2,3},{3,4},{4,5},{5,6},{6,7},{8,9},{9,10},{10,11},{11... | collective-permute-start | bytes 1572872 | tf_op jit(solution)/shard_map/ppermute | solution.py:442
  194.0 27.7 %copy-start.1 = (f32[2,256,512]{2,1,0:T(8,128)S(1)}, f32[2,256,512]{2,1,0:T(8,128)}, u32[]{:S(2)}) copy-start(f32[2,256,512]{2,1,0:T(8,128)} %refs_3_.1) | copy-start | bytes 3145732
  194.0 27.7 %copy-start.12 = (f32[2,256,512]{2,1,0:T(8,128)S(1)}, f32[2,256,512]{2,1,0:T(8,128)}, u32[]{:S(2)}) copy-start(f32[2,256,512]{2,1,0:T(8,128)} %copy-done.11) | copy-start | bytes 3145732
  194.0 27.7 %copy-start.16 = (f32[8,128]{1,0:T(8,128)S(1)}, f32[8,128]{1,0:T(8,128)}, u32[]{:S(2)}) copy-start(f32[8,128]{1,0:T(8,128)} %get-tuple-element.64.rate_first) | copy-start | bytes 12292
  216.4 5.3 %collective-permute-start.13 = (f32[64,32,128]{2,1,0:T(8,128)S(1)}, f32[64,32,128]{2,1,0:T(8,128)S(1)}, u32[]{:S(2)}, u32[]{:S(2)}) collective-permute-start(f32[64,32,128]{2,1,0:T(8,128)S(1)} %all_to_all.32.refs_0_), channel_id=1, source_target_pairs={{0,1},{1,0},{2,3},{3,2},{4,5},{5,4},{6,7},{7,6},{8,9},{9,8},{10,11... | collective-permute-start | bytes 3145736 | tf_op jit(solution)/shard_map/ppermute | solution.py:465
